TPU v7x, 32 devices: a whole 2x2x4 slice. The times are simulated.
32 devices in a mesh: sec: 2 (over x), blk: 16 (over z, y, core).
Axes of the slice: x: 2, y: 2, z: 4, core: 2. Of those that a mesh axis runs over, the one named last changes fastest.
Arguments:
- column_state: float32 [2, 64, 512, 512], P('sec', None, 'blk'), may hold values from -6 to 6
- forcing: bfloat16 [2, 8, 512, 512], P('sec', None, 'blk'), may hold values from -6 to 6
- couple_gain: bfloat16 [2, 64, 8], P('sec'), may hold values from -2 to 2
- diffusion: float32 [2, 64], P('sec'), may hold values from 0.2 to 0.24
- mixing: float32 [2, 64, 64], P('sec'), may hold values from -0.75 to 0.75
- export_map: float32 [2, 8, 64], P('sec'), may hold values from -0.75 to 0.75
- land_mask: int32 [512, 512], P('blk'), may hold values 0 or 1
- sources: int32 [2, 2048, 3], P('sec', 'blk'), may hold values from 0 to 2047, as said below
- regrid_weights: bfloat16 [2, 2048, 3, 128, 128], P('sec', 'blk'), may hold values from -0.3125 to 0.3125
Outputs:
- new_state: float32 [2, 64, 512, 512], P('sec', None, 'blk')
- coupled: bfloat16 [2, 8, 512, 512], P('sec', None, 'blk')
Inputs may be any that keep to these rules, and one draw needn't show every extreme that they name: `sources`: an entry of a destination tile in block b names a tile of the other component whose block lies within 2 blocks of b, counted cyclically over the blocks; the distance 2 occurs on both sides in every block.
All inputs are finite; a program needn't handle non-finite values. No bound on the sum of `land_mask` on one device may be relied on, other than what follows from the above.
Results may differ from a plain program's by a relative error of at most 0.0048.
Values may be sent and summed in bfloat16 or wider, within the bound.
No kernel may reach another device: no remote copies, remote signals or barrier semaphores. Data moves between devices by JAX's collectives and lax.ppermute only.
A program may use at most 128 MiB of HBM per device.

v0:
```python
import jax
import jax.numpy as jnp
from jax import lax
from jax.experimental import pallas as pl
from jax.experimental.pallas import tpu as pltpu
from jax.sharding import PartitionSpec as P

TC = 128
OV = 3
REACH = 2
NSTEP = 4
EDGE = NSTEP
F32 = jnp.float32
BF16 = jnp.bfloat16
VMEM = pltpu.VMEM
MIB = 2**20


def split(value):
    high = value.astype(BF16)
    return high, (value - high.astype(F32)).astype(BF16)


def column(row):
    n = row.shape[1]
    eye = lax.broadcasted_iota(jnp.int32, (n, n), 0) == lax.broadcasted_iota(jnp.int32, (n, n), 1)
    return jnp.sum(jnp.where(eye, jnp.broadcast_to(row, (n, n)), 0.0), axis=1, keepdims=True)


def stacked(matrix):
    high, low = split(matrix)
    return jnp.concatenate([high, high, low], axis=1)


def mixers(mixing, export_map):
    n = mixing.shape[0]
    eye = lax.broadcasted_iota(jnp.int32, (n, n), 0) == lax.broadcasted_iota(jnp.int32, (n, n), 1)
    step = 0.5 * (jnp.where(eye, 1.0, 0.0) + mixing)
    out = jnp.dot(export_map, step, precision=lax.Precision.HIGHEST, preferred_element_type=F32)
    return stacked(jnp.concatenate([step, out], axis=0))


def rows_of(blocks, first, size, stride):
    return jnp.concatenate([block[pl.ds(first, size, stride=stride), :] for block in blocks], axis=1)


def blocks_of(ref):
    return [ref.at[index] for index in range(ref.shape[0])]


def diffused(here, above, below, wet, rate, rest):
    columns = here.shape[1]
    near = above + below + pltpu.roll(here, 1, 1) + pltpu.roll(here, columns - 1, 1)
    return jnp.where(wet > 0.0, rate * near + rest * here, here)


def mixed(factor, value):
    high, low = split(value)
    return jnp.dot(factor, jnp.concatenate([high, low, high], axis=0), preferred_element_type=F32)


def load_force(forcing_ref, force):
    value = forcing_ref[...].astype(F32)
    for index in range(force.shape[0]):
        force[index] = value[:, index * TC : (index + 1) * TC]


def edge_kernel(*refs):
    forcing_ref, gain_ref, wet_ref, down_ref, up_ref, force = refs[-6:]
    blocks = (len(refs) - 6) // 2
    top_refs = refs[:blocks]
    bottom_refs = refs[blocks : 2 * blocks]
    levels, fields = gain_ref.shape
    columns = forcing_ref.shape[1]
    rows = forcing_ref.shape[0] // fields
    load_force(forcing_ref, force)
    gain = gain_ref[...]
    for state_refs, out_ref, first, inside in (
        (top_refs, down_ref, 0, 0),
        (bottom_refs, up_ref, rows - EDGE, 8 - EDGE),
    ):
        state = [ref.reshape(levels * 8, TC) for ref in state_refs]
        for row in range(EDGE):
            pushed = rows_of(blocks_of(force), first + row, fields, rows).astype(BF16)
            value = rows_of(state, inside + row, levels, 8) + jnp.dot(
                gain, pushed, preferred_element_type=F32
            )
            out_ref[levels * row : levels * (row + 1), :] = value.astype(BF16)
        out_ref[levels * EDGE :, :] = jnp.concatenate(
            [wet_ref[first : first + EDGE, :], jnp.zeros((16 - EDGE, columns), F32)], axis=0
        ).astype(BF16)


def inner_kernel(*refs):
    state_refs = refs[:-12]
    forcing_ref, gain_ref, rate_ref, mixing_ref, export_ref, wet_ref = refs[-12:-6]
    final_ref, edge_ref, surface_ref, even, odd, force = refs[-6:]
    levels, fields = gain_ref.shape
    rows, columns = wet_ref.shape
    load_force(forcing_ref, force)
    gain = gain_ref[...]

    @pl.loop(0, rows // 4)
    def _(group):
        for part in range(4):
            row = group * 4 + part
            pushed = rows_of(blocks_of(force), row, fields, rows).astype(BF16)
            even[row] = rows_of(state_refs, row, levels, rows) + jnp.dot(
                gain, pushed, preferred_element_type=F32
            )

    rate = column(rate_ref[...])
    rest = 1.0 - 4.0 * rate
    factor = mixers(mixing_ref[...], export_ref[...])
    step_factor = factor[:levels]
    for step in range(1, NSTEP + 1):
        source, target = (even, odd) if step % 2 else (odd, even)
        last = step == NSTEP

        @pl.loop(0, (rows - 2 * step) // 2)
        def _(pair, source=source, target=target, step=step, last=last):
            for part in range(2):
                row = step + 2 * pair + part
                value = diffused(
                    source[row],
                    source[row - 1],
                    source[row + 1],
                    wet_ref[pl.ds(row, 1), :],
                    rate,
                    rest,
                )
                result = mixed(factor if last else step_factor, value)
                if last:
                    final_ref[row - EDGE] = result[:levels]
                    surface = jnp.tanh(result[levels:]).astype(BF16)
                    per_row = columns // TC
                    for tile in range(per_row):
                        surface_ref[(row - EDGE) * per_row + tile] = surface[
                            :, tile * TC : (tile + 1) * TC
                        ]
                else:
                    target[row] = result

    for step in range(NSTEP):
        source = odd if step % 2 else even
        edge_ref[0, step, 0] = source[step]
        edge_ref[0, step, 1] = source[step + 1]
        edge_ref[1, step, 0] = source[rows - 2 - step]
        edge_ref[1, step, 1] = source[rows - 1 - step]


def outer_kernel(
    low_ref,
    high_ref,
    edge_ref,
    rate_ref,
    mixing_ref,
    export_ref,
    wet_ref,
    final_ref,
    surface_ref,
    even,
    odd,
    wet,
):
    levels = mixing_ref.shape[0]
    rows, columns = wet_ref.shape
    per_row = columns // TC
    rate = column(rate_ref[...])
    rest = 1.0 - 4.0 * rate
    factor = mixers(mixing_ref[...], export_ref[...])
    step_factor = factor[:levels]
    wet[0, 0:EDGE, :] = low_ref[levels * EDGE :, :].astype(F32)[0:EDGE]
    wet[0, EDGE : 2 * EDGE, :] = wet_ref[0:EDGE, :]
    wet[1, 0:EDGE, :] = wet_ref[rows - EDGE : rows, :]
    wet[1, EDGE : 2 * EDGE, :] = high_ref[levels * EDGE :, :].astype(F32)[0:EDGE]
    for row in range(EDGE):
        even[0, row] = low_ref[levels * row : levels * (row + 1), :].astype(F32)
        even[1, row + 2] = high_ref[levels * row : levels * (row + 1), :].astype(F32)
    for step in range(1, NSTEP + 1):
        source, target = (even, odd) if step % 2 else (odd, even)
        last = step == NSTEP
        for item in range(2):
            source[0, EDGE + item] = edge_ref[0, step - 1, item]
            source[1, item] = edge_ref[1, step - 1, item]
        for side in range(2):
            first_wet = step if side == 0 else NSTEP - step
            shift = 0 if side == 0 else 2

            @pl.loop(0, EDGE // 2)
            def _(pair):
                for part in range(2):
                    row = 2 * pair + part
                    value = diffused(
                        source[side, row + 1],
                        source[side, row],
                        source[side, row + 2],
                        wet[side, pl.ds(first_wet + row, 1), :],
                        rate,
                        rest,
                    )
                    result = mixed(factor if last else step_factor, value)
                    if last:
                        final_ref[side, row] = result[:levels]
                        surface = jnp.tanh(result[levels:]).astype(BF16)
                        for tile in range(per_row):
                            surface_ref[(side * EDGE + row) * per_row + tile] = surface[
                                :, tile * TC : (tile + 1) * TC
                            ]
                    else:
                        target[side, row + shift] = result


def write_kernel(inner_ref, outer_ref, state_ref):
    levels = inner_ref.shape[1]
    rows = inner_ref.shape[0] + 2 * EDGE

    for row in range(EDGE):
        state_ref[pl.ds(row, levels, stride=rows), :] = outer_ref[0, row]
        state_ref[pl.ds(rows - EDGE + row, levels, stride=rows), :] = outer_ref[1, row]

    @pl.loop(0, rows - 2 * EDGE)
    def _(row):
        state_ref[pl.ds(row + EDGE, levels, stride=rows), :] = inner_ref[row]


def regrid_kernel(position_ref, *refs):
    inner_refs = refs[0:6]
    outer_refs = refs[6:12]
    weight_ref, out_ref, held, sums, sems = refs[12:]
    step = pl.program_id(0)
    tiles_step = weight_ref.shape[0]
    inner_tiles = inner_refs[0].shape[0]
    edge_tiles = outer_refs[0].shape[0] // 2
    tiles = inner_tiles + 2 * edge_tiles
    fields = inner_refs[0].shape[1]
    columns = out_ref.shape[1]
    rows = out_ref.shape[0] // fields
    per_row = columns // TC

    @pl.when(step == 0)
    def _():
        copies = []
        for slot in range(6):
            start = slot * tiles
            for piece, (source, place) in enumerate(
                (
                    (inner_refs[slot], pl.ds(start + edge_tiles, inner_tiles)),
                    (outer_refs[slot].at[pl.ds(0, edge_tiles)], pl.ds(start, edge_tiles)),
                    (
                        outer_refs[slot].at[pl.ds(edge_tiles, edge_tiles)],
                        pl.ds(start + edge_tiles + inner_tiles, edge_tiles),
                    ),
                )
            ):
                copies.append(
                    pltpu.make_async_copy(source, held.at[place], sems.at[slot, piece])
                )
        for copy in copies:
            copy.start()
        for copy in copies:
            copy.wait()

    for pair in range(tiles_step // 2):
        lefts = []
        for item in range(2):
            base = (step * tiles_step + 2 * pair + item) * OV
            lefts.append(
                jnp.concatenate([held[position_ref[base + slot]] for slot in range(OV)], axis=1)
            )
        left = jnp.concatenate(lefts, axis=0)
        right = jnp.concatenate([weight_ref[2 * pair], weight_ref[2 * pair + 1]], axis=1)
        result = jnp.dot(left, right, preferred_element_type=F32)
        for item in range(2):
            tile = 2 * pair + item
            row = step * (tiles_step // per_row) + tile // per_row
            sums[tile % per_row, pl.ds(row, fields, stride=rows), :] = result[
                item * fields : (item + 1) * fields, item * TC : (item + 1) * TC
            ]

    @pl.when(step == pl.num_programs(0) - 1)
    def _():
        for index in range(per_row):
            out_ref[:, index * TC : (index + 1) * TC] = sums[index].astype(BF16)


def on_device(
    column_state,
    forcing,
    couple_gain,
    diffusion,
    mixing,
    export_map,
    land_mask,
    sources,
    regrid_weights,
):
    section = lax.axis_index("sec")
    shard = lax.axis_index("blk")
    count = lax.axis_size("blk")
    _, levels, rows, columns = column_state.shape
    fields = forcing.shape[1]
    tiles = rows * columns // TC
    per_row = columns // TC
    inner_rows = rows - 2 * EDGE
    inner_tiles = inner_rows * per_row
    outer_tiles = 2 * EDGE * per_row
    state = column_state[0]
    force = forcing[0].reshape(fields * rows, columns)
    gain = couple_gain[0]
    rate = diffusion
    mixer = mixing[0]
    export = export_map[0]
    wetness = jnp.where(section == 1, land_mask.astype(F32), jnp.ones(land_mask.shape, F32))
    whole = pl.BlockSpec(memory_space=VMEM)

    payload = levels * EDGE + 16
    down, up = pl.pallas_call(
        edge_kernel,
        grid=(1,),
        in_specs=[
            pl.BlockSpec((levels, 8, TC), lambda i, j=index, k=k: (0, k, j))
            for k in (0, rows // 8 - 1)
            for index in range(per_row)
        ]
        + [
            pl.BlockSpec((fields * rows, columns), lambda i: (0, 0)),
            pl.BlockSpec((levels, fields), lambda i: (0, 0)),
            pl.BlockSpec((rows, columns), lambda i: (0, 0)),
        ],
        out_specs=[pl.BlockSpec((payload, columns), lambda i: (0, 0))] * 2,
        out_shape=[jax.ShapeDtypeStruct((payload, columns), BF16)] * 2,
        scratch_shapes=[VMEM((per_row, fields * rows, TC), F32)],
        compiler_params=pltpu.CompilerParams(vmem_limit_bytes=16 * MIB),
        cost_estimate=pl.CostEstimate(flops=10**7, bytes_accessed=3 * MIB, transcendentals=0),
        name="edges",
    )(*[state] * (2 * per_row), force, gain, wetness)
    upward = [(i, i + 1) for i in range(count - 1)]
    downward = [(i + 1, i) for i in range(count - 1)]
    low = lax.ppermute(up, "blk", upward)
    high = lax.ppermute(down, "blk", downward)

    inner_final, edges, inner_surface = pl.pallas_call(
        inner_kernel,
        grid=(1,),
        in_specs=[
            pl.BlockSpec((levels * rows, TC), lambda i, j=index: (0, j)) for index in range(per_row)
        ]
        + [whole] * 6,
        out_specs=[whole] * 3,
        out_shape=[
            jax.ShapeDtypeStruct((inner_rows, levels, columns), F32),
            jax.ShapeDtypeStruct((2, NSTEP, 2, levels, columns), F32),
            jax.ShapeDtypeStruct((inner_tiles, fields, TC), BF16),
        ],
        scratch_shapes=[
            VMEM((rows, levels, columns), F32),
            VMEM((rows, levels, columns), F32),
            VMEM((per_row, fields * rows, TC), F32),
        ],
        compiler_params=pltpu.CompilerParams(vmem_limit_bytes=32 * MIB),
        cost_estimate=pl.CostEstimate(flops=10**10, bytes_accessed=20 * MIB, transcendentals=0),
        name="inner",
    )(*[state.reshape(levels * rows, columns)] * per_row, force, gain, rate, mixer, export, wetness)

    outer_final, outer_surface = pl.pallas_call(
        outer_kernel,
        in_specs=[whole] * 7,
        out_specs=[whole] * 2,
        out_shape=[
            jax.ShapeDtypeStruct((2, EDGE, levels, columns), F32),
            jax.ShapeDtypeStruct((outer_tiles, fields, TC), BF16),
        ],
        scratch_shapes=[
            VMEM((2, EDGE + 2, levels, columns), F32),
            VMEM((2, EDGE + 2, levels, columns), F32),
            VMEM((2, 2 * EDGE, columns), F32),
        ],
        compiler_params=pltpu.CompilerParams(vmem_limit_bytes=16 * MIB),
        cost_estimate=pl.CostEstimate(flops=3 * 10**9, bytes_accessed=4 * MIB, transcendentals=0),
        name="outer",
    )(low, high, edges, rate, mixer, export, wetness)

    new_state = pl.pallas_call(
        write_kernel,
        grid=(per_row,),
        in_specs=[
            pl.BlockSpec((inner_rows, levels, TC), lambda j: (0, 0, j)),
            pl.BlockSpec((2, EDGE, levels, TC), lambda j: (0, 0, 0, j)),
        ],
        out_specs=pl.BlockSpec((levels * rows, TC), lambda j: (0, j)),
        out_shape=jax.ShapeDtypeStruct((levels * rows, columns), F32),
        compiler_params=pltpu.CompilerParams(vmem_limit_bytes=16 * MIB),
        cost_estimate=pl.CostEstimate(flops=0, bytes_accessed=8 * MIB, transcendentals=0),
        name="write",
    )(inner_final, outer_final)

    section_count = lax.axis_size("sec")
    across = [(i, section_count - 1 - i) for i in range(section_count)]
    later = [(i, (i + 2) % count) for i in range(count)]
    earlier = [(i, (i - 2) % count) for i in range(count)]
    mates = [(i, i ^ 1) for i in range(count)]

    def gathered(surface):
        here = lax.ppermute(surface, "sec", across)
        before = lax.ppermute(here, "blk", later)
        after = lax.ppermute(here, "blk", earlier)
        own = [before, here, after]
        other = [lax.ppermute(piece, "blk", mates) for piece in own]
        return own + other

    inner_pieces = gathered(inner_surface)
    outer_pieces = gathered(outer_surface)

    core = shard % 2
    wanted = sources.reshape(-1)
    away = wanted // tiles - (shard - core) + 2
    away = away % count
    same_core = away % 2 == core
    positions = (jnp.where(same_core, 0, 3) + away // 2) * tiles + wanted % tiles

    tiles_step = 16
    weights = regrid_weights.reshape(tiles, OV * TC, TC)
    anywhere = pl.BlockSpec(memory_space=pl.ANY)
    coupled = pl.pallas_call(
        regrid_kernel,
        grid_spec=pltpu.PrefetchScalarGridSpec(
            num_scalar_prefetch=1,
            grid=(tiles // tiles_step,),
            in_specs=[anywhere] * 12
            + [pl.BlockSpec((tiles_step, OV * TC, TC), lambda i, p: (i, 0, 0))],
            out_specs=pl.BlockSpec((fields * rows, columns), lambda i, p: (0, 0)),
            scratch_shapes=[
                VMEM((6 * tiles, fields, TC), BF16),
                VMEM((per_row, fields * rows, TC), F32),
                pltpu.SemaphoreType.DMA((6, 3)),
            ],
        ),
        out_shape=jax.ShapeDtypeStruct((fields * rows, columns), BF16),
        compiler_params=pltpu.CompilerParams(vmem_limit_bytes=16 * MIB),
        cost_estimate=pl.CostEstimate(flops=10**9, bytes_accessed=16 * MIB, transcendentals=0),
        name="regrid",
    )(positions, *inner_pieces, *outer_pieces, weights)

    return (
        new_state.reshape(1, levels, rows, columns),
        coupled.reshape(1, fields, rows, columns),
    )


def solution(mesh):
    in_specs = (
        P("sec", None, "blk", None),
        P("sec", None, "blk", None),
        P("sec", None, None),
        P("sec", None),
        P("sec", None, None),
        P("sec", None, None),
        P("blk", None),
        P("sec", "blk", None),
        P("sec", "blk", None, None, None),
    )
    out_specs = (P("sec", None, "blk", None), P("sec", None, "blk", None))
    return jax.shard_map(
        on_device, mesh=mesh, in_specs=in_specs, out_specs=out_specs, check_vma=False
    )
```

profile of v0, /device:TPU:0, one launch (start us, length us, event | category | flops | bytes accessed | tf_op | source)
XLA Modules:
  0.0 86.8 jit_solution(165191466771938060)
XLA Ops:
  0.6 0.8 copy.12
  1.4 0.8 convert_select_fusion.refs_9_.refs_10_.wet_ref
  2.3 2.2 %copy-done = f32[1,64,32,512]{3,2,1,0:T(8,128)S(1)} copy-done((f32[1,64,32,512]{3,2,1,0:T(8,128)S(1)}, f32[1,64,32,512]{3,2,1,0:T(8,128)}, u32[]{:S(2)}) %copy-start) | copy-done | bytes 4194328
  4.5 0.9 %copy-done.5 = bf16[1,8,32,512]{3,2,1,0:T(8,128)(2,1)S(1)} copy-done((bf16[1,8,32,512]{3,2,1,0:T(8,128)(2,1)S(1)}, bf16[1,8,32,512]{3,2,1,0:T(8,128)(2,1)}, u32[]{:S(2)}) %copy-start.5) | copy-done | bytes 262168
  5.4 0.0 copy-start.9
  5.4 0.5 edges.1
  5.9 2.6 %collective-permute-start = (bf16[272,512]{1,0:T(8,128)(2,1)S(1)}, bf16[272,512]{1,0:T(8,128)(2,1)S(1)}, u32[]{:S(2)}, u32[]{:S(2)}) collective-permute-start(bf16[272,512]{1,0:T(8,128)(2,1)S(1)} %get-tuple-element.10), channel_id=1, source_target_pairs={{0,1},{1,2},{2,3},{3,4},{4,5},{5,6},{6,7},{7,8},{8,9},{9,10},{10,1... | collective-permute-start | bytes 835592 | tf_op jit(solution)/shard_map/ppermute | solution.py:340
  8.6 1.3 %collective-permute-start.1 = (bf16[272,512]{1,0:T(8,128)(2,1)S(1)}, bf16[272,512]{1,0:T(8,128)(2,1)S(1)}, u32[]{:S(2)}, u32[]{:S(2)}) collective-permute-start(bf16[272,512]{1,0:T(8,128)(2,1)S(1)} %get-tuple-element.11), channel_id=1, source_target_pairs={{1,0},{2,1},{3,2},{4,3},{5,4},{6,5},{7,6},{8,7},{9,8},{10,9},{11,1... | collective-permute-start | bytes 835592 | tf_op jit(solution)/shard_map/ppermute | solution.py:341
  9.9 25.6 %inner.1 = (f32[24,64,512]{2,1,0:T(8,128)S(1)}, f32[2,4,2,64,512]{4,3,2,1,0:T(8,128)S(1)}, bf16[96,8,128]{2,1,0:T(8,128)(2,1)S(1)}) custom-call(f32[2048,512]{1,0:T(8,128)S(1)} %bitcast.17, f32[2048,512]{1,0:T(8,128)S(1)} %bitcast.18, f32[2048,512]{1,0:T(8,128)S(1)} %bitcast.19, f32[2048,512]{1,0:T(8,128)S(1)} %bitcast.20, bf16[256,512]{1,0:T(8,128)(2,1)S(1)} %bitcast.23, ...), custom_call_target="tpu_custom_call" | custom-call | flops 10000000000 | bytes 20971520 | tf_op jit(solution)/shard_map/inner/pallas_call | solution.py:343
  35.5 2.4 %collective-permute-start.2 = (bf16[96,8,128]{2,1,0:T(8,128)(2,1)S(1)}, bf16[96,8,128]{2,1,0:T(8,128)(2,1)S(1)}, u32[]{:S(2)}, u32[]{:S(2)}) collective-permute-start(bf16[96,8,128]{2,1,0:T(8,128)(2,1)S(1)} %get-tuple-element.14), channel_id=1, source_target_pairs={{0,16},{16,0},{1,17},{17,1},{2,18},{18,2},{3,19},{19,3},{4,20},{20... | collective-permute-start | bytes 589832 | tf_op jit(solution)/shard_map/ppermute | solution.py:405
  37.9 3.8 %collective-permute-done.2.refs_1_ = bf16[96,8,128]{2,1,0:T(8,128)(2,1)S(1)} collective-permute-done((bf16[96,8,128]{2,1,0:T(8,128)(2,1)S(1)}, bf16[96,8,128]{2,1,0:T(8,128)(2,1)S(1)}, u32[]{:S(2)}, u32[]{:S(2)}) %collective-permute-start.2) | collective-permute-done | bytes 196640 | tf_op jit(solution)/shard_map/ppermute | solution.py:405
  41.7 5.5 %collective-permute-start.3 = (bf16[96,8,128]{2,1,0:T(8,128)(2,1)S(1)}, bf16[96,8,128]{2,1,0:T(8,128)(2,1)S(1)}, u32[]{:S(2)}, u32[]{:S(2)}) collective-permute-start(bf16[96,8,128]{2,1,0:T(8,128)(2,1)S(1)} %collective-permute-done.2.refs_1_), channel_id=1, source_target_pairs={{0,2},{1,3},{2,4},{3,5},{4,6},{5,7},{6,8},{7,9},{8,10},{9,11},{10,... | collective-permute-start | bytes 589832 | tf_op jit(solution)/shard_map/ppermute | solution.py:406
  47.2 2.0 %collective-permute-start.4 = (bf16[96,8,128]{2,1,0:T(8,128)(2,1)S(1)}, bf16[96,8,128]{2,1,0:T(8,128)(2,1)}, u32[]{:S(2)}, u32[]{:S(2)}) collective-permute-start(bf16[96,8,128]{2,1,0:T(8,128)(2,1)S(1)} %collective-permute-done.2.refs_1_), channel_id=1, source_target_pairs={{0,14},{1,15},{2,0},{3,1},{4,2},{5,3},{6,4},{7,5},{8,6},{9,7},{10,... | collective-permute-start | bytes 589832 | tf_op jit(solution)/shard_map/ppermute | solution.py:407
  49.2 6.3 %outer.1 = (f32[2,4,64,512]{3,2,1,0:T(8,128)S(1)}, bf16[32,8,128]{2,1,0:T(8,128)(2,1)S(1)}) custom-call(bf16[272,512]{1,0:T(8,128)(2,1)S(1)} %collective-permute-done.low_ref, bf16[272,512]{1,0:T(8,128)(2,1)S(1)} %collective-permute-done.1.high_ref, f32[2,4,2,64,512]{4,3,2,1,0:T(8,128)S(1)} %get-tuple-element.12.edge_ref, f32[1,64]{1,0:T(1,128)S(1)} %copy-done.9, ...), custom_call_target="tpu_custom_call" | custom-call | flops 3000000000 | bytes 4194304 | tf_op jit(solution)/shard_map/outer/pallas_call | solution.py:366
  55.5 0.0 copy-start.3
  55.6 1.0 %copy-done.3 = f32[2,4,64,512]{3,2,1,0:T(8,128)} copy-done((f32[2,4,64,512]{3,2,1,0:T(8,128)}, f32[2,4,64,512]{3,2,1,0:T(8,128)S(1)}, u32[]{:S(2)}) %copy-start.3) | copy-done | bytes 1048600
  56.5 1.5 %collective-permute-start.8 = (bf16[32,8,128]{2,1,0:T(8,128)(2,1)S(1)}, bf16[32,8,128]{2,1,0:T(8,128)(2,1)}, u32[]{:S(2)}, u32[]{:S(2)}) collective-permute-start(bf16[32,8,128]{2,1,0:T(8,128)(2,1)S(1)} %get-tuple-element.15), channel_id=1, source_target_pairs={{0,16},{16,0},{1,17},{17,1},{2,18},{18,2},{3,19},{19,3},{4,20},{20... | collective-permute-start | bytes 196616 | tf_op jit(solution)/shard_map/ppermute | solution.py:405
  58.0 3.1 %collective-permute-done.8.refs_7_ = bf16[32,8,128]{2,1,0:T(8,128)(2,1)} collective-permute-done((bf16[32,8,128]{2,1,0:T(8,128)(2,1)S(1)}, bf16[32,8,128]{2,1,0:T(8,128)(2,1)}, u32[]{:S(2)}, u32[]{:S(2)}) %collective-permute-start.8) | collective-permute-done | bytes 65568 | tf_op jit(solution)/shard_map/ppermute | solution.py:405
  61.1 0.0 collective-permute-start.9
  61.1 4.7 %collective-permute-start.10 = (bf16[32,8,128]{2,1,0:T(8,128)(2,1)}, bf16[32,8,128]{2,1,0:T(8,128)(2,1)}, u32[]{:S(2)}, u32[]{:S(2)}) collective-permute-start(bf16[32,8,128]{2,1,0:T(8,128)(2,1)} %collective-permute-done.8.refs_7_), channel_id=1, source_target_pairs={{0,14},{1,15},{2,0},{3,1},{4,2},{5,3},{6,4},{7,5},{8,6},{9,7},{10,... | collective-permute-start | bytes 196616 | tf_op jit(solution)/shard_map/ppermute | solution.py:407
  65.8 0.7 copy.13
  66.6 1.0 %reshape.17 = s32[384]{0:T(512)S(1)} reshape(s32[1,128,3]{2,1,0:T(8,128)} %copy.13) | data formatting | bytes 3072 | tf_op jit(solution)/shard_map/reshape | solution.py:416
  67.6 0.1 collective-permute-start.12
  67.7 0.5 collective-permute-start.5
  68.2 0.1 collective-permute-start.7
  68.3 0.1 collective-permute-done.9.refs_6_
  68.4 0.3 collective-permute-start.11
  68.7 0.2 collective-permute-start.13
  69.0 1.2 %copy-done.4 = f32[2,4,64,512]{3,2,1,0:T(8,128)S(1)} copy-done((f32[2,4,64,512]{3,2,1,0:T(8,128)S(1)}, f32[2,4,64,512]{3,2,1,0:T(8,128)}, u32[]{:S(2)}) %copy-start.4) | copy-done | bytes 1048600
  70.2 5.8 %write.1 = f32[2048,512]{1,0:T(8,128)} custom-call(f32[24,64,512]{2,1,0:T(8,128)S(1)} %get-tuple-element.9.inner_ref, f32[2,4,64,512]{3,2,1,0:T(8,128)S(1)} %copy-done.4), custom_call_target="tpu_custom_call" | custom-call | bytes 8388608 | tf_op jit(solution)/shard_map/write/pallas_call | solution.py:384
  76.0 4.6 %copy-done.2 = bf16[1,128,3,128,128]{4,3,2,1,0:T(8,128)(2,1)S(1)} copy-done((bf16[1,128,3,128,128]{4,3,2,1,0:T(8,128)(2,1)S(1)}, bf16[1,128,3,128,128]{4,3,2,1,0:T(8,128)(2,1)}, u32[]{:S(2)}) %copy-start.2) | copy-done | bytes 12582936
  80.5 6.2 %regrid.1 = bf16[256,512]{1,0:T(8,128)(2,1)} custom-call(s32[384]{0:T(512)S(1)} %fusion.6.position_ref, bf16[96,8,128]{2,1,0:T(8,128)(2,1)S(1)} %collective-permute-done.3.refs_0_, bf16[96,8,128]{2,1,0:T(8,128)(2,1)S(1)} %collective-permute-done.2.refs_1_, bf16[96,8,128]{2,1,0:T(8,128)(2,1)} %collective-permute-done.4.refs_2_, ...), custom_call_target="tpu_custom_call" | custom-call | flops 1000000000 | bytes 16777216 | tf_op jit(solution)/shard_map/regrid/pallas_call | solution.py:425
  (28 shorter events, 0.1 us)
Async XLA Ops:
  2.3 2.2 %copy-start = (f32[1,64,32,512]{3,2,1,0:T(8,128)S(1)}, f32[1,64,32,512]{3,2,1,0:T(8,128)}, u32[]{:S(2)}) copy-start(f32[1,64,32,512]{3,2,1,0:T(8,128)} %param.9) | copy-start | bytes 12582916
  4.4 0.9 %copy-start.5 = (bf16[1,8,32,512]{3,2,1,0:T(8,128)(2,1)S(1)}, bf16[1,8,32,512]{3,2,1,0:T(8,128)(2,1)}, u32[]{:S(2)}) copy-start(bf16[1,8,32,512]{3,2,1,0:T(8,128)(2,1)} %param.10) | copy-start | bytes 786436
  5.4 4.5 %copy-start.1 = (f32[1,64,32,512]{3,2,1,0:T(8,128)S(1)}, f32[1,64,32,512]{3,2,1,0:T(8,128)}, u32[]{:S(2)}) copy-start(f32[1,64,32,512]{3,2,1,0:T(8,128)} %param.9) | copy-start | bytes 12582916
  5.4 4.5 %copy-start.6 = (bf16[1,8,32,512]{3,2,1,0:T(8,128)(2,1)S(1)}, bf16[1,8,32,512]{3,2,1,0:T(8,128)(2,1)}, u32[]{:S(2)}) copy-start(bf16[1,8,32,512]{3,2,1,0:T(8,128)(2,1)} %param.10) | copy-start | bytes 786436
  5.4 4.5 %copy-start.7 = (f32[1,64,64]{2,1,0:T(8,128)S(1)}, f32[1,64,64]{2,1,0:T(8,128)}, u32[]{:S(2)}) copy-start(f32[1,64,64]{2,1,0:T(8,128)} %param.13) | copy-start | bytes 49156
  5.4 4.5 %copy-start.8 = (f32[1,8,64]{2,1,0:T(8,128)S(1)}, f32[1,8,64]{2,1,0:T(8,128)}, u32[]{:S(2)}) copy-start(f32[1,8,64]{2,1,0:T(8,128)} %param.14) | copy-start | bytes 6148
  5.4 4.5 %copy-start.9 = (f32[1,64]{1,0:T(1,128)S(1)}, f32[1,64]{1,0:T(1,128)}, u32[]{:S(2)}) copy-start(f32[1,64]{1,0:T(1,128)} %rate_ref.1) | copy-start | bytes 772
  5.9 43.3 %collective-permute-start = (bf16[272,512]{1,0:T(8,128)(2,1)S(1)}, bf16[272,512]{1,0:T(8,128)(2,1)S(1)}, u32[]{:S(2)}, u32[]{:S(2)}) collective-permute-start(bf16[272,512]{1,0:T(8,128)(2,1)S(1)} %get-tuple-element.10), channel_id=1, source_target_pairs={{0,1},{1,2},{2,3},{3,4},{4,5},{5,6},{6,7},{7,8},{8,9},{9,10},{10,1... | collective-permute-start | bytes 835592 | tf_op jit(solution)/shard_map/ppermute | solution.py:340
  8.6 40.6 %collective-permute-start.1 = (bf16[272,512]{1,0:T(8,128)(2,1)S(1)}, bf16[272,512]{1,0:T(8,128)(2,1)S(1)}, u32[]{:S(2)}, u32[]{:S(2)}) collective-permute-start(bf16[272,512]{1,0:T(8,128)(2,1)S(1)} %get-tuple-element.11), channel_id=1, source_target_pairs={{1,0},{2,1},{3,2},{4,3},{5,4},{6,5},{7,6},{8,7},{9,8},{10,9},{11,1... | collective-permute-start | bytes 835592 | tf_op jit(solution)/shard_map/ppermute | solution.py:341
  35.5 6.1 %collective-permute-start.2 = (bf16[96,8,128]{2,1,0:T(8,128)(2,1)S(1)}, bf16[96,8,128]{2,1,0:T(8,128)(2,1)S(1)}, u32[]{:S(2)}, u32[]{:S(2)}) collective-permute-start(bf16[96,8,128]{2,1,0:T(8,128)(2,1)S(1)} %get-tuple-element.14), channel_id=1, source_target_pairs={{0,16},{16,0},{1,17},{17,1},{2,18},{18,2},{3,19},{19,3},{4,20},{20... | collective-permute-start | bytes 589832 | tf_op jit(solution)/shard_map/ppermute | solution.py:405
  41.7 26.0 %collective-permute-start.3 = (bf16[96,8,128]{2,1,0:T(8,128)(2,1)S(1)}, bf16[96,8,128]{2,1,0:T(8,128)(2,1)S(1)}, u32[]{:S(2)}, u32[]{:S(2)}) collective-permute-start(bf16[96,8,128]{2,1,0:T(8,128)(2,1)S(1)} %collective-permute-done.2.refs_1_), channel_id=1, source_target_pairs={{0,2},{1,3},{2,4},{3,5},{4,6},{5,7},{6,8},{7,9},{8,10},{9,11},{10,... | collective-permute-start | bytes 589832 | tf_op jit(solution)/shard_map/ppermute | solution.py:406
  47.2 20.5 %collective-permute-start.4 = (bf16[96,8,128]{2,1,0:T(8,128)(2,1)S(1)}, bf16[96,8,128]{2,1,0:T(8,128)(2,1)}, u32[]{:S(2)}, u32[]{:S(2)}) collective-permute-start(bf16[96,8,128]{2,1,0:T(8,128)(2,1)S(1)} %collective-permute-done.2.refs_1_), channel_id=1, source_target_pairs={{0,14},{1,15},{2,0},{3,1},{4,2},{5,3},{6,4},{7,5},{8,6},{9,7},{10,... | collective-permute-start | bytes 589832 | tf_op jit(solution)/shard_map/ppermute | solution.py:407
  49.2 19.0 %collective-permute-start.6 = (bf16[96,8,128]{2,1,0:T(8,128)(2,1)S(1)}, bf16[96,8,128]{2,1,0:T(8,128)(2,1)}, u32[]{:S(2)}, u32[]{:S(2)}) collective-permute-start(bf16[96,8,128]{2,1,0:T(8,128)(2,1)S(1)} %collective-permute-done.2.refs_1_), channel_id=1, source_target_pairs={{0,1},{1,0},{2,3},{3,2},{4,5},{5,4},{6,7},{7,6},{8,9},{9,8},{10,11... | collective-permute-start | bytes 589832 | tf_op jit(solution)/shard_map/ppermute | solution.py:409
  49.2 16.7 %copy-start.10 = (s32[1,128,3]{1,0,2:T(1,128)S(1)}, s32[1,128,3]{1,0,2:T(1,128)}, u32[]{:S(2)}) copy-start(s32[1,128,3]{1,0,2:T(1,128)} %param.16) | copy-start | bytes 4612
  55.5 1.0 %copy-start.3 = (f32[2,4,64,512]{3,2,1,0:T(8,128)}, f32[2,4,64,512]{3,2,1,0:T(8,128)S(1)}, u32[]{:S(2)}) copy-start(f32[2,4,64,512]{3,2,1,0:T(8,128)S(1)} %get-tuple-element.13.outer_ref) | copy-start | bytes 3145732
  56.5 4.6 %collective-permute-start.8 = (bf16[32,8,128]{2,1,0:T(8,128)(2,1)S(1)}, bf16[32,8,128]{2,1,0:T(8,128)(2,1)}, u32[]{:S(2)}, u32[]{:S(2)}) collective-permute-start(bf16[32,8,128]{2,1,0:T(8,128)(2,1)S(1)} %get-tuple-element.15), channel_id=1, source_target_pairs={{0,16},{16,0},{1,17},{17,1},{2,18},{18,2},{3,19},{19,3},{4,20},{20... | collective-permute-start | bytes 196616 | tf_op jit(solution)/shard_map/ppermute | solution.py:405
  61.1 7.3 %collective-permute-start.9 = (bf16[32,8,128]{2,1,0:T(8,128)(2,1)}, bf16[32,8,128]{2,1,0:T(8,128)(2,1)}, u32[]{:S(2)}, u32[]{:S(2)}) collective-permute-start(bf16[32,8,128]{2,1,0:T(8,128)(2,1)} %collective-permute-done.8.refs_7_), channel_id=1, source_target_pairs={{0,2},{1,3},{2,4},{3,5},{4,6},{5,7},{6,8},{7,9},{8,10},{9,11},{10,... | collective-permute-start | bytes 196616 | tf_op jit(solution)/shard_map/ppermute | solution.py:406
  61.1 7.6 %collective-permute-start.10 = (bf16[32,8,128]{2,1,0:T(8,128)(2,1)}, bf16[32,8,128]{2,1,0:T(8,128)(2,1)}, u32[]{:S(2)}, u32[]{:S(2)}) collective-permute-start(bf16[32,8,128]{2,1,0:T(8,128)(2,1)} %collective-permute-done.8.refs_7_), channel_id=1, source_target_pairs={{0,14},{1,15},{2,0},{3,1},{4,2},{5,3},{6,4},{7,5},{8,6},{9,7},{10,... | collective-permute-start | bytes 196616 | tf_op jit(solution)/shard_map/ppermute | solution.py:407
  67.6 8.3 %collective-permute-start.12 = (bf16[32,8,128]{2,1,0:T(8,128)(2,1)}, bf16[32,8,128]{2,1,0:T(8,128)(2,1)S(1)}, u32[]{:S(2)}, u32[]{:S(2)}) collective-permute-start(bf16[32,8,128]{2,1,0:T(8,128)(2,1)} %collective-permute-done.8.refs_7_), channel_id=1, source_target_pairs={{0,1},{1,0},{2,3},{3,2},{4,5},{5,4},{6,7},{7,6},{8,9},{9,8},{10,11... | collective-permute-start | bytes 196616 | tf_op jit(solution)/shard_map/ppermute | solution.py:409
  67.7 8.2 %collective-permute-start.5 = (bf16[96,8,128]{2,1,0:T(8,128)(2,1)S(1)}, bf16[96,8,128]{2,1,0:T(8,128)(2,1)S(1)}, u32[]{:S(2)}, u32[]{:S(2)}) collective-permute-start(bf16[96,8,128]{2,1,0:T(8,128)(2,1)S(1)} %collective-permute-done.3.refs_0_), channel_id=1, source_target_pairs={{0,1},{1,0},{2,3},{3,2},{4,5},{5,4},{6,7},{7,6},{8,9},{9,8},{10,11... | collective-permute-start | bytes 589832 | tf_op jit(solution)/shard_map/ppermute | solution.py:409
  68.2 7.7 %collective-permute-start.7 = (bf16[96,8,128]{2,1,0:T(8,128)(2,1)}, bf16[96,8,128]{2,1,0:T(8,128)(2,1)S(1)}, u32[]{:S(2)}, u32[]{:S(2)}) collective-permute-start(bf16[96,8,128]{2,1,0:T(8,128)(2,1)} %collective-permute-done.4.refs_2_), channel_id=1, source_target_pairs={{0,1},{1,0},{2,3},{3,2},{4,5},{5,4},{6,7},{7,6},{8,9},{9,8},{10,11... | collective-permute-start | bytes 589832 | tf_op jit(solution)/shard_map/ppermute | solution.py:409
  68.4 7.5 %collective-permute-start.11 = (bf16[32,8,128]{2,1,0:T(8,128)(2,1)}, bf16[32,8,128]{2,1,0:T(8,128)(2,1)S(1)}, u32[]{:S(2)}, u32[]{:S(2)}) collective-permute-start(bf16[32,8,128]{2,1,0:T(8,128)(2,1)} %collective-permute-done.9.refs_6_), channel_id=1, source_target_pairs={{0,1},{1,0},{2,3},{3,2},{4,5},{5,4},{6,7},{7,6},{8,9},{9,8},{10,11... | collective-permute-start | bytes 196616 | tf_op jit(solution)/shard_map/ppermute | solution.py:409
  68.7 7.2 %collective-permute-start.13 = (bf16[32,8,128]{2,1,0:T(8,128)(2,1)}, bf16[32,8,128]{2,1,0:T(8,128)(2,1)S(1)}, u32[]{:S(2)}, u32[]{:S(2)}) collective-permute-start(bf16[32,8,128]{2,1,0:T(8,128)(2,1)} %collective-permute-done.10.refs_8_), channel_id=1, source_target_pairs={{0,1},{1,0},{2,3},{3,2},{4,5},{5,4},{6,7},{7,6},{8,9},{9,8},{10,11... | collective-permute-start | bytes 196616 | tf_op jit(solution)/shard_map/ppermute | solution.py:409
  68.9 1.2 %copy-start.4 = (f32[2,4,64,512]{3,2,1,0:T(8,128)S(1)}, f32[2,4,64,512]{3,2,1,0:T(8,128)}, u32[]{:S(2)}) copy-start(f32[2,4,64,512]{3,2,1,0:T(8,128)} %copy-done.3) | copy-start | bytes 3145732
  76.0 4.6 %copy-start.2 = (bf16[1,128,3,128,128]{4,3,2,1,0:T(8,128)(2,1)S(1)}, bf16[1,128,3,128,128]{4,3,2,1,0:T(8,128)(2,1)}, u32[]{:S(2)}) copy-start(bf16[1,128,3,128,128]{4,3,2,1,0:T(8,128)(2,1)} %param.17) | copy-start | bytes 37748740
where the time goes:
time: 87.2 us; the launch traced here: 86.8 us
  Pallas kernels  44.4 us (51%)
  starting transfers between devices  21.2 us (24%)
  local copies, waits for them, and re-layouts  12.5 us (14%)
  waiting for transfers between devices  6.97 us (8%)
  other arithmetic  0.88 us (1%)
    pallas_call x1, Pallas kernels, on_device(): pl.pallas_call(inner_kernel, grid=(1,), in_specs=[pl.BlockSpec((levels *...  25.6 us
    unnamed x24, local copies, waits for them, and re-layouts  11.4 us
    ppermute x2, waiting for transfers between devices, gathered(): here = lax.ppermute(surface, 'sec', across)  6.85 us
    ppermute x2, starting transfers between devices, gathered(): after = lax.ppermute(here, 'blk', earlier)  6.7 us
    pallas_call x1, Pallas kernels, on_device(): pl.pallas_call(outer_kernel, in_specs=[whole] * 7, out_specs=[whole] * 2,...  6.34 us
    pallas_call x1, Pallas kernels, on_device(): pl.pallas_call(regrid_kernel, grid_spec=pltpu.PrefetchScalarGridSpec(num_...  6.25 us
    pallas_call x1, Pallas kernels, on_device(): pl.pallas_call(write_kernel, grid=(per_row,), in_specs=[pl.BlockSpec((inn...  5.75 us
    ppermute x2, starting transfers between devices, gathered(): before = lax.ppermute(here, 'blk', later)  5.53 us
  transfers between devices with their start and end apart: 14, of which 3 were waited for; matrix products, arithmetic and copies ran while one was open for 2% of the time, Pallas kernels for 43%

commit v1 on v0

--- a/solution.py
+++ b/solution.py
@@ -44,6 +44,14 @@
     return jnp.concatenate([block[pl.ds(first, size, stride=stride), :] for block in blocks], axis=1)
 
 
+def driven(gain, pushed):
+    return lax.dot_general(gain, pushed, (((0,), (0,)), ((), ())), preferred_element_type=F32)
+
+
+def wetness_of(mask):
+    return jnp.where((mask > 0) | (lax.axis_index("sec") != 1), 1.0, 0.0)
+
+
 def blocks_of(ref):
     return [ref.at[index] for index in range(ref.shape[0])]
 
@@ -66,11 +74,11 @@
 
 
 def edge_kernel(*refs):
-    forcing_ref, gain_ref, wet_ref, down_ref, up_ref, force = refs[-6:]
+    forcing_ref, gain_ref, mask_ref, down_ref, up_ref, force = refs[-6:]
     blocks = (len(refs) - 6) // 2
     top_refs = refs[:blocks]
     bottom_refs = refs[blocks : 2 * blocks]
-    levels, fields = gain_ref.shape
+    fields, levels = gain_ref.shape
     columns = forcing_ref.shape[1]
     rows = forcing_ref.shape[0] // fields
     load_force(forcing_ref, force)
@@ -82,22 +90,21 @@
         state = [ref.reshape(levels * 8, TC) for ref in state_refs]
         for row in range(EDGE):
             pushed = rows_of(blocks_of(force), first + row, fields, rows).astype(BF16)
-            value = rows_of(state, inside + row, levels, 8) + jnp.dot(
-                gain, pushed, preferred_element_type=F32
-            )
+            value = rows_of(state, inside + row, levels, 8) + driven(gain, pushed)
             out_ref[levels * row : levels * (row + 1), :] = value.astype(BF16)
         out_ref[levels * EDGE :, :] = jnp.concatenate(
-            [wet_ref[first : first + EDGE, :], jnp.zeros((16 - EDGE, columns), F32)], axis=0
+            [wetness_of(mask_ref[first : first + EDGE, :]), jnp.zeros((16 - EDGE, columns), F32)], axis=0
         ).astype(BF16)
 
 
 def inner_kernel(*refs):
-    state_refs = refs[:-12]
-    forcing_ref, gain_ref, rate_ref, mixing_ref, export_ref, wet_ref = refs[-12:-6]
-    final_ref, edge_ref, surface_ref, even, odd, force = refs[-6:]
-    levels, fields = gain_ref.shape
+    state_refs = refs[:-13]
+    forcing_ref, gain_ref, rate_ref, mixing_ref, export_ref, mask_ref = refs[-13:-7]
+    final_ref, edge_ref, surface_ref, even, odd, force, wet_ref = refs[-7:]
+    fields, levels = gain_ref.shape
     rows, columns = wet_ref.shape
     load_force(forcing_ref, force)
+    wet_ref[...] = wetness_of(mask_ref[...])
     gain = gain_ref[...]
 
     @pl.loop(0, rows // 4)
@@ -105,9 +112,7 @@
         for part in range(4):
             row = group * 4 + part
             pushed = rows_of(blocks_of(force), row, fields, rows).astype(BF16)
-            even[row] = rows_of(state_refs, row, levels, rows) + jnp.dot(
-                gain, pushed, preferred_element_type=F32
-            )
+            even[row] = rows_of(state_refs, row, levels, rows) + driven(gain, pushed)
 
     rate = column(rate_ref[...])
     rest = 1.0 - 4.0 * rate
@@ -117,10 +122,13 @@
         source, target = (even, odd) if step % 2 else (odd, even)
         last = step == NSTEP
 
-        @pl.loop(0, (rows - 2 * step) // 2)
-        def _(pair, source=source, target=target, step=step, last=last):
-            for part in range(2):
-                row = step + 2 * pair + part
+        todo = rows - 2 * step
+        at_once = max(n for n in (1, 2, 3, 4, 5) if todo % n == 0)
+
+        @pl.loop(0, todo // at_once)
+        def _(group, source=source, target=target, step=step, last=last, at_once=at_once):
+            for part in range(at_once):
+                row = step + at_once * group + part
                 value = diffused(
                     source[row],
                     source[row - 1],
@@ -156,7 +164,8 @@
     rate_ref,
     mixing_ref,
     export_ref,
-    wet_ref,
+    mask_ref,
+    inner_ref,
     final_ref,
     surface_ref,
     even,
@@ -164,15 +173,17 @@
     wet,
 ):
     levels = mixing_ref.shape[0]
-    rows, columns = wet_ref.shape
+    rows, columns = mask_ref.shape
+    inner_tiles = inner_ref.shape[0]
     per_row = columns // TC
     rate = column(rate_ref[...])
     rest = 1.0 - 4.0 * rate
     factor = mixers(mixing_ref[...], export_ref[...])
     step_factor = factor[:levels]
     wet[0, 0:EDGE, :] = low_ref[levels * EDGE :, :].astype(F32)[0:EDGE]
-    wet[0, EDGE : 2 * EDGE, :] = wet_ref[0:EDGE, :]
-    wet[1, 0:EDGE, :] = wet_ref[rows - EDGE : rows, :]
+    wet[0, EDGE : 2 * EDGE, :] = wetness_of(mask_ref[0:EDGE, :])
+    wet[1, 0:EDGE, :] = wetness_of(mask_ref[rows - EDGE : rows, :])
+    surface_ref[pl.ds(EDGE * per_row, inner_tiles)] = inner_ref[...]
     wet[1, EDGE : 2 * EDGE, :] = high_ref[levels * EDGE :, :].astype(F32)[0:EDGE]
     for row in range(EDGE):
         even[0, row] = low_ref[levels * row : levels * (row + 1), :].astype(F32)
@@ -187,10 +198,10 @@
             first_wet = step if side == 0 else NSTEP - step
             shift = 0 if side == 0 else 2
 
-            @pl.loop(0, EDGE // 2)
+            @pl.loop(0, 1)
             def _(pair):
-                for part in range(2):
-                    row = 2 * pair + part
+                for part in range(EDGE):
+                    row = EDGE * pair + part
                     value = diffused(
                         source[side, row + 1],
                         source[side, row],
@@ -204,7 +215,7 @@
                         final_ref[side, row] = result[:levels]
                         surface = jnp.tanh(result[levels:]).astype(BF16)
                         for tile in range(per_row):
-                            surface_ref[(side * EDGE + row) * per_row + tile] = surface[
+                            surface_ref[(side * (rows - EDGE) + row) * per_row + tile] = surface[
                                 :, tile * TC : (tile + 1) * TC
                             ]
                     else:
@@ -225,63 +236,56 @@
 
 
 def regrid_kernel(position_ref, *refs):
-    inner_refs = refs[0:6]
-    outer_refs = refs[6:12]
-    weight_ref, out_ref, held, sums, sems = refs[12:]
-    step = pl.program_id(0)
-    tiles_step = weight_ref.shape[0]
-    inner_tiles = inner_refs[0].shape[0]
-    edge_tiles = outer_refs[0].shape[0] // 2
-    tiles = inner_tiles + 2 * edge_tiles
-    fields = inner_refs[0].shape[1]
-    columns = out_ref.shape[1]
-    rows = out_ref.shape[0] // fields
-    per_row = columns // TC
-
-    @pl.when(step == 0)
-    def _():
-        copies = []
-        for slot in range(6):
-            start = slot * tiles
-            for piece, (source, place) in enumerate(
-                (
-                    (inner_refs[slot], pl.ds(start + edge_tiles, inner_tiles)),
-                    (outer_refs[slot].at[pl.ds(0, edge_tiles)], pl.ds(start, edge_tiles)),
-                    (
-                        outer_refs[slot].at[pl.ds(edge_tiles, edge_tiles)],
-                        pl.ds(start + edge_tiles + inner_tiles, edge_tiles),
-                    ),
+    piece_refs = refs[0:6]
+    weight_ref, out_ref, held, weights, sums, piece_sems, weight_sems = refs[6:]
+    tiles, fields, _ = piece_refs[0].shape
+    chunks = weight_sems.shape[0]
+    tiles_chunk = tiles // chunks
+    per_row, total_rows, _ = sums.shape
+    rows = total_rows // fields
+
+    def weight_copy(chunk):
+        part = pl.ds(chunk * tiles_chunk, tiles_chunk)
+        return pltpu.make_async_copy(weight_ref.at[part], weights.at[part], weight_sems.at[chunk])
+
+    copies = [
+        pltpu.make_async_copy(source, held.at[pl.ds(slot * tiles, tiles)], piece_sems.at[slot])
+        for slot, source in enumerate(piece_refs)
+    ]
+    for copy in copies:
+        copy.start()
+    for chunk in range(chunks):
+        weight_copy(chunk).start()
+    for copy in copies:
+        copy.wait()
+
+    @pl.loop(0, chunks)
+    def _(chunk):
+        weight_copy(chunk).wait()
+        for pair in range(tiles_chunk // 2):
+            first = chunk * tiles_chunk + 2 * pair
+            lefts = []
+            for item in range(2):
+                base = (first + item) * OV
+                lefts.append(
+                    jnp.concatenate([held[position_ref[base + slot]] for slot in range(OV)], axis=1)
                 )
-            ):
-                copies.append(
-                    pltpu.make_async_copy(source, held.at[place], sems.at[slot, piece])
-                )
-        for copy in copies:
-            copy.start()
-        for copy in copies:
-            copy.wait()
-
-    for pair in range(tiles_step // 2):
-        lefts = []
-        for item in range(2):
-            base = (step * tiles_step + 2 * pair + item) * OV
-            lefts.append(
-                jnp.concatenate([held[position_ref[base + slot]] for slot in range(OV)], axis=1)
-            )
-        left = jnp.concatenate(lefts, axis=0)
-        right = jnp.concatenate([weight_ref[2 * pair], weight_ref[2 * pair + 1]], axis=1)
-        result = jnp.dot(left, right, preferred_element_type=F32)
-        for item in range(2):
-            tile = 2 * pair + item
-            row = step * (tiles_step // per_row) + tile // per_row
-            sums[tile % per_row, pl.ds(row, fields, stride=rows), :] = result[
-                item * fields : (item + 1) * fields, item * TC : (item + 1) * TC
-            ]
-
-    @pl.when(step == pl.num_programs(0) - 1)
-    def _():
-        for index in range(per_row):
-            out_ref[:, index * TC : (index + 1) * TC] = sums[index].astype(BF16)
+            left = jnp.concatenate(lefts, axis=0)
+            right = jnp.concatenate([weights[first], weights[first + 1]], axis=1)
+            result = jnp.dot(left, right, preferred_element_type=F32)
+            for item in range(2):
+                tile = 2 * pair + item
+                row = chunk * (tiles_chunk // per_row) + tile // per_row
+                sums[tile % per_row, pl.ds(row, fields, stride=rows), :] = result[
+                    item * fields : (item + 1) * fields, item * TC : (item + 1) * TC
+                ]
+
+    for index in range(per_row):
+        out_ref[:, index * TC : (index + 1) * TC] = sums[index].astype(BF16)
+
+
+def in_hbm(value):
+    return pltpu.with_memory_space_constraint(value, pltpu.HBM)
 
 
 def on_device(
@@ -295,7 +299,6 @@
     sources,
     regrid_weights,
 ):
-    section = lax.axis_index("sec")
     shard = lax.axis_index("blk")
     count = lax.axis_size("blk")
     _, levels, rows, columns = column_state.shape
@@ -304,14 +307,13 @@
     per_row = columns // TC
     inner_rows = rows - 2 * EDGE
     inner_tiles = inner_rows * per_row
-    outer_tiles = 2 * EDGE * per_row
-    state = column_state[0]
-    force = forcing[0].reshape(fields * rows, columns)
-    gain = couple_gain[0]
+    state = in_hbm(column_state[0])
+    force = in_hbm(forcing.reshape(fields * rows, columns))
+    gain = in_hbm(couple_gain[0].T)
+    land_mask = in_hbm(land_mask)
     rate = diffusion
     mixer = mixing[0]
     export = export_map[0]
-    wetness = jnp.where(section == 1, land_mask.astype(F32), jnp.ones(land_mask.shape, F32))
     whole = pl.BlockSpec(memory_space=VMEM)
 
     payload = levels * EDGE + 16
@@ -325,7 +327,7 @@
         ]
         + [
             pl.BlockSpec((fields * rows, columns), lambda i: (0, 0)),
-            pl.BlockSpec((levels, fields), lambda i: (0, 0)),
+            pl.BlockSpec((fields, levels), lambda i: (0, 0)),
             pl.BlockSpec((rows, columns), lambda i: (0, 0)),
         ],
         out_specs=[pl.BlockSpec((payload, columns), lambda i: (0, 0))] * 2,
@@ -334,7 +336,7 @@
         compiler_params=pltpu.CompilerParams(vmem_limit_bytes=16 * MIB),
         cost_estimate=pl.CostEstimate(flops=10**7, bytes_accessed=3 * MIB, transcendentals=0),
         name="edges",
-    )(*[state] * (2 * per_row), force, gain, wetness)
+    )(*[state] * (2 * per_row), force, gain, land_mask)
     upward = [(i, i + 1) for i in range(count - 1)]
     downward = [(i + 1, i) for i in range(count - 1)]
     low = lax.ppermute(up, "blk", upward)
@@ -357,19 +359,20 @@
             VMEM((rows, levels, columns), F32),
             VMEM((rows, levels, columns), F32),
             VMEM((per_row, fields * rows, TC), F32),
+            VMEM((rows, columns), F32),
         ],
         compiler_params=pltpu.CompilerParams(vmem_limit_bytes=32 * MIB),
         cost_estimate=pl.CostEstimate(flops=10**10, bytes_accessed=20 * MIB, transcendentals=0),
         name="inner",
-    )(*[state.reshape(levels * rows, columns)] * per_row, force, gain, rate, mixer, export, wetness)
-
-    outer_final, outer_surface = pl.pallas_call(
+    )(*[in_hbm(column_state.reshape(levels * rows, columns))] * per_row, force, gain, rate, mixer, export, land_mask)
+
+    outer_final, surface = pl.pallas_call(
         outer_kernel,
-        in_specs=[whole] * 7,
+        in_specs=[whole] * 8,
         out_specs=[whole] * 2,
         out_shape=[
             jax.ShapeDtypeStruct((2, EDGE, levels, columns), F32),
-            jax.ShapeDtypeStruct((outer_tiles, fields, TC), BF16),
+            jax.ShapeDtypeStruct((tiles, fields, TC), BF16),
         ],
         scratch_shapes=[
             VMEM((2, EDGE + 2, levels, columns), F32),
@@ -379,7 +382,7 @@
         compiler_params=pltpu.CompilerParams(vmem_limit_bytes=16 * MIB),
         cost_estimate=pl.CostEstimate(flops=3 * 10**9, bytes_accessed=4 * MIB, transcendentals=0),
         name="outer",
-    )(low, high, edges, rate, mixer, export, wetness)
+    )(low, high, edges, rate, mixer, export, land_mask, inner_surface)
 
     new_state = pl.pallas_call(
         write_kernel,
@@ -401,17 +404,6 @@
     earlier = [(i, (i - 2) % count) for i in range(count)]
     mates = [(i, i ^ 1) for i in range(count)]
 
-    def gathered(surface):
-        here = lax.ppermute(surface, "sec", across)
-        before = lax.ppermute(here, "blk", later)
-        after = lax.ppermute(here, "blk", earlier)
-        own = [before, here, after]
-        other = [lax.ppermute(piece, "blk", mates) for piece in own]
-        return own + other
-
-    inner_pieces = gathered(inner_surface)
-    outer_pieces = gathered(outer_surface)
-
     core = shard % 2
     wanted = sources.reshape(-1)
     away = wanted // tiles - (shard - core) + 2
@@ -419,28 +411,37 @@
     same_core = away % 2 == core
     positions = (jnp.where(same_core, 0, 3) + away // 2) * tiles + wanted % tiles
 
-    tiles_step = 16
-    weights = regrid_weights.reshape(tiles, OV * TC, TC)
+    weights = in_hbm(regrid_weights.reshape(tiles, OV * TC, TC))
+
+    here = lax.ppermute(surface, "sec", across)
+    here, new_state, positions = lax.optimization_barrier((here, new_state, positions))
+    before = lax.ppermute(here, "blk", later)
+    after = lax.ppermute(here, "blk", earlier)
+    other = lax.ppermute(here, "blk", mates)
+    pieces = [before, here, after]
+    pieces += [lax.ppermute(before, "blk", mates), other, lax.ppermute(after, "blk", mates)]
+
     anywhere = pl.BlockSpec(memory_space=pl.ANY)
     coupled = pl.pallas_call(
         regrid_kernel,
         grid_spec=pltpu.PrefetchScalarGridSpec(
             num_scalar_prefetch=1,
-            grid=(tiles // tiles_step,),
-            in_specs=[anywhere] * 12
-            + [pl.BlockSpec((tiles_step, OV * TC, TC), lambda i, p: (i, 0, 0))],
+            grid=(1,),
+            in_specs=[anywhere] * 7,
             out_specs=pl.BlockSpec((fields * rows, columns), lambda i, p: (0, 0)),
             scratch_shapes=[
                 VMEM((6 * tiles, fields, TC), BF16),
+                VMEM((tiles, OV * TC, TC), BF16),
                 VMEM((per_row, fields * rows, TC), F32),
-                pltpu.SemaphoreType.DMA((6, 3)),
+                pltpu.SemaphoreType.DMA((6,)),
+                pltpu.SemaphoreType.DMA((16,)),
             ],
         ),
         out_shape=jax.ShapeDtypeStruct((fields * rows, columns), BF16),
-        compiler_params=pltpu.CompilerParams(vmem_limit_bytes=16 * MIB),
+        compiler_params=pltpu.CompilerParams(vmem_limit_bytes=24 * MIB),
         cost_estimate=pl.CostEstimate(flops=10**9, bytes_accessed=16 * MIB, transcendentals=0),
         name="regrid",
-    )(positions, *inner_pieces, *outer_pieces, weights)
+    )(positions, *pieces, weights)
 
     return (
         new_state.reshape(1, levels, rows, columns),

time: 87.2 us -> 70.2 us (0.81)
  local copies, waits for them, and re-layouts: 12.5 us -> 2.53 us
  starting transfers between devices: 21.2 us -> 13.1 us
  waiting for transfers between devices: 6.97 us -> 11.6 us
  Pallas kernels: 44.4 us -> 41.9 us
    unnamed x24 -> x13, local copies, waits for them, and re-layouts: 11.4 us -> 2.32 us
    ppermute x12 -> x6, starting transfers between devices: 17.3 us -> 9.41 us  [the longest x1 4.04 us: on_device(): before = lax.ppermute(here, 'blk', later)]
    ppermute x12 -> x6, waiting for transfers between devices: 6.96 us -> 11.6 us  [the longest x1 7.91 us: on_device(): before = lax.ppermute(here, 'blk', later)]
    pallas_call x1, Pallas kernels: 25.6 us -> 23 us  [on_device(): pl.pallas_call(inner_kernel, grid=(1,), in_specs=[pl.BlockSpec((levels *...]
    pallas_call x1, Pallas kernels: 6.34 us -> 4.59 us  [on_device(): pl.pallas_call(outer_kernel, in_specs=[whole] * 8, out_specs=[whole] * 2,...]
    pallas_call x1, Pallas kernels: 0.49 us -> 2.03 us  [on_device(): pl.pallas_call(edge_kernel, grid=(1,), in_specs=[pl.BlockSpec((levels, 8,...]
  transfers between devices with their start and end apart: 14 -> 8, of which waited for: 3 -> 3; matrix products, arithmetic and copies ran while one was open for 2% -> 0% of each run, Pallas kernels for 43% -> 41%
where the time goes in v1:
time: 70.2 us; the launch traced here: 69.9 us
  Pallas kernels  41.9 us (60%)
  starting transfers between devices  13.1 us (19%)
  waiting for transfers between devices  11.6 us (17%)
  local copies, waits for them, and re-layouts  2.53 us (4%)
  between operations  0.77 us (1%)
    pallas_call x1, Pallas kernels, on_device(): pl.pallas_call(inner_kernel, grid=(1,), in_specs=[pl.BlockSpec((levels *...  23 us
    ppermute x1, waiting for transfers between devices, on_device(): before = lax.ppermute(here, 'blk', later)  7.91 us
    pallas_call x1, Pallas kernels, on_device(): pl.pallas_call(regrid_kernel, grid_spec=pltpu.PrefetchScalarGridSpec(num_...  6.48 us
    pallas_call x1, Pallas kernels, on_device(): pl.pallas_call(write_kernel, grid=(per_row,), in_specs=[pl.BlockSpec((inn...  5.75 us
    pallas_call x1, Pallas kernels, on_device(): pl.pallas_call(outer_kernel, in_specs=[whole] * 8, out_specs=[whole] * 2,...  4.59 us
    ppermute x1, starting transfers between devices, on_device(): before = lax.ppermute(here, 'blk', later)  4.04 us
    ppermute x1, starting transfers between devices, on_device(): after = lax.ppermute(here, 'blk', earlier)  3.04 us
    ppermute x1, starting transfers between devices, on_device(): low = lax.ppermute(up, 'blk', upward)  2.38 us
  transfers between devices with their start and end apart: 8, of which 3 were waited for; matrix products, arithmetic and copies ran while one was open for 0% of the time, Pallas kernels for 41%

profile of v1, /device:TPU:0, one launch (start us, length us, event | category | flops | bytes accessed | tf_op | source)
XLA Modules:
  0.0 69.9 jit_solution(12719440487063498989)
XLA Ops:
  0.6 0.0 copy-start.2
  0.7 2.0 %edges.1 = (bf16[272,512]{1,0:T(8,128)(2,1)S(1)}, bf16[272,512]{1,0:T(8,128)(2,1)S(1)}) custom-call(f32[64,32,512]{2,1,0:T(8,128)} %bitcast.15, f32[64,32,512]{2,1,0:T(8,128)} %bitcast.16, f32[64,32,512]{2,1,0:T(8,128)} %bitcast.17, f32[64,32,512]{2,1,0:T(8,128)} %bitcast.18, f32[64,32,512]{2,1,0:T(8,128)} %bitcast.19, f32[64,32,512]{2,1,0:T(8,128)} %bitcast.20, ...), custom_call_target="tpu_custom_call" | custom-call | flops 10000000 | bytes 3145728 | tf_op jit(solution)/shard_map/edges/pallas_call | solution.py:320
  2.7 2.4 %collective-permute-start = (bf16[272,512]{1,0:T(8,128)(2,1)S(1)}, bf16[272,512]{1,0:T(8,128)(2,1)S(1)}, u32[]{:S(2)}, u32[]{:S(2)}) collective-permute-start(bf16[272,512]{1,0:T(8,128)(2,1)S(1)} %get-tuple-element.12), channel_id=1, source_target_pairs={{0,1},{1,2},{2,3},{3,4},{4,5},{5,6},{6,7},{7,8},{8,9},{9,10},{10,1... | collective-permute-start | bytes 835592 | tf_op jit(solution)/shard_map/ppermute | solution.py:342
  5.1 1.3 %collective-permute-start.1 = (bf16[272,512]{1,0:T(8,128)(2,1)S(1)}, bf16[272,512]{1,0:T(8,128)(2,1)S(1)}, u32[]{:S(2)}, u32[]{:S(2)}) collective-permute-start(bf16[272,512]{1,0:T(8,128)(2,1)S(1)} %get-tuple-element.13), channel_id=1, source_target_pairs={{1,0},{2,1},{3,2},{4,3},{5,4},{6,5},{7,6},{8,7},{9,8},{10,9},{11,1... | collective-permute-start | bytes 835592 | tf_op jit(solution)/shard_map/ppermute | solution.py:343
  6.4 0.0 copy-done.2
  6.4 0.0 copy-done.3
  6.4 0.0 copy-done.4
  6.4 23.0 %inner.1 = (f32[24,64,512]{2,1,0:T(8,128)S(1)}, f32[2,4,2,64,512]{4,3,2,1,0:T(8,128)S(1)}, bf16[96,8,128]{2,1,0:T(8,128)(2,1)S(1)}) custom-call(f32[2048,512]{1,0:T(8,128)} %bitcast.23, f32[2048,512]{1,0:T(8,128)} %bitcast.24, f32[2048,512]{1,0:T(8,128)} %bitcast.25, f32[2048,512]{1,0:T(8,128)} %bitcast.26, bf16[256,512]{1,0:T(8,128)(2,1)} %bitcast.30, ...), custom_call_target="tpu_custom_call" | custom-call | flops 10000000000 | bytes 20971520 | tf_op jit(solution)/shard_map/inner/pallas_call | solution.py:345
  29.4 0.0 collective-permute-done.low_ref
  29.5 0.0 collective-permute-done.1.high_ref
  29.5 0.0 copy-start.5
  29.5 4.6 %outer.1 = (f32[2,4,64,512]{3,2,1,0:T(8,128)S(1)}, bf16[128,8,128]{2,1,0:T(8,128)(2,1)}) custom-call(bf16[272,512]{1,0:T(8,128)(2,1)S(1)} %collective-permute-done.low_ref, bf16[272,512]{1,0:T(8,128)(2,1)S(1)} %collective-permute-done.1.high_ref, f32[2,4,2,64,512]{4,3,2,1,0:T(8,128)S(1)} %get-tuple-element.14.edge_ref, f32[1,64]{1,0:T(1,128)S(1)} %copy-done.4, ...), custom_call_target="tpu_custom_call" | custom-call | flops 3000000000 | bytes 4194304 | tf_op jit(solution)/shard_map/outer/pallas_call | solution.py:369
  34.1 1.0 %copy-done = f32[2,4,64,512]{3,2,1,0:T(8,128)} copy-done((f32[2,4,64,512]{3,2,1,0:T(8,128)}, f32[2,4,64,512]{3,2,1,0:T(8,128)S(1)}, u32[]{:S(2)}) %copy-start) | copy-done | bytes 1048600
  35.0 2.3 %collective-permute-start.2 = (bf16[128,8,128]{2,1,0:T(8,128)(2,1)}, bf16[128,8,128]{2,1,0:T(8,128)(2,1)S(1)}, u32[]{:S(2)}, u32[]{:S(2)}) collective-permute-start(bf16[128,8,128]{2,1,0:T(8,128)(2,1)} %get-tuple-element.16), channel_id=1, source_target_pairs={{0,16},{16,0},{1,17},{17,1},{2,18},{18,2},{3,19},{19,3},{4,20},{20... | collective-permute-start | bytes 786440 | tf_op jit(solution)/shard_map/ppermute | solution.py:416
  37.4 0.0 copy-done.5
  37.4 0.1 copy.11
  37.5 0.2 reshape.24
  37.7 0.0 copy-start.1
  37.8 1.2 %copy-done.1 = f32[2,4,64,512]{3,2,1,0:T(8,128)S(1)} copy-done((f32[2,4,64,512]{3,2,1,0:T(8,128)S(1)}, f32[2,4,64,512]{3,2,1,0:T(8,128)}, u32[]{:S(2)}) %copy-start.1) | copy-done | bytes 1048600
  39.0 5.8 %write.1 = f32[2048,512]{1,0:T(8,128)} custom-call(f32[24,64,512]{2,1,0:T(8,128)S(1)} %get-tuple-element.17.inner_ref, f32[2,4,64,512]{3,2,1,0:T(8,128)S(1)} %copy-done.1), custom_call_target="tpu_custom_call" | custom-call | bytes 8388608 | tf_op jit(solution)/shard_map/write/pallas_call | solution.py:387
  44.7 0.0 collective-permute-done.2.refs_1_
  44.7 4.0 %collective-permute-start.3 = (bf16[128,8,128]{2,1,0:T(8,128)(2,1)S(1)}, bf16[128,8,128]{2,1,0:T(8,128)(2,1)S(1)}, u32[]{:S(2)}, u32[]{:S(2)}) collective-permute-start(bf16[128,8,128]{2,1,0:T(8,128)(2,1)S(1)} %collective-permute-done.2.refs_1_), channel_id=1, source_target_pairs={{0,2},{1,3},{2,4},{3,5},{4,6},{5,7},{6,8},{7,9},{8,10},{9,11},{10,... | collective-permute-start | bytes 786440 | tf_op jit(solution)/shard_map/ppermute | solution.py:418
  48.8 3.0 %collective-permute-start.4 = (bf16[128,8,128]{2,1,0:T(8,128)(2,1)S(1)}, bf16[128,8,128]{2,1,0:T(8,128)(2,1)S(1)}, u32[]{:S(2)}, u32[]{:S(2)}) collective-permute-start(bf16[128,8,128]{2,1,0:T(8,128)(2,1)S(1)} %collective-permute-done.2.refs_1_), channel_id=1, source_target_pairs={{0,14},{1,15},{2,0},{3,1},{4,2},{5,3},{6,4},{7,5},{8,6},{9,7},{10,... | collective-permute-start | bytes 786440 | tf_op jit(solution)/shard_map/ppermute | solution.py:419
  51.8 0.0 collective-permute-start.6
  51.8 7.9 %collective-permute-done.3.refs_0_ = bf16[128,8,128]{2,1,0:T(8,128)(2,1)S(1)} collective-permute-done((bf16[128,8,128]{2,1,0:T(8,128)(2,1)S(1)}, bf16[128,8,128]{2,1,0:T(8,128)(2,1)S(1)}, u32[]{:S(2)}, u32[]{:S(2)}) %collective-permute-start.3) | collective-permute-done | bytes 262176 | tf_op jit(solution)/shard_map/ppermute | solution.py:418
  59.7 0.0 collective-permute-start.5
  59.7 2.2 %collective-permute-done.4.refs_2_ = bf16[128,8,128]{2,1,0:T(8,128)(2,1)S(1)} collective-permute-done((bf16[128,8,128]{2,1,0:T(8,128)(2,1)S(1)}, bf16[128,8,128]{2,1,0:T(8,128)(2,1)S(1)}, u32[]{:S(2)}, u32[]{:S(2)}) %collective-permute-start.4) | collective-permute-done | bytes 262176 | tf_op jit(solution)/shard_map/ppermute | solution.py:419
  61.9 0.0 collective-permute-start.7
  61.9 0.0 collective-permute-done.6.refs_4_
  61.9 0.0 collective-permute-done.5.refs_3_
  61.9 1.5 %collective-permute-done.7.refs_5_ = bf16[128,8,128]{2,1,0:T(8,128)(2,1)S(1)} collective-permute-done((bf16[128,8,128]{2,1,0:T(8,128)(2,1)S(1)}, bf16[128,8,128]{2,1,0:T(8,128)(2,1)S(1)}, u32[]{:S(2)}, u32[]{:S(2)}) %collective-permute-start.7) | collective-permute-done | bytes 262176 | tf_op jit(solution)/shard_map/ppermute | solution.py:422
  63.5 6.5 %regrid.1 = bf16[256,512]{1,0:T(8,128)(2,1)} custom-call(s32[384]{0:T(512)S(1)} %fusion.6.position_ref, bf16[128,8,128]{2,1,0:T(8,128)(2,1)S(1)} %collective-permute-done.3.refs_0_, bf16[128,8,128]{2,1,0:T(8,128)(2,1)S(1)} %collective-permute-done.2.refs_1_, bf16[128,8,128]{2,1,0:T(8,128)(2,1)S(1)} %collective-permute-done.4.refs_2_, ...), custom_call_target="tpu_custom_call" | custom-call | flops 1000000000 | bytes 16777216 | tf_op jit(solution)/shard_map/regrid/pallas_call | solution.py:425
  (4 shorter events, 0.0 us)
Async XLA Ops:
  0.6 5.8 %copy-start.2 = (f32[1,64,64]{2,1,0:T(8,128)S(1)}, f32[1,64,64]{2,1,0:T(8,128)}, u32[]{:S(2)}) copy-start(f32[1,64,64]{2,1,0:T(8,128)} %param.13) | copy-start | bytes 49156
  0.6 5.8 %copy-start.3 = (f32[1,8,64]{2,1,0:T(8,128)S(1)}, f32[1,8,64]{2,1,0:T(8,128)}, u32[]{:S(2)}) copy-start(f32[1,8,64]{2,1,0:T(8,128)} %param.14) | copy-start | bytes 6148
  0.7 5.8 %copy-start.4 = (f32[1,64]{1,0:T(1,128)S(1)}, f32[1,64]{1,0:T(1,128)}, u32[]{:S(2)}) copy-start(f32[1,64]{1,0:T(1,128)} %rate_ref.1) | copy-start | bytes 772
  2.7 26.8 %collective-permute-start = (bf16[272,512]{1,0:T(8,128)(2,1)S(1)}, bf16[272,512]{1,0:T(8,128)(2,1)S(1)}, u32[]{:S(2)}, u32[]{:S(2)}) collective-permute-start(bf16[272,512]{1,0:T(8,128)(2,1)S(1)} %get-tuple-element.12), channel_id=1, source_target_pairs={{0,1},{1,2},{2,3},{3,4},{4,5},{5,6},{6,7},{7,8},{8,9},{9,10},{10,1... | collective-permute-start | bytes 835592 | tf_op jit(solution)/shard_map/ppermute | solution.py:342
  5.1 24.4 %collective-permute-start.1 = (bf16[272,512]{1,0:T(8,128)(2,1)S(1)}, bf16[272,512]{1,0:T(8,128)(2,1)S(1)}, u32[]{:S(2)}, u32[]{:S(2)}) collective-permute-start(bf16[272,512]{1,0:T(8,128)(2,1)S(1)} %get-tuple-element.13), channel_id=1, source_target_pairs={{1,0},{2,1},{3,2},{4,3},{5,4},{6,5},{7,6},{8,7},{9,8},{10,9},{11,1... | collective-permute-start | bytes 835592 | tf_op jit(solution)/shard_map/ppermute | solution.py:343
  29.5 7.9 %copy-start.5 = (s32[1,128,3]{1,0,2:T(1,128)S(1)}, s32[1,128,3]{1,0,2:T(1,128)}, u32[]{:S(2)}) copy-start(s32[1,128,3]{1,0,2:T(1,128)} %param.16) | copy-start | bytes 4612
  34.1 1.0 %copy-start = (f32[2,4,64,512]{3,2,1,0:T(8,128)}, f32[2,4,64,512]{3,2,1,0:T(8,128)S(1)}, u32[]{:S(2)}) copy-start(f32[2,4,64,512]{3,2,1,0:T(8,128)S(1)} %get-tuple-element.18.outer_ref) | copy-start | bytes 3145732
  35.0 9.7 %collective-permute-start.2 = (bf16[128,8,128]{2,1,0:T(8,128)(2,1)}, bf16[128,8,128]{2,1,0:T(8,128)(2,1)S(1)}, u32[]{:S(2)}, u32[]{:S(2)}) collective-permute-start(bf16[128,8,128]{2,1,0:T(8,128)(2,1)} %get-tuple-element.16), channel_id=1, source_target_pairs={{0,16},{16,0},{1,17},{17,1},{2,18},{18,2},{3,19},{19,3},{4,20},{20... | collective-permute-start | bytes 786440 | tf_op jit(solution)/shard_map/ppermute | solution.py:416
  37.7 1.2 %copy-start.1 = (f32[2,4,64,512]{3,2,1,0:T(8,128)S(1)}, f32[2,4,64,512]{3,2,1,0:T(8,128)}, u32[]{:S(2)}) copy-start(f32[2,4,64,512]{3,2,1,0:T(8,128)} %copy-done) | copy-start | bytes 3145732
  44.7 15.0 %collective-permute-start.3 = (bf16[128,8,128]{2,1,0:T(8,128)(2,1)S(1)}, bf16[128,8,128]{2,1,0:T(8,128)(2,1)S(1)}, u32[]{:S(2)}, u32[]{:S(2)}) collective-permute-start(bf16[128,8,128]{2,1,0:T(8,128)(2,1)S(1)} %collective-permute-done.2.refs_1_), channel_id=1, source_target_pairs={{0,2},{1,3},{2,4},{3,5},{4,6},{5,7},{6,8},{7,9},{8,10},{9,11},{10,... | collective-permute-start | bytes 786440 | tf_op jit(solution)/shard_map/ppermute | solution.py:418
  48.8 13.2 %collective-permute-start.4 = (bf16[128,8,128]{2,1,0:T(8,128)(2,1)S(1)}, bf16[128,8,128]{2,1,0:T(8,128)(2,1)S(1)}, u32[]{:S(2)}, u32[]{:S(2)}) collective-permute-start(bf16[128,8,128]{2,1,0:T(8,128)(2,1)S(1)} %collective-permute-done.2.refs_1_), channel_id=1, source_target_pairs={{0,14},{1,15},{2,0},{3,1},{4,2},{5,3},{6,4},{7,5},{8,6},{9,7},{10,... | collective-permute-start | bytes 786440 | tf_op jit(solution)/shard_map/ppermute | solution.py:419
  51.8 10.1 %collective-permute-start.6 = (bf16[128,8,128]{2,1,0:T(8,128)(2,1)S(1)}, bf16[128,8,128]{2,1,0:T(8,128)(2,1)S(1)}, u32[]{:S(2)}, u32[]{:S(2)}) collective-permute-start(bf16[128,8,128]{2,1,0:T(8,128)(2,1)S(1)} %collective-permute-done.2.refs_1_), channel_id=1, source_target_pairs={{0,1},{1,0},{2,3},{3,2},{4,5},{5,4},{6,7},{7,6},{8,9},{9,8},{10,11... | collective-permute-start | bytes 786440 | tf_op jit(solution)/shard_map/ppermute | solution.py:420
  59.7 2.2 %collective-permute-start.5 = (bf16[128,8,128]{2,1,0:T(8,128)(2,1)S(1)}, bf16[128,8,128]{2,1,0:T(8,128)(2,1)S(1)}, u32[]{:S(2)}, u32[]{:S(2)}) collective-permute-start(bf16[128,8,128]{2,1,0:T(8,128)(2,1)S(1)} %collective-permute-done.3.refs_0_), channel_id=1, source_target_pairs={{0,1},{1,0},{2,3},{3,2},{4,5},{5,4},{6,7},{7,6},{8,9},{9,8},{10,11... | collective-permute-start | bytes 786440 | tf_op jit(solution)/shard_map/ppermute | solution.py:422
  61.9 1.5 %collective-permute-start.7 = (bf16[128,8,128]{2,1,0:T(8,128)(2,1)S(1)}, bf16[128,8,128]{2,1,0:T(8,128)(2,1)S(1)}, u32[]{:S(2)}, u32[]{:S(2)}) collective-permute-start(bf16[128,8,128]{2,1,0:T(8,128)(2,1)S(1)} %collective-permute-done.4.refs_2_), channel_id=1, source_target_pairs={{0,1},{1,0},{2,3},{3,2},{4,5},{5,4},{6,7},{7,6},{8,9},{9,8},{10,11... | collective-permute-start | bytes 786440 | tf_op jit(solution)/shard_map/ppermute | solution.py:422

commit v2 on v1

--- a/solution.py
+++ b/solution.py
@@ -58,7 +58,10 @@
 
 def diffused(here, above, below, wet, rate, rest):
     columns = here.shape[1]
-    near = above + below + pltpu.roll(here, 1, 1) + pltpu.roll(here, columns - 1, 1)
+    rounded = here.astype(BF16)
+    left = pltpu.roll(rounded, 1, 1).astype(F32)
+    right = pltpu.roll(rounded, columns - 1, 1).astype(F32)
+    near = (above + below) + (left + right)
     return jnp.where(wet > 0.0, rate * near + rest * here, here)
 
 
@@ -97,22 +100,51 @@
         ).astype(BF16)
 
 
-def inner_kernel(*refs):
-    state_refs = refs[:-13]
-    forcing_ref, gain_ref, rate_ref, mixing_ref, export_ref, mask_ref = refs[-13:-7]
-    final_ref, edge_ref, surface_ref, even, odd, force, wet_ref = refs[-7:]
+def inner_kernel(
+    state_ref,
+    forcing_ref,
+    gain_ref,
+    rate_ref,
+    mixing_ref,
+    export_ref,
+    mask_ref,
+    final_ref,
+    edge_ref,
+    surface_ref,
+    even,
+    odd,
+    arrived,
+    force,
+    wet_ref,
+    sems,
+):
     fields, levels = gain_ref.shape
-    rows, columns = wet_ref.shape
+    rows, columns = mask_ref.shape
+    blocks = columns // TC
+
+    def arrival(group, block):
+        return pltpu.make_async_copy(
+            state_ref.at[:, pl.ds(group * 8, 8), pl.ds(block * TC, TC)],
+            arrived.at[group, block],
+            sems.at[group, block],
+        )
+
+    for group in range(rows // 8):
+        for block in range(blocks):
+            arrival(group, block).start()
     load_force(forcing_ref, force)
     wet_ref[...] = wetness_of(mask_ref[...])
     gain = gain_ref[...]
 
-    @pl.loop(0, rows // 4)
+    @pl.loop(0, rows // 8)
     def _(group):
-        for part in range(4):
-            row = group * 4 + part
+        for block in range(blocks):
+            arrival(group, block).wait()
+        state = [arrived.at[group, block].reshape(levels * 8, TC) for block in range(blocks)]
+        for part in range(8):
+            row = group * 8 + part
             pushed = rows_of(blocks_of(force), row, fields, rows).astype(BF16)
-            even[row] = rows_of(state_refs, row, levels, rows) + driven(gain, pushed)
+            even[row] = rows_of(state, part, levels, 8) + driven(gain, pushed)
 
     rate = column(rate_ref[...])
     rest = 1.0 - 4.0 * rate
@@ -123,7 +155,7 @@
         last = step == NSTEP
 
         todo = rows - 2 * step
-        at_once = max(n for n in (1, 2, 3, 4, 5) if todo % n == 0)
+        at_once = todo // 2
 
         @pl.loop(0, todo // at_once)
         def _(group, source=source, target=target, step=step, last=last, at_once=at_once):
@@ -197,29 +229,25 @@
         for side in range(2):
             first_wet = step if side == 0 else NSTEP - step
             shift = 0 if side == 0 else 2
-
-            @pl.loop(0, 1)
-            def _(pair):
-                for part in range(EDGE):
-                    row = EDGE * pair + part
-                    value = diffused(
-                        source[side, row + 1],
-                        source[side, row],
-                        source[side, row + 2],
-                        wet[side, pl.ds(first_wet + row, 1), :],
-                        rate,
-                        rest,
-                    )
-                    result = mixed(factor if last else step_factor, value)
-                    if last:
-                        final_ref[side, row] = result[:levels]
-                        surface = jnp.tanh(result[levels:]).astype(BF16)
-                        for tile in range(per_row):
-                            surface_ref[(side * (rows - EDGE) + row) * per_row + tile] = surface[
-                                :, tile * TC : (tile + 1) * TC
-                            ]
-                    else:
-                        target[side, row + shift] = result
+            for row in range(EDGE):
+                value = diffused(
+                    source[side, row + 1],
+                    source[side, row],
+                    source[side, row + 2],
+                    wet[side, first_wet + row : first_wet + row + 1, :],
+                    rate,
+                    rest,
+                )
+                result = mixed(factor if last else step_factor, value)
+                if last:
+                    final_ref[side, row] = result[:levels]
+                    surface = jnp.tanh(result[levels:]).astype(BF16)
+                    for tile in range(per_row):
+                        surface_ref[(side * (rows - EDGE) + row) * per_row + tile] = surface[
+                            :, tile * TC : (tile + 1) * TC
+                        ]
+                else:
+                    target[side, row + shift] = result
 
 
 def write_kernel(inner_ref, outer_ref, state_ref):
@@ -344,11 +372,7 @@
 
     inner_final, edges, inner_surface = pl.pallas_call(
         inner_kernel,
-        grid=(1,),
-        in_specs=[
-            pl.BlockSpec((levels * rows, TC), lambda i, j=index: (0, j)) for index in range(per_row)
-        ]
-        + [whole] * 6,
+        in_specs=[pl.BlockSpec(memory_space=pl.ANY)] + [whole] * 6,
         out_specs=[whole] * 3,
         out_shape=[
             jax.ShapeDtypeStruct((inner_rows, levels, columns), F32),
@@ -358,13 +382,15 @@
         scratch_shapes=[
             VMEM((rows, levels, columns), F32),
             VMEM((rows, levels, columns), F32),
+            VMEM((rows // 8, per_row, levels, 8, TC), F32),
             VMEM((per_row, fields * rows, TC), F32),
             VMEM((rows, columns), F32),
+            pltpu.SemaphoreType.DMA((rows // 8, per_row)),
         ],
         compiler_params=pltpu.CompilerParams(vmem_limit_bytes=32 * MIB),
         cost_estimate=pl.CostEstimate(flops=10**10, bytes_accessed=20 * MIB, transcendentals=0),
         name="inner",
-    )(*[in_hbm(column_state.reshape(levels * rows, columns))] * per_row, force, gain, rate, mixer, export, land_mask)
+    )(state, force, gain, rate, mixer, export, land_mask)
 
     outer_final, surface = pl.pallas_call(
         outer_kernel,

time: 70.2 us -> 60.5 us (0.86)
  Pallas kernels: 41.9 us -> 32.2 us
    pallas_call x1, Pallas kernels: 23 us -> 13.6 us  [on_device(): pl.pallas_call(inner_kernel, in_specs=[pl.BlockSpec(memory_space=pl.ANY)]...]
  transfers between devices with their start and end apart: 8 -> 8, of which waited for: 3 -> 3; matrix products, arithmetic and copies ran while one was open for 0% -> 1% of each run, Pallas kernels for 41% -> 32%
where the time goes in v2:
time: 60.5 us; the launch traced here: 60.2 us
  Pallas kernels  32.2 us (53%)
  starting transfers between devices  13.1 us (22%)
  waiting for transfers between devices  11.7 us (19%)
  local copies, waits for them, and re-layouts  2.53 us (4%)
  between operations  0.77 us (1%)
    pallas_call x1, Pallas kernels, on_device(): pl.pallas_call(inner_kernel, in_specs=[pl.BlockSpec(memory_space=pl.ANY)]...  13.6 us
    ppermute x1, waiting for transfers between devices, on_device(): before = lax.ppermute(here, 'blk', later)  7.92 us
    pallas_call x1, Pallas kernels, on_device(): pl.pallas_call(regrid_kernel, grid_spec=pltpu.PrefetchScalarGridSpec(num_...  6.48 us
    pallas_call x1, Pallas kernels, on_device(): pl.pallas_call(write_kernel, grid=(per_row,), in_specs=[pl.BlockSpec((inn...  5.75 us
    pallas_call x1, Pallas kernels, on_device(): pl.pallas_call(outer_kernel, in_specs=[whole] * 8, out_specs=[whole] * 2,...  4.35 us
    ppermute x1, starting transfers between devices, on_device(): before = lax.ppermute(here, 'blk', later)  4.05 us
    ppermute x1, starting transfers between devices, on_device(): after = lax.ppermute(here, 'blk', earlier)  3 us
    ppermute x1, starting transfers between devices, on_device(): low = lax.ppermute(up, 'blk', upward)  2.38 us
  transfers between devices with their start and end apart: 8, of which 3 were waited for; matrix products, arithmetic and copies ran while one was open for 1% of the time, Pallas kernels for 32%

profile of v2, /device:TPU:0, one launch (start us, length us, event | category | flops | bytes accessed | tf_op | source)
XLA Modules:
  0.0 60.2 jit_solution(11863463843270841476)
XLA Ops:
  0.6 0.0 copy-start.2
  0.6 0.0 copy-start.3
  0.7 0.0 copy-start.4
  0.7 2.0 %edges.1 = (bf16[272,512]{1,0:T(8,128)(2,1)S(1)}, bf16[272,512]{1,0:T(8,128)(2,1)S(1)}) custom-call(f32[64,32,512]{2,1,0:T(8,128)} %bitcast.14, f32[64,32,512]{2,1,0:T(8,128)} %bitcast.15, f32[64,32,512]{2,1,0:T(8,128)} %bitcast.16, f32[64,32,512]{2,1,0:T(8,128)} %bitcast.17, f32[64,32,512]{2,1,0:T(8,128)} %bitcast.18, f32[64,32,512]{2,1,0:T(8,128)} %bitcast.19, ...), custom_call_target="tpu_custom_call" | custom-call | flops 10000000 | bytes 3145728 | tf_op jit(solution)/shard_map/edges/pallas_call | solution.py:348
  2.7 2.4 %collective-permute-start = (bf16[272,512]{1,0:T(8,128)(2,1)S(1)}, bf16[272,512]{1,0:T(8,128)(2,1)S(1)}, u32[]{:S(2)}, u32[]{:S(2)}) collective-permute-start(bf16[272,512]{1,0:T(8,128)(2,1)S(1)} %get-tuple-element.12), channel_id=1, source_target_pairs={{0,1},{1,2},{2,3},{3,4},{4,5},{5,6},{6,7},{7,8},{8,9},{9,10},{10,1... | collective-permute-start | bytes 835592 | tf_op jit(solution)/shard_map/ppermute | solution.py:370
  5.1 1.3 %collective-permute-start.1 = (bf16[272,512]{1,0:T(8,128)(2,1)S(1)}, bf16[272,512]{1,0:T(8,128)(2,1)S(1)}, u32[]{:S(2)}, u32[]{:S(2)}) collective-permute-start(bf16[272,512]{1,0:T(8,128)(2,1)S(1)} %get-tuple-element.13), channel_id=1, source_target_pairs={{1,0},{2,1},{3,2},{4,3},{5,4},{6,5},{7,6},{8,7},{9,8},{10,9},{11,1... | collective-permute-start | bytes 835592 | tf_op jit(solution)/shard_map/ppermute | solution.py:371
  6.4 0.0 copy-done.2
  6.4 0.0 copy-done.3
  6.4 13.6 %inner.1 = (f32[24,64,512]{2,1,0:T(8,128)S(1)}, f32[2,4,2,64,512]{4,3,2,1,0:T(8,128)S(1)}, bf16[96,8,128]{2,1,0:T(8,128)(2,1)S(1)}) custom-call(f32[64,32,512]{2,1,0:T(8,128)} %bitcast.22, bf16[256,512]{1,0:T(8,128)(2,1)} %bitcast.26, bf16[8,64]{1,0:T(8,128)(2,1)} %bitcast.29, f32[1,64]{1,0:T(1,128)S(1)} %copy-done.4, f32[64,64]{1,0:T(8,128)S(1)} %bitcast.10, ...), custom_call_target="tpu_custom_call" | custom-call | flops 10000000000 | bytes 20971520 | tf_op jit(solution)/shard_map/inner/pallas_call | solution.py:373
  20.0 0.0 collective-permute-done.low_ref
  20.0 0.0 collective-permute-done.1.high_ref
  20.0 0.0 copy-start.5
  20.0 4.3 %outer.1 = (f32[2,4,64,512]{3,2,1,0:T(8,128)S(1)}, bf16[128,8,128]{2,1,0:T(8,128)(2,1)}) custom-call(bf16[272,512]{1,0:T(8,128)(2,1)S(1)} %collective-permute-done.low_ref, bf16[272,512]{1,0:T(8,128)(2,1)S(1)} %collective-permute-done.1.high_ref, f32[2,4,2,64,512]{4,3,2,1,0:T(8,128)S(1)} %get-tuple-element.14.edge_ref, f32[1,64]{1,0:T(1,128)S(1)} %copy-done.4, ...), custom_call_target="tpu_custom_call" | custom-call | flops 3000000000 | bytes 4194304 | tf_op jit(solution)/shard_map/outer/pallas_call | solution.py:395
  24.4 1.0 %copy-done = f32[2,4,64,512]{3,2,1,0:T(8,128)} copy-done((f32[2,4,64,512]{3,2,1,0:T(8,128)}, f32[2,4,64,512]{3,2,1,0:T(8,128)S(1)}, u32[]{:S(2)}) %copy-start) | copy-done | bytes 1048600
  25.3 2.3 %collective-permute-start.2 = (bf16[128,8,128]{2,1,0:T(8,128)(2,1)}, bf16[128,8,128]{2,1,0:T(8,128)(2,1)S(1)}, u32[]{:S(2)}, u32[]{:S(2)}) collective-permute-start(bf16[128,8,128]{2,1,0:T(8,128)(2,1)} %get-tuple-element.16), channel_id=1, source_target_pairs={{0,16},{16,0},{1,17},{17,1},{2,18},{18,2},{3,19},{19,3},{4,20},{20... | collective-permute-start | bytes 786440 | tf_op jit(solution)/shard_map/ppermute | solution.py:442
  27.7 0.1 copy.11
  27.8 0.2 reshape.20
  28.0 0.0 copy-start.1
  28.1 1.2 %copy-done.1 = f32[2,4,64,512]{3,2,1,0:T(8,128)S(1)} copy-done((f32[2,4,64,512]{3,2,1,0:T(8,128)S(1)}, f32[2,4,64,512]{3,2,1,0:T(8,128)}, u32[]{:S(2)}) %copy-start.1) | copy-done | bytes 1048600
  29.3 5.8 %write.1 = f32[2048,512]{1,0:T(8,128)} custom-call(f32[24,64,512]{2,1,0:T(8,128)S(1)} %get-tuple-element.17.inner_ref, f32[2,4,64,512]{3,2,1,0:T(8,128)S(1)} %copy-done.1), custom_call_target="tpu_custom_call" | custom-call | bytes 8388608 | tf_op jit(solution)/shard_map/write/pallas_call | solution.py:413
  35.0 0.0 collective-permute-done.2.refs_1_
  35.0 4.1 %collective-permute-start.3 = (bf16[128,8,128]{2,1,0:T(8,128)(2,1)S(1)}, bf16[128,8,128]{2,1,0:T(8,128)(2,1)S(1)}, u32[]{:S(2)}, u32[]{:S(2)}) collective-permute-start(bf16[128,8,128]{2,1,0:T(8,128)(2,1)S(1)} %collective-permute-done.2.refs_1_), channel_id=1, source_target_pairs={{0,2},{1,3},{2,4},{3,5},{4,6},{5,7},{6,8},{7,9},{8,10},{9,11},{10,... | collective-permute-start | bytes 786440 | tf_op jit(solution)/shard_map/ppermute | solution.py:444
  39.1 3.0 %collective-permute-start.4 = (bf16[128,8,128]{2,1,0:T(8,128)(2,1)S(1)}, bf16[128,8,128]{2,1,0:T(8,128)(2,1)S(1)}, u32[]{:S(2)}, u32[]{:S(2)}) collective-permute-start(bf16[128,8,128]{2,1,0:T(8,128)(2,1)S(1)} %collective-permute-done.2.refs_1_), channel_id=1, source_target_pairs={{0,14},{1,15},{2,0},{3,1},{4,2},{5,3},{6,4},{7,5},{8,6},{9,7},{10,... | collective-permute-start | bytes 786440 | tf_op jit(solution)/shard_map/ppermute | solution.py:445
  42.1 0.0 collective-permute-start.6
  42.1 7.9 %collective-permute-done.3.refs_0_ = bf16[128,8,128]{2,1,0:T(8,128)(2,1)S(1)} collective-permute-done((bf16[128,8,128]{2,1,0:T(8,128)(2,1)S(1)}, bf16[128,8,128]{2,1,0:T(8,128)(2,1)S(1)}, u32[]{:S(2)}, u32[]{:S(2)}) %collective-permute-start.3) | collective-permute-done | bytes 262176 | tf_op jit(solution)/shard_map/ppermute | solution.py:444
  50.0 0.0 collective-permute-start.5
  50.0 2.2 %collective-permute-done.4.refs_2_ = bf16[128,8,128]{2,1,0:T(8,128)(2,1)S(1)} collective-permute-done((bf16[128,8,128]{2,1,0:T(8,128)(2,1)S(1)}, bf16[128,8,128]{2,1,0:T(8,128)(2,1)S(1)}, u32[]{:S(2)}, u32[]{:S(2)}) %collective-permute-start.4) | collective-permute-done | bytes 262176 | tf_op jit(solution)/shard_map/ppermute | solution.py:445
  52.2 0.0 collective-permute-start.7
  52.2 0.0 collective-permute-done.6.refs_4_
  52.2 0.0 collective-permute-done.5.refs_3_
  52.2 1.5 %collective-permute-done.7.refs_5_ = bf16[128,8,128]{2,1,0:T(8,128)(2,1)S(1)} collective-permute-done((bf16[128,8,128]{2,1,0:T(8,128)(2,1)S(1)}, bf16[128,8,128]{2,1,0:T(8,128)(2,1)S(1)}, u32[]{:S(2)}, u32[]{:S(2)}) %collective-permute-start.7) | collective-permute-done | bytes 262176 | tf_op jit(solution)/shard_map/ppermute | solution.py:448
  53.7 6.5 %regrid.1 = bf16[256,512]{1,0:T(8,128)(2,1)} custom-call(s32[384]{0:T(512)S(1)} %fusion.6.position_ref, bf16[128,8,128]{2,1,0:T(8,128)(2,1)S(1)} %collective-permute-done.3.refs_0_, bf16[128,8,128]{2,1,0:T(8,128)(2,1)S(1)} %collective-permute-done.2.refs_1_, bf16[128,8,128]{2,1,0:T(8,128)(2,1)S(1)} %collective-permute-done.4.refs_2_, ...), custom_call_target="tpu_custom_call" | custom-call | flops 1000000000 | bytes 16777216 | tf_op jit(solution)/shard_map/regrid/pallas_call | solution.py:451
  (4 shorter events, 0.0 us)
Async XLA Ops:
  0.6 5.8 %copy-start.2 = (f32[1,64,64]{2,1,0:T(8,128)S(1)}, f32[1,64,64]{2,1,0:T(8,128)}, u32[]{:S(2)}) copy-start(f32[1,64,64]{2,1,0:T(8,128)} %param.13) | copy-start | bytes 49156
  0.6 5.8 %copy-start.3 = (f32[1,8,64]{2,1,0:T(8,128)S(1)}, f32[1,8,64]{2,1,0:T(8,128)}, u32[]{:S(2)}) copy-start(f32[1,8,64]{2,1,0:T(8,128)} %param.14) | copy-start | bytes 6148
  0.7 5.8 %copy-start.4 = (f32[1,64]{1,0:T(1,128)S(1)}, f32[1,64]{1,0:T(1,128)}, u32[]{:S(2)}) copy-start(f32[1,64]{1,0:T(1,128)} %rate_ref.3) | copy-start | bytes 772
  2.7 17.3 %collective-permute-start = (bf16[272,512]{1,0:T(8,128)(2,1)S(1)}, bf16[272,512]{1,0:T(8,128)(2,1)S(1)}, u32[]{:S(2)}, u32[]{:S(2)}) collective-permute-start(bf16[272,512]{1,0:T(8,128)(2,1)S(1)} %get-tuple-element.12), channel_id=1, source_target_pairs={{0,1},{1,2},{2,3},{3,4},{4,5},{5,6},{6,7},{7,8},{8,9},{9,10},{10,1... | collective-permute-start | bytes 835592 | tf_op jit(solution)/shard_map/ppermute | solution.py:370
  5.1 14.9 %collective-permute-start.1 = (bf16[272,512]{1,0:T(8,128)(2,1)S(1)}, bf16[272,512]{1,0:T(8,128)(2,1)S(1)}, u32[]{:S(2)}, u32[]{:S(2)}) collective-permute-start(bf16[272,512]{1,0:T(8,128)(2,1)S(1)} %get-tuple-element.13), channel_id=1, source_target_pairs={{1,0},{2,1},{3,2},{4,3},{5,4},{6,5},{7,6},{8,7},{9,8},{10,9},{11,1... | collective-permute-start | bytes 835592 | tf_op jit(solution)/shard_map/ppermute | solution.py:371
  20.0 7.7 %copy-start.5 = (s32[1,128,3]{1,0,2:T(1,128)S(1)}, s32[1,128,3]{1,0,2:T(1,128)}, u32[]{:S(2)}) copy-start(s32[1,128,3]{1,0,2:T(1,128)} %param.16) | copy-start | bytes 4612
  24.4 1.0 %copy-start = (f32[2,4,64,512]{3,2,1,0:T(8,128)}, f32[2,4,64,512]{3,2,1,0:T(8,128)S(1)}, u32[]{:S(2)}) copy-start(f32[2,4,64,512]{3,2,1,0:T(8,128)S(1)} %get-tuple-element.18.outer_ref) | copy-start | bytes 3145732
  25.3 9.7 %collective-permute-start.2 = (bf16[128,8,128]{2,1,0:T(8,128)(2,1)}, bf16[128,8,128]{2,1,0:T(8,128)(2,1)S(1)}, u32[]{:S(2)}, u32[]{:S(2)}) collective-permute-start(bf16[128,8,128]{2,1,0:T(8,128)(2,1)} %get-tuple-element.16), channel_id=1, source_target_pairs={{0,16},{16,0},{1,17},{17,1},{2,18},{18,2},{3,19},{19,3},{4,20},{20... | collective-permute-start | bytes 786440 | tf_op jit(solution)/shard_map/ppermute | solution.py:442
  28.0 1.2 %copy-start.1 = (f32[2,4,64,512]{3,2,1,0:T(8,128)S(1)}, f32[2,4,64,512]{3,2,1,0:T(8,128)}, u32[]{:S(2)}) copy-start(f32[2,4,64,512]{3,2,1,0:T(8,128)} %copy-done) | copy-start | bytes 3145732
  35.0 15.0 %collective-permute-start.3 = (bf16[128,8,128]{2,1,0:T(8,128)(2,1)S(1)}, bf16[128,8,128]{2,1,0:T(8,128)(2,1)S(1)}, u32[]{:S(2)}, u32[]{:S(2)}) collective-permute-start(bf16[128,8,128]{2,1,0:T(8,128)(2,1)S(1)} %collective-permute-done.2.refs_1_), channel_id=1, source_target_pairs={{0,2},{1,3},{2,4},{3,5},{4,6},{5,7},{6,8},{7,9},{8,10},{9,11},{10,... | collective-permute-start | bytes 786440 | tf_op jit(solution)/shard_map/ppermute | solution.py:444
  39.1 13.1 %collective-permute-start.4 = (bf16[128,8,128]{2,1,0:T(8,128)(2,1)S(1)}, bf16[128,8,128]{2,1,0:T(8,128)(2,1)S(1)}, u32[]{:S(2)}, u32[]{:S(2)}) collective-permute-start(bf16[128,8,128]{2,1,0:T(8,128)(2,1)S(1)} %collective-permute-done.2.refs_1_), channel_id=1, source_target_pairs={{0,14},{1,15},{2,0},{3,1},{4,2},{5,3},{6,4},{7,5},{8,6},{9,7},{10,... | collective-permute-start | bytes 786440 | tf_op jit(solution)/shard_map/ppermute | solution.py:445
  42.1 10.1 %collective-permute-start.6 = (bf16[128,8,128]{2,1,0:T(8,128)(2,1)S(1)}, bf16[128,8,128]{2,1,0:T(8,128)(2,1)S(1)}, u32[]{:S(2)}, u32[]{:S(2)}) collective-permute-start(bf16[128,8,128]{2,1,0:T(8,128)(2,1)S(1)} %collective-permute-done.2.refs_1_), channel_id=1, source_target_pairs={{0,1},{1,0},{2,3},{3,2},{4,5},{5,4},{6,7},{7,6},{8,9},{9,8},{10,11... | collective-permute-start | bytes 786440 | tf_op jit(solution)/shard_map/ppermute | solution.py:446
  50.0 2.2 %collective-permute-start.5 = (bf16[128,8,128]{2,1,0:T(8,128)(2,1)S(1)}, bf16[128,8,128]{2,1,0:T(8,128)(2,1)S(1)}, u32[]{:S(2)}, u32[]{:S(2)}) collective-permute-start(bf16[128,8,128]{2,1,0:T(8,128)(2,1)S(1)} %collective-permute-done.3.refs_0_), channel_id=1, source_target_pairs={{0,1},{1,0},{2,3},{3,2},{4,5},{5,4},{6,7},{7,6},{8,9},{9,8},{10,11... | collective-permute-start | bytes 786440 | tf_op jit(solution)/shard_map/ppermute | solution.py:448
  52.2 1.5 %collective-permute-start.7 = (bf16[128,8,128]{2,1,0:T(8,128)(2,1)S(1)}, bf16[128,8,128]{2,1,0:T(8,128)(2,1)S(1)}, u32[]{:S(2)}, u32[]{:S(2)}) collective-permute-start(bf16[128,8,128]{2,1,0:T(8,128)(2,1)S(1)} %collective-permute-done.4.refs_2_), channel_id=1, source_target_pairs={{0,1},{1,0},{2,3},{3,2},{4,5},{5,4},{6,7},{7,6},{8,9},{9,8},{10,11... | collective-permute-start | bytes 786440 | tf_op jit(solution)/shard_map/ppermute | solution.py:448

commit v3 on v2

--- a/solution.py
+++ b/solution.py
@@ -135,6 +135,10 @@
     load_force(forcing_ref, force)
     wet_ref[...] = wetness_of(mask_ref[...])
     gain = gain_ref[...]
+    rate = column(rate_ref[...])
+    rest = 1.0 - 4.0 * rate
+    factor = mixers(mixing_ref[...], export_ref[...])
+    step_factor = factor[:levels]
 
     @pl.loop(0, rows // 8)
     def _(group):
@@ -146,10 +150,6 @@
             pushed = rows_of(blocks_of(force), row, fields, rows).astype(BF16)
             even[row] = rows_of(state, part, levels, 8) + driven(gain, pushed)
 
-    rate = column(rate_ref[...])
-    rest = 1.0 - 4.0 * rate
-    factor = mixers(mixing_ref[...], export_ref[...])
-    step_factor = factor[:levels]
     for step in range(1, NSTEP + 1):
         source, target = (even, odd) if step % 2 else (odd, even)
         last = step == NSTEP
@@ -263,33 +263,42 @@
         state_ref[pl.ds(row + EDGE, levels, stride=rows), :] = inner_ref[row]
 
 
+def load_kernel(source_ref, target_ref, sems):
+    chunks = sems.shape[0]
+    size = source_ref.shape[0] // chunks
+    copies = [
+        pltpu.make_async_copy(
+            source_ref.at[pl.ds(chunk * size, size)],
+            target_ref.at[pl.ds(chunk * size, size)],
+            sems.at[chunk],
+        )
+        for chunk in range(chunks)
+    ]
+    for copy in copies:
+        copy.start()
+    for copy in copies:
+        copy.wait()
+
+
 def regrid_kernel(position_ref, *refs):
     piece_refs = refs[0:6]
-    weight_ref, out_ref, held, weights, sums, piece_sems, weight_sems = refs[6:]
+    weights, out_ref, held, sums, sems = refs[6:]
     tiles, fields, _ = piece_refs[0].shape
-    chunks = weight_sems.shape[0]
+    chunks = 4
     tiles_chunk = tiles // chunks
     per_row, total_rows, _ = sums.shape
     rows = total_rows // fields
-
-    def weight_copy(chunk):
-        part = pl.ds(chunk * tiles_chunk, tiles_chunk)
-        return pltpu.make_async_copy(weight_ref.at[part], weights.at[part], weight_sems.at[chunk])
-
     copies = [
-        pltpu.make_async_copy(source, held.at[pl.ds(slot * tiles, tiles)], piece_sems.at[slot])
-        for slot, source in enumerate(piece_refs)
+        pltpu.make_async_copy(source, held.at[pl.ds(index * tiles, tiles)], sems.at[index])
+        for index, source in enumerate(piece_refs)
     ]
     for copy in copies:
         copy.start()
-    for chunk in range(chunks):
-        weight_copy(chunk).start()
     for copy in copies:
         copy.wait()
 
     @pl.loop(0, chunks)
     def _(chunk):
-        weight_copy(chunk).wait()
         for pair in range(tiles_chunk // 2):
             first = chunk * tiles_chunk + 2 * pair
             lefts = []
@@ -343,6 +352,7 @@
     mixer = mixing[0]
     export = export_map[0]
     whole = pl.BlockSpec(memory_space=VMEM)
+    anywhere = pl.BlockSpec(memory_space=pl.ANY)
 
     payload = levels * EDGE + 16
     down, up = pl.pallas_call(
@@ -375,9 +385,9 @@
         in_specs=[pl.BlockSpec(memory_space=pl.ANY)] + [whole] * 6,
         out_specs=[whole] * 3,
         out_shape=[
-            jax.ShapeDtypeStruct((inner_rows, levels, columns), F32),
-            jax.ShapeDtypeStruct((2, NSTEP, 2, levels, columns), F32),
-            jax.ShapeDtypeStruct((inner_tiles, fields, TC), BF16),
+            VMEM((inner_rows, levels, columns), F32),
+            VMEM((2, NSTEP, 2, levels, columns), F32),
+            VMEM((inner_tiles, fields, TC), BF16),
         ],
         scratch_shapes=[
             VMEM((rows, levels, columns), F32),
@@ -387,7 +397,7 @@
             VMEM((rows, columns), F32),
             pltpu.SemaphoreType.DMA((rows // 8, per_row)),
         ],
-        compiler_params=pltpu.CompilerParams(vmem_limit_bytes=32 * MIB),
+        compiler_params=pltpu.CompilerParams(vmem_limit_bytes=18 * MIB),
         cost_estimate=pl.CostEstimate(flops=10**10, bytes_accessed=20 * MIB, transcendentals=0),
         name="inner",
     )(state, force, gain, rate, mixer, export, land_mask)
@@ -397,8 +407,8 @@
         in_specs=[whole] * 8,
         out_specs=[whole] * 2,
         out_shape=[
-            jax.ShapeDtypeStruct((2, EDGE, levels, columns), F32),
-            jax.ShapeDtypeStruct((tiles, fields, TC), BF16),
+            VMEM((2, EDGE, levels, columns), F32),
+            VMEM((tiles, fields, TC), BF16),
         ],
         scratch_shapes=[
             VMEM((2, EDGE + 2, levels, columns), F32),
@@ -410,6 +420,40 @@
         name="outer",
     )(low, high, edges, rate, mixer, export, land_mask, inner_surface)
 
+    section_count = lax.axis_size("sec")
+    across = [(i, section_count - 1 - i) for i in range(section_count)]
+    later = [(i, (i + 2) % count) for i in range(count)]
+    earlier = [(i, (i - 2) % count) for i in range(count)]
+    mates = [(i, i ^ 1) for i in range(count)]
+
+    core = shard % 2
+    wanted = sources.reshape(-1)
+    away = wanted // tiles - (shard - core) + 2
+    away = away % count
+    same_core = away % 2 == core
+    positions = (jnp.where(same_core, 0, 3) + away // 2) * tiles + wanted % tiles
+
+    weights = in_hbm(regrid_weights.reshape(tiles, OV * TC, TC))
+
+    raw = regrid_weights.reshape(tiles, OV * TC, TC)
+    raw, surface = lax.optimization_barrier((raw, surface))
+    here = lax.ppermute(surface, "sec", across)
+    weights = pl.pallas_call(
+        load_kernel,
+        in_specs=[anywhere],
+        out_specs=whole,
+        out_shape=VMEM((tiles, OV * TC, TC), BF16),
+        scratch_shapes=[pltpu.SemaphoreType.DMA((16,))],
+        compiler_params=pltpu.CompilerParams(vmem_limit_bytes=16 * MIB),
+        cost_estimate=pl.CostEstimate(flops=0, bytes_accessed=12 * MIB, transcendentals=0),
+        name="load",
+    )(in_hbm(raw))
+    here, positions, inner_final, outer_final, weights = lax.optimization_barrier(
+        (here, positions, inner_final, outer_final, weights)
+    )
+    before = lax.ppermute(here, "blk", later)
+    after = lax.ppermute(here, "blk", earlier)
+    other = lax.ppermute(here, "blk", mates)
     new_state = pl.pallas_call(
         write_kernel,
         grid=(per_row,),
@@ -419,52 +463,29 @@
         ],
         out_specs=pl.BlockSpec((levels * rows, TC), lambda j: (0, j)),
         out_shape=jax.ShapeDtypeStruct((levels * rows, columns), F32),
-        compiler_params=pltpu.CompilerParams(vmem_limit_bytes=16 * MIB),
+        compiler_params=pltpu.CompilerParams(vmem_limit_bytes=8 * MIB),
         cost_estimate=pl.CostEstimate(flops=0, bytes_accessed=8 * MIB, transcendentals=0),
         name="write",
     )(inner_final, outer_final)
-
-    section_count = lax.axis_size("sec")
-    across = [(i, section_count - 1 - i) for i in range(section_count)]
-    later = [(i, (i + 2) % count) for i in range(count)]
-    earlier = [(i, (i - 2) % count) for i in range(count)]
-    mates = [(i, i ^ 1) for i in range(count)]
-
-    core = shard % 2
-    wanted = sources.reshape(-1)
-    away = wanted // tiles - (shard - core) + 2
-    away = away % count
-    same_core = away % 2 == core
-    positions = (jnp.where(same_core, 0, 3) + away // 2) * tiles + wanted % tiles
-
-    weights = in_hbm(regrid_weights.reshape(tiles, OV * TC, TC))
-
-    here = lax.ppermute(surface, "sec", across)
-    here, new_state, positions = lax.optimization_barrier((here, new_state, positions))
-    before = lax.ppermute(here, "blk", later)
-    after = lax.ppermute(here, "blk", earlier)
-    other = lax.ppermute(here, "blk", mates)
+    before, after, other, new_state = lax.optimization_barrier((before, after, other, new_state))
     pieces = [before, here, after]
     pieces += [lax.ppermute(before, "blk", mates), other, lax.ppermute(after, "blk", mates)]
 
-    anywhere = pl.BlockSpec(memory_space=pl.ANY)
     coupled = pl.pallas_call(
         regrid_kernel,
         grid_spec=pltpu.PrefetchScalarGridSpec(
             num_scalar_prefetch=1,
             grid=(1,),
-            in_specs=[anywhere] * 7,
+            in_specs=[anywhere] * 6 + [whole],
             out_specs=pl.BlockSpec((fields * rows, columns), lambda i, p: (0, 0)),
             scratch_shapes=[
                 VMEM((6 * tiles, fields, TC), BF16),
-                VMEM((tiles, OV * TC, TC), BF16),
                 VMEM((per_row, fields * rows, TC), F32),
                 pltpu.SemaphoreType.DMA((6,)),
-                pltpu.SemaphoreType.DMA((16,)),
             ],
         ),
         out_shape=jax.ShapeDtypeStruct((fields * rows, columns), BF16),
-        compiler_params=pltpu.CompilerParams(vmem_limit_bytes=24 * MIB),
+        compiler_params=pltpu.CompilerParams(vmem_limit_bytes=8 * MIB),
         cost_estimate=pl.CostEstimate(flops=10**9, bytes_accessed=16 * MIB, transcendentals=0),
         name="regrid",
     )(positions, *pieces, weights)

time: 60.5 us -> 57.3 us (0.947)
  waiting for transfers between devices: 11.7 us -> 7.1 us
  Pallas kernels: 32.2 us -> 34 us
  local copies, waits for them, and re-layouts: 2.53 us -> 1.31 us
  starting transfers between devices: 13.1 us -> 13.8 us
    pallas_call x0 -> x1, Pallas kernels: none -> 4.81 us  [on_device(): pl.pallas_call(load_kernel, in_specs=[anywhere], out_specs=whole, out_sha...]
    ppermute x1, starting transfers between devices: 4.05 us -> 0.01 us  [on_device(): before = lax.ppermute(here, 'blk', later)]
    ppermute x1, waiting for transfers between devices: 7.92 us -> 4.9 us  [on_device(): before = lax.ppermute(here, 'blk', later)]
    pallas_call x1, Pallas kernels: 6.48 us -> 3.74 us  [on_device(): pl.pallas_call(regrid_kernel, grid_spec=pltpu.PrefetchScalarGridSpec(num_...]
    ppermute x1, starting transfers between devices: 3 us -> 5.39 us  [on_device(): after = lax.ppermute(here, 'blk', earlier)]
    ppermute x1, starting transfers between devices: 0.01 us -> 1.89 us  [on_device(): other = lax.ppermute(here, 'blk', mates)]
    ppermute x1, waiting for transfers between devices: 2.2 us -> 0.47 us  [on_device(): after = lax.ppermute(here, 'blk', earlier)]
    unnamed x13, local copies, waits for them, and re-layouts: 2.32 us -> 1.11 us
  transfers between devices with their start and end apart: 8 -> 8, of which waited for: 3 -> 5; matrix products, arithmetic and copies ran while one was open for 1% -> 1% of each run, Pallas kernels for 32% -> 42%
where the time goes in v3:
time: 57.3 us; the launch traced here: 57 us
  Pallas kernels  34 us (59%)
  starting transfers between devices  13.8 us (24%)
  waiting for transfers between devices  7.1 us (12%)
  local copies, waits for them, and re-layouts  1.31 us (2%)
  between operations  0.76 us (1%)
    pallas_call x1, Pallas kernels, on_device(): pl.pallas_call(inner_kernel, in_specs=[pl.BlockSpec(memory_space=pl.ANY)]...  13.5 us
    pallas_call x1, Pallas kernels, on_device(): pl.pallas_call(write_kernel, grid=(per_row,), in_specs=[pl.BlockSpec((inn...  5.75 us
    ppermute x1, starting transfers between devices, on_device(): after = lax.ppermute(here, 'blk', earlier)  5.39 us
    ppermute x1, waiting for transfers between devices, on_device(): before = lax.ppermute(here, 'blk', later)  4.9 us
    pallas_call x1, Pallas kernels, on_device(): pl.pallas_call(load_kernel, in_specs=[anywhere], out_specs=whole, out_sha...  4.81 us
    pallas_call x1, Pallas kernels, on_device(): pl.pallas_call(outer_kernel, in_specs=[whole] * 8, out_specs=[whole] * 2,...  4.24 us
    pallas_call x1, Pallas kernels, on_device(): pl.pallas_call(regrid_kernel, grid_spec=pltpu.PrefetchScalarGridSpec(num_...  3.74 us
    ppermute x1, starting transfers between devices, on_device(): low = lax.ppermute(up, 'blk', upward)  2.38 us
  transfers between devices with their start and end apart: 8, of which 5 were waited for; matrix products, arithmetic and copies ran while one was open for 1% of the time, Pallas kernels for 42%

profile of v3, /device:TPU:0, one launch (start us, length us, event | category | flops | bytes accessed | tf_op | source)
XLA Modules:
  0.0 57.0 jit_solution(992479004897297502)
XLA Ops:
  0.6 0.0 copy-start.2
  0.6 0.0 copy-start.3
  0.7 0.0 copy-start.4
  0.7 2.0 %edges.1 = (bf16[272,512]{1,0:T(8,128)(2,1)S(1)}, bf16[272,512]{1,0:T(8,128)(2,1)S(1)}) custom-call(f32[64,32,512]{2,1,0:T(8,128)} %bitcast.14, f32[64,32,512]{2,1,0:T(8,128)} %bitcast.15, f32[64,32,512]{2,1,0:T(8,128)} %bitcast.16, f32[64,32,512]{2,1,0:T(8,128)} %bitcast.17, f32[64,32,512]{2,1,0:T(8,128)} %bitcast.18, f32[64,32,512]{2,1,0:T(8,128)} %bitcast.19, ...), custom_call_target="tpu_custom_call" | custom-call | flops 10000000 | bytes 3145728 | tf_op jit(solution)/shard_map/edges/pallas_call | solution.py:358
  2.7 2.4 %collective-permute-start = (bf16[272,512]{1,0:T(8,128)(2,1)S(1)}, bf16[272,512]{1,0:T(8,128)(2,1)S(1)}, u32[]{:S(2)}, u32[]{:S(2)}) collective-permute-start(bf16[272,512]{1,0:T(8,128)(2,1)S(1)} %get-tuple-element.20), channel_id=1, source_target_pairs={{0,1},{1,2},{2,3},{3,4},{4,5},{5,6},{6,7},{7,8},{8,9},{9,10},{10,1... | collective-permute-start | bytes 835592 | tf_op jit(solution)/shard_map/ppermute | solution.py:380
  5.1 1.3 %collective-permute-start.1 = (bf16[272,512]{1,0:T(8,128)(2,1)S(1)}, bf16[272,512]{1,0:T(8,128)(2,1)S(1)}, u32[]{:S(2)}, u32[]{:S(2)}) collective-permute-start(bf16[272,512]{1,0:T(8,128)(2,1)S(1)} %get-tuple-element.21), channel_id=1, source_target_pairs={{1,0},{2,1},{3,2},{4,3},{5,4},{6,5},{7,6},{8,7},{9,8},{10,9},{11,1... | collective-permute-start | bytes 835592 | tf_op jit(solution)/shard_map/ppermute | solution.py:381
  6.4 0.0 copy-done.2
  6.4 0.0 copy-done.3
  6.4 13.5 %inner.1 = (f32[24,64,512]{2,1,0:T(8,128)S(1)}, f32[2,4,2,64,512]{4,3,2,1,0:T(8,128)S(1)}, bf16[96,8,128]{2,1,0:T(8,128)(2,1)S(1)}) custom-call(f32[64,32,512]{2,1,0:T(8,128)} %bitcast.22, bf16[256,512]{1,0:T(8,128)(2,1)} %bitcast.26, bf16[8,64]{1,0:T(8,128)(2,1)} %bitcast.29, f32[1,64]{1,0:T(1,128)S(1)} %copy-done.4, f32[64,64]{1,0:T(8,128)S(1)} %bitcast.10, ...), custom_call_target="tpu_custom_call" | custom-call | flops 10000000000 | bytes 20971520 | tf_op jit(solution)/shard_map/inner/pallas_call | solution.py:383
  19.9 0.0 collective-permute-done.low_ref
  19.9 0.0 collective-permute-done.1.high_ref
  19.9 0.0 copy-start.5
  19.9 4.2 %outer.1 = (f32[2,4,64,512]{3,2,1,0:T(8,128)S(1)}, bf16[128,8,128]{2,1,0:T(8,128)(2,1)}) custom-call(bf16[272,512]{1,0:T(8,128)(2,1)S(1)} %collective-permute-done.low_ref, bf16[272,512]{1,0:T(8,128)(2,1)S(1)} %collective-permute-done.1.high_ref, f32[2,4,2,64,512]{4,3,2,1,0:T(8,128)S(1)} %get-tuple-element.22.edge_ref, f32[1,64]{1,0:T(1,128)S(1)} %copy-done.4, ...), custom_call_target="tpu_custom_call" | custom-call | flops 3000000000 | bytes 4194304 | tf_op jit(solution)/shard_map/outer/pallas_call | solution.py:405
  24.2 1.0 %copy-done = f32[2,4,64,512]{3,2,1,0:T(8,128)} copy-done((f32[2,4,64,512]{3,2,1,0:T(8,128)}, f32[2,4,64,512]{3,2,1,0:T(8,128)S(1)}, u32[]{:S(2)}) %copy-start) | copy-done | bytes 1048600
  25.1 2.3 %collective-permute-start.2 = (bf16[128,8,128]{2,1,0:T(8,128)(2,1)}, bf16[128,8,128]{2,1,0:T(8,128)(2,1)S(1)}, u32[]{:S(2)}, u32[]{:S(2)}) collective-permute-start(bf16[128,8,128]{2,1,0:T(8,128)(2,1)} %get-tuple-element.25), channel_id=1, source_target_pairs={{0,16},{16,0},{1,17},{17,1},{2,18},{18,2},{3,19},{19,3},{4,20},{20... | collective-permute-start | bytes 786440 | tf_op jit(solution)/shard_map/ppermute | solution.py:440
  27.5 0.1 copy.11
  27.6 0.2 reshape.21
  27.8 0.0 copy-start.1
  27.8 4.8 %load.1.refs_6_ = bf16[128,384,128]{2,1,0:T(8,128)(2,1)S(1)} custom-call(bf16[128,384,128]{2,1,0:T(8,128)(2,1)} %bitcast.23), custom_call_target="tpu_custom_call" | custom-call | bytes 12582912 | tf_op jit(solution)/shard_map/load/pallas_call | solution.py:441
  32.6 0.3 collective-permute-done.2.refs_1_
  33.0 1.9 %collective-permute-start.5 = (bf16[128,8,128]{2,1,0:T(8,128)(2,1)S(1)}, bf16[128,8,128]{2,1,0:T(8,128)(2,1)S(1)}, u32[]{:S(2)}, u32[]{:S(2)}) collective-permute-start(bf16[128,8,128]{2,1,0:T(8,128)(2,1)S(1)} %collective-permute-done.2.refs_1_), channel_id=1, source_target_pairs={{0,1},{1,0},{2,3},{3,2},{4,5},{5,4},{6,7},{7,6},{8,9},{9,8},{10,11... | collective-permute-start | bytes 786440 | tf_op jit(solution)/shard_map/ppermute | solution.py:456
  34.9 5.4 %collective-permute-start.4 = (bf16[128,8,128]{2,1,0:T(8,128)(2,1)S(1)}, bf16[128,8,128]{2,1,0:T(8,128)(2,1)S(1)}, u32[]{:S(2)}, u32[]{:S(2)}) collective-permute-start(bf16[128,8,128]{2,1,0:T(8,128)(2,1)S(1)} %collective-permute-done.2.refs_1_), channel_id=1, source_target_pairs={{0,14},{1,15},{2,0},{3,1},{4,2},{5,3},{6,4},{7,5},{8,6},{9,7},{10,... | collective-permute-start | bytes 786440 | tf_op jit(solution)/shard_map/ppermute | solution.py:455
  40.2 0.0 collective-permute-start.3
  40.3 5.8 %write.1 = f32[2048,512]{1,0:T(8,128)} custom-call(f32[24,64,512]{2,1,0:T(8,128)S(1)} %get-tuple-element.30.inner_ref, f32[2,4,64,512]{3,2,1,0:T(8,128)S(1)} %copy-done.1), custom_call_target="tpu_custom_call" | custom-call | bytes 8388608 | tf_op jit(solution)/shard_map/write/pallas_call | solution.py:457
  46.0 0.0 collective-permute-done.5.refs_4_
  46.0 0.5 collective-permute-done.4.refs_2_
  46.5 4.9 %collective-permute-done.3.refs_0_ = bf16[128,8,128]{2,1,0:T(8,128)(2,1)S(1)} collective-permute-done((bf16[128,8,128]{2,1,0:T(8,128)(2,1)S(1)}, bf16[128,8,128]{2,1,0:T(8,128)(2,1)S(1)}, u32[]{:S(2)}, u32[]{:S(2)}) %collective-permute-start.3) | collective-permute-done | bytes 262176 | tf_op jit(solution)/shard_map/ppermute | solution.py:454
  51.4 0.0 collective-permute-start.6
  51.4 0.5 collective-permute-start.7
  51.9 1.0 %collective-permute-done.6.refs_3_ = bf16[128,8,128]{2,1,0:T(8,128)(2,1)S(1)} collective-permute-done((bf16[128,8,128]{2,1,0:T(8,128)(2,1)S(1)}, bf16[128,8,128]{2,1,0:T(8,128)(2,1)S(1)}, u32[]{:S(2)}, u32[]{:S(2)}) %collective-permute-start.6) | collective-permute-done | bytes 262176 | tf_op jit(solution)/shard_map/ppermute | solution.py:472
  52.9 0.4 collective-permute-done.7.refs_5_
  53.3 3.7 %regrid.1 = bf16[256,512]{1,0:T(8,128)(2,1)} custom-call(s32[384]{0:T(512)S(1)} %fusion.6.position_ref, bf16[128,8,128]{2,1,0:T(8,128)(2,1)S(1)} %collective-permute-done.3.refs_0_, bf16[128,8,128]{2,1,0:T(8,128)(2,1)S(1)} %collective-permute-done.2.refs_1_, bf16[128,8,128]{2,1,0:T(8,128)(2,1)S(1)} %collective-permute-done.4.refs_2_, ...), custom_call_target="tpu_custom_call" | custom-call | flops 1000000000 | bytes 16777216 | tf_op jit(solution)/shard_map/regrid/pallas_call | solution.py:474
  (5 shorter events, 0.0 us)
Async XLA Ops:
  0.6 5.8 %copy-start.2 = (f32[1,64,64]{2,1,0:T(8,128)S(1)}, f32[1,64,64]{2,1,0:T(8,128)}, u32[]{:S(2)}) copy-start(f32[1,64,64]{2,1,0:T(8,128)} %param.13) | copy-start | bytes 49156
  0.6 5.8 %copy-start.3 = (f32[1,8,64]{2,1,0:T(8,128)S(1)}, f32[1,8,64]{2,1,0:T(8,128)}, u32[]{:S(2)}) copy-start(f32[1,8,64]{2,1,0:T(8,128)} %param.14) | copy-start | bytes 6148
  0.7 5.8 %copy-start.4 = (f32[1,64]{1,0:T(1,128)S(1)}, f32[1,64]{1,0:T(1,128)}, u32[]{:S(2)}) copy-start(f32[1,64]{1,0:T(1,128)} %rate_ref.3) | copy-start | bytes 772
  2.7 17.2 %collective-permute-start = (bf16[272,512]{1,0:T(8,128)(2,1)S(1)}, bf16[272,512]{1,0:T(8,128)(2,1)S(1)}, u32[]{:S(2)}, u32[]{:S(2)}) collective-permute-start(bf16[272,512]{1,0:T(8,128)(2,1)S(1)} %get-tuple-element.20), channel_id=1, source_target_pairs={{0,1},{1,2},{2,3},{3,4},{4,5},{5,6},{6,7},{7,8},{8,9},{9,10},{10,1... | collective-permute-start | bytes 835592 | tf_op jit(solution)/shard_map/ppermute | solution.py:380
  5.1 14.8 %collective-permute-start.1 = (bf16[272,512]{1,0:T(8,128)(2,1)S(1)}, bf16[272,512]{1,0:T(8,128)(2,1)S(1)}, u32[]{:S(2)}, u32[]{:S(2)}) collective-permute-start(bf16[272,512]{1,0:T(8,128)(2,1)S(1)} %get-tuple-element.21), channel_id=1, source_target_pairs={{1,0},{2,1},{3,2},{4,3},{5,4},{6,5},{7,6},{8,7},{9,8},{10,9},{11,1... | collective-permute-start | bytes 835592 | tf_op jit(solution)/shard_map/ppermute | solution.py:381
  19.9 7.6 %copy-start.5 = (s32[1,128,3]{1,0,2:T(1,128)S(1)}, s32[1,128,3]{1,0,2:T(1,128)}, u32[]{:S(2)}) copy-start(s32[1,128,3]{1,0,2:T(1,128)} %param.16) | copy-start | bytes 4612
  24.2 1.0 %copy-start = (f32[2,4,64,512]{3,2,1,0:T(8,128)}, f32[2,4,64,512]{3,2,1,0:T(8,128)S(1)}, u32[]{:S(2)}) copy-start(f32[2,4,64,512]{3,2,1,0:T(8,128)S(1)} %get-tuple-element.31.outer_ref) | copy-start | bytes 3145732
  25.1 7.8 %collective-permute-start.2 = (bf16[128,8,128]{2,1,0:T(8,128)(2,1)}, bf16[128,8,128]{2,1,0:T(8,128)(2,1)S(1)}, u32[]{:S(2)}, u32[]{:S(2)}) collective-permute-start(bf16[128,8,128]{2,1,0:T(8,128)(2,1)} %get-tuple-element.25), channel_id=1, source_target_pairs={{0,16},{16,0},{1,17},{17,1},{2,18},{18,2},{3,19},{19,3},{4,20},{20... | collective-permute-start | bytes 786440 | tf_op jit(solution)/shard_map/ppermute | solution.py:440
  27.8 12.4 %copy-start.1 = (f32[2,4,64,512]{3,2,1,0:T(8,128)S(1)}, f32[2,4,64,512]{3,2,1,0:T(8,128)}, u32[]{:S(2)}) copy-start(f32[2,4,64,512]{3,2,1,0:T(8,128)} %copy-done) | copy-start | bytes 3145732
  33.0 13.0 %collective-permute-start.5 = (bf16[128,8,128]{2,1,0:T(8,128)(2,1)S(1)}, bf16[128,8,128]{2,1,0:T(8,128)(2,1)S(1)}, u32[]{:S(2)}, u32[]{:S(2)}) collective-permute-start(bf16[128,8,128]{2,1,0:T(8,128)(2,1)S(1)} %collective-permute-done.2.refs_1_), channel_id=1, source_target_pairs={{0,1},{1,0},{2,3},{3,2},{4,5},{5,4},{6,7},{7,6},{8,9},{9,8},{10,11... | collective-permute-start | bytes 786440 | tf_op jit(solution)/shard_map/ppermute | solution.py:456
  34.9 11.6 %collective-permute-start.4 = (bf16[128,8,128]{2,1,0:T(8,128)(2,1)S(1)}, bf16[128,8,128]{2,1,0:T(8,128)(2,1)S(1)}, u32[]{:S(2)}, u32[]{:S(2)}) collective-permute-start(bf16[128,8,128]{2,1,0:T(8,128)(2,1)S(1)} %collective-permute-done.2.refs_1_), channel_id=1, source_target_pairs={{0,14},{1,15},{2,0},{3,1},{4,2},{5,3},{6,4},{7,5},{8,6},{9,7},{10,... | collective-permute-start | bytes 786440 | tf_op jit(solution)/shard_map/ppermute | solution.py:455
  40.2 11.1 %collective-permute-start.3 = (bf16[128,8,128]{2,1,0:T(8,128)(2,1)S(1)}, bf16[128,8,128]{2,1,0:T(8,128)(2,1)S(1)}, u32[]{:S(2)}, u32[]{:S(2)}) collective-permute-start(bf16[128,8,128]{2,1,0:T(8,128)(2,1)S(1)} %collective-permute-done.2.refs_1_), channel_id=1, source_target_pairs={{0,2},{1,3},{2,4},{3,5},{4,6},{5,7},{6,8},{7,9},{8,10},{9,11},{10,... | collective-permute-start | bytes 786440 | tf_op jit(solution)/shard_map/ppermute | solution.py:454
  51.4 1.5 %collective-permute-start.6 = (bf16[128,8,128]{2,1,0:T(8,128)(2,1)S(1)}, bf16[128,8,128]{2,1,0:T(8,128)(2,1)S(1)}, u32[]{:S(2)}, u32[]{:S(2)}) collective-permute-start(bf16[128,8,128]{2,1,0:T(8,128)(2,1)S(1)} %collective-permute-done.3.refs_0_), channel_id=1, source_target_pairs={{0,1},{1,0},{2,3},{3,2},{4,5},{5,4},{6,7},{7,6},{8,9},{9,8},{10,11... | collective-permute-start | bytes 786440 | tf_op jit(solution)/shard_map/ppermute | solution.py:472
  51.4 1.9 %collective-permute-start.7 = (bf16[128,8,128]{2,1,0:T(8,128)(2,1)S(1)}, bf16[128,8,128]{2,1,0:T(8,128)(2,1)S(1)}, u32[]{:S(2)}, u32[]{:S(2)}) collective-permute-start(bf16[128,8,128]{2,1,0:T(8,128)(2,1)S(1)} %collective-permute-done.4.refs_2_), channel_id=1, source_target_pairs={{0,1},{1,0},{2,3},{3,2},{4,5},{5,4},{6,7},{7,6},{8,9},{9,8},{10,11... | collective-permute-start | bytes 786440 | tf_op jit(solution)/shard_map/ppermute | solution.py:472

commit v4 on v3

--- a/solution.py
+++ b/solution.py
@@ -56,13 +56,13 @@
     return [ref.at[index] for index in range(ref.shape[0])]
 
 
-def diffused(here, above, below, wet, rate, rest):
+def diffused(here, above, below, wet, rate):
     columns = here.shape[1]
     rounded = here.astype(BF16)
     left = pltpu.roll(rounded, 1, 1).astype(F32)
     right = pltpu.roll(rounded, columns - 1, 1).astype(F32)
     near = (above + below) + (left + right)
-    return jnp.where(wet > 0.0, rate * near + rest * here, here)
+    return here + wet * (rate * (near - 4.0 * here))
 
 
 def mixed(factor, value):
@@ -136,12 +136,10 @@
     wet_ref[...] = wetness_of(mask_ref[...])
     gain = gain_ref[...]
     rate = column(rate_ref[...])
-    rest = 1.0 - 4.0 * rate
     factor = mixers(mixing_ref[...], export_ref[...])
     step_factor = factor[:levels]
 
-    @pl.loop(0, rows // 8)
-    def _(group):
+    for group in range(rows // 8):
         for block in range(blocks):
             arrival(group, block).wait()
         state = [arrived.at[group, block].reshape(levels * 8, TC) for block in range(blocks)]
@@ -154,32 +152,26 @@
         source, target = (even, odd) if step % 2 else (odd, even)
         last = step == NSTEP
 
-        todo = rows - 2 * step
-        at_once = todo // 2
-
-        @pl.loop(0, todo // at_once)
-        def _(group, source=source, target=target, step=step, last=last, at_once=at_once):
-            for part in range(at_once):
-                row = step + at_once * group + part
-                value = diffused(
-                    source[row],
-                    source[row - 1],
-                    source[row + 1],
-                    wet_ref[pl.ds(row, 1), :],
-                    rate,
-                    rest,
-                )
-                result = mixed(factor if last else step_factor, value)
-                if last:
-                    final_ref[row - EDGE] = result[:levels]
-                    surface = jnp.tanh(result[levels:]).astype(BF16)
-                    per_row = columns // TC
-                    for tile in range(per_row):
-                        surface_ref[(row - EDGE) * per_row + tile] = surface[
-                            :, tile * TC : (tile + 1) * TC
-                        ]
-                else:
-                    target[row] = result
+
+        for row in range(step, rows - step):
+            value = diffused(
+                source[row],
+                source[row - 1],
+                source[row + 1],
+                wet_ref[row : row + 1, :],
+                rate,
+            )
+            result = mixed(factor if last else step_factor, value)
+            if last:
+                final_ref[row - EDGE] = result[:levels]
+                surface = jnp.tanh(result[levels:]).astype(BF16)
+                per_row = columns // TC
+                for tile in range(per_row):
+                    surface_ref[(row - EDGE) * per_row + tile] = surface[
+                        :, tile * TC : (tile + 1) * TC
+                    ]
+            else:
+                target[row] = result
 
     for step in range(NSTEP):
         source = odd if step % 2 else even
@@ -209,7 +201,6 @@
     inner_tiles = inner_ref.shape[0]
     per_row = columns // TC
     rate = column(rate_ref[...])
-    rest = 1.0 - 4.0 * rate
     factor = mixers(mixing_ref[...], export_ref[...])
     step_factor = factor[:levels]
     wet[0, 0:EDGE, :] = low_ref[levels * EDGE :, :].astype(F32)[0:EDGE]
@@ -236,7 +227,6 @@
                     source[side, row + 2],
                     wet[side, first_wet + row : first_wet + row + 1, :],
                     rate,
-                    rest,
                 )
                 result = mixed(factor if last else step_factor, value)
                 if last:
@@ -453,7 +443,6 @@
     )
     before = lax.ppermute(here, "blk", later)
     after = lax.ppermute(here, "blk", earlier)
-    other = lax.ppermute(here, "blk", mates)
     new_state = pl.pallas_call(
         write_kernel,
         grid=(per_row,),
@@ -467,7 +456,8 @@
         cost_estimate=pl.CostEstimate(flops=0, bytes_accessed=8 * MIB, transcendentals=0),
         name="write",
     )(inner_final, outer_final)
-    before, after, other, new_state = lax.optimization_barrier((before, after, other, new_state))
+    late, new_state = lax.optimization_barrier((here, new_state))
+    other = lax.ppermute(late, "blk", mates)
     pieces = [before, here, after]
     pieces += [lax.ppermute(before, "blk", mates), other, lax.ppermute(after, "blk", mates)]
 

time: 57.3 us -> 54.3 us (0.948)
  waiting for transfers between devices: 7.1 us -> 5.29 us
  Pallas kernels: 34 us -> 33 us
    ppermute x1, waiting for transfers between devices: 4.9 us -> 0.16 us  [on_device(): before = lax.ppermute(here, 'blk', later)]
    ppermute x1, waiting for transfers between devices: 0.47 us -> 3.44 us  [on_device(): after = lax.ppermute(here, 'blk', earlier)]
    ppermute x1, starting transfers between devices: 5.39 us -> 7.32 us  [on_device(): after = lax.ppermute(here, 'blk', earlier)]
    ppermute x1, starting transfers between devices: 1.89 us -> 0.01 us  [on_device(): other = lax.ppermute(late, 'blk', mates)]
    pallas_call x1, Pallas kernels: 13.5 us -> 12.3 us  [on_device(): pl.pallas_call(inner_kernel, in_specs=[pl.BlockSpec(memory_space=pl.ANY)]...]
    ppermute x1, waiting for transfers between devices: 1.02 us -> 0.37 us  [on_device(): lax.ppermute(before, 'blk', mates)]
    ppermute x1, waiting for transfers between devices: 0.37 us -> 1.02 us  [on_device(): lax.ppermute(after, 'blk', mates)]
where the time goes in v4:
time: 54.3 us; the launch traced here: 54 us
  Pallas kernels  33 us (61%)
  starting transfers between devices  13.6 us (25%)
  waiting for transfers between devices  5.29 us (10%)
  local copies, waits for them, and re-layouts  1.31 us (2%)
  between operations  0.76 us (1%)
    pallas_call x1, Pallas kernels, on_device(): pl.pallas_call(inner_kernel, in_specs=[pl.BlockSpec(memory_space=pl.ANY)]...  12.3 us
    ppermute x1, starting transfers between devices, on_device(): after = lax.ppermute(here, 'blk', earlier)  7.32 us
    pallas_call x1, Pallas kernels, on_device(): pl.pallas_call(write_kernel, grid=(per_row,), in_specs=[pl.BlockSpec((inn...  5.75 us
    pallas_call x1, Pallas kernels, on_device(): pl.pallas_call(load_kernel, in_specs=[anywhere], out_specs=whole, out_sha...  4.81 us
    pallas_call x1, Pallas kernels, on_device(): pl.pallas_call(outer_kernel, in_specs=[whole] * 8, out_specs=[whole] * 2,...  4.33 us
    pallas_call x1, Pallas kernels, on_device(): pl.pallas_call(regrid_kernel, grid_spec=pltpu.PrefetchScalarGridSpec(num_...  3.73 us
    ppermute x1, waiting for transfers between devices, on_device(): after = lax.ppermute(here, 'blk', earlier)  3.44 us
    ppermute x1, starting transfers between devices, on_device(): low = lax.ppermute(up, 'blk', upward)  2.38 us
  transfers between devices with their start and end apart: 8, of which 5 were waited for; matrix products, arithmetic and copies ran while one was open for 1% of the time, Pallas kernels for 42%

profile of v4, /device:TPU:0, one launch (start us, length us, event | category | flops | bytes accessed | tf_op | source)
XLA Modules:
  0.0 54.0 jit_solution(2295781596208520508)
XLA Ops:
  0.6 0.0 copy-start.2
  0.6 0.0 copy-start.3
  0.7 0.0 copy-start.4
  0.7 2.0 %edges.1 = (bf16[272,512]{1,0:T(8,128)(2,1)S(1)}, bf16[272,512]{1,0:T(8,128)(2,1)S(1)}) custom-call(f32[64,32,512]{2,1,0:T(8,128)} %bitcast.14, f32[64,32,512]{2,1,0:T(8,128)} %bitcast.15, f32[64,32,512]{2,1,0:T(8,128)} %bitcast.16, f32[64,32,512]{2,1,0:T(8,128)} %bitcast.17, f32[64,32,512]{2,1,0:T(8,128)} %bitcast.18, f32[64,32,512]{2,1,0:T(8,128)} %bitcast.19, ...), custom_call_target="tpu_custom_call" | custom-call | flops 10000000 | bytes 3145728 | tf_op jit(solution)/shard_map/edges/pallas_call | solution.py:348
  2.7 2.4 %collective-permute-start = (bf16[272,512]{1,0:T(8,128)(2,1)S(1)}, bf16[272,512]{1,0:T(8,128)(2,1)S(1)}, u32[]{:S(2)}, u32[]{:S(2)}) collective-permute-start(bf16[272,512]{1,0:T(8,128)(2,1)S(1)} %get-tuple-element.18), channel_id=1, source_target_pairs={{0,1},{1,2},{2,3},{3,4},{4,5},{5,6},{6,7},{7,8},{8,9},{9,10},{10,1... | collective-permute-start | bytes 835592 | tf_op jit(solution)/shard_map/ppermute | solution.py:370
  5.1 1.3 %collective-permute-start.1 = (bf16[272,512]{1,0:T(8,128)(2,1)S(1)}, bf16[272,512]{1,0:T(8,128)(2,1)S(1)}, u32[]{:S(2)}, u32[]{:S(2)}) collective-permute-start(bf16[272,512]{1,0:T(8,128)(2,1)S(1)} %get-tuple-element.19), channel_id=1, source_target_pairs={{1,0},{2,1},{3,2},{4,3},{5,4},{6,5},{7,6},{8,7},{9,8},{10,9},{11,1... | collective-permute-start | bytes 835592 | tf_op jit(solution)/shard_map/ppermute | solution.py:371
  6.4 0.0 copy-done.2
  6.4 12.3 %inner.1 = (f32[24,64,512]{2,1,0:T(8,128)S(1)}, f32[2,4,2,64,512]{4,3,2,1,0:T(8,128)S(1)}, bf16[96,8,128]{2,1,0:T(8,128)(2,1)S(1)}) custom-call(f32[64,32,512]{2,1,0:T(8,128)} %bitcast.22, bf16[256,512]{1,0:T(8,128)(2,1)} %bitcast.26, bf16[8,64]{1,0:T(8,128)(2,1)} %bitcast.29, f32[1,64]{1,0:T(1,128)S(1)} %copy-done.4, f32[64,64]{1,0:T(8,128)S(1)} %bitcast.10, ...), custom_call_target="tpu_custom_call" | custom-call | flops 10000000000 | bytes 20971520 | tf_op jit(solution)/shard_map/inner/pallas_call | solution.py:373
  18.7 0.0 collective-permute-done.low_ref
  18.7 0.0 collective-permute-done.1.high_ref
  18.8 0.0 copy-start.5
  18.8 4.3 %outer.1 = (f32[2,4,64,512]{3,2,1,0:T(8,128)S(1)}, bf16[128,8,128]{2,1,0:T(8,128)(2,1)}) custom-call(bf16[272,512]{1,0:T(8,128)(2,1)S(1)} %collective-permute-done.low_ref, bf16[272,512]{1,0:T(8,128)(2,1)S(1)} %collective-permute-done.1.high_ref, f32[2,4,2,64,512]{4,3,2,1,0:T(8,128)S(1)} %get-tuple-element.20.edge_ref, f32[1,64]{1,0:T(1,128)S(1)} %copy-done.4, ...), custom_call_target="tpu_custom_call" | custom-call | flops 3000000000 | bytes 4194304 | tf_op jit(solution)/shard_map/outer/pallas_call | solution.py:395
  23.1 1.0 %copy-done = f32[2,4,64,512]{3,2,1,0:T(8,128)} copy-done((f32[2,4,64,512]{3,2,1,0:T(8,128)}, f32[2,4,64,512]{3,2,1,0:T(8,128)S(1)}, u32[]{:S(2)}) %copy-start) | copy-done | bytes 1048600
  24.1 2.3 %collective-permute-start.2 = (bf16[128,8,128]{2,1,0:T(8,128)(2,1)}, bf16[128,8,128]{2,1,0:T(8,128)(2,1)S(1)}, u32[]{:S(2)}, u32[]{:S(2)}) collective-permute-start(bf16[128,8,128]{2,1,0:T(8,128)(2,1)} %get-tuple-element.23), channel_id=1, source_target_pairs={{0,16},{16,0},{1,17},{17,1},{2,18},{18,2},{3,19},{19,3},{4,20},{20... | collective-permute-start | bytes 786440 | tf_op jit(solution)/shard_map/ppermute | solution.py:430
  26.4 0.1 copy.11
  26.5 0.2 reshape.21
  26.7 0.0 copy-start.1
  26.7 4.8 %load.1.refs_6_ = bf16[128,384,128]{2,1,0:T(8,128)(2,1)S(1)} custom-call(bf16[128,384,128]{2,1,0:T(8,128)(2,1)} %bitcast.23), custom_call_target="tpu_custom_call" | custom-call | bytes 12582912 | tf_op jit(solution)/shard_map/load/pallas_call | solution.py:431
  31.6 0.3 collective-permute-done.2.refs_1_
  31.8 7.3 %collective-permute-start.4 = (bf16[128,8,128]{2,1,0:T(8,128)(2,1)S(1)}, bf16[128,8,128]{2,1,0:T(8,128)(2,1)S(1)}, u32[]{:S(2)}, u32[]{:S(2)}) collective-permute-start(bf16[128,8,128]{2,1,0:T(8,128)(2,1)S(1)} %collective-permute-done.2.refs_1_), channel_id=1, source_target_pairs={{0,14},{1,15},{2,0},{3,1},{4,2},{5,3},{6,4},{7,5},{8,6},{9,7},{10,... | collective-permute-start | bytes 786440 | tf_op jit(solution)/shard_map/ppermute | solution.py:445
  39.2 0.0 collective-permute-start.3
  39.2 0.0 copy-done.1
  39.2 5.8 %write.1 = f32[2048,512]{1,0:T(8,128)} custom-call(f32[24,64,512]{2,1,0:T(8,128)S(1)} %get-tuple-element.28.inner_ref, f32[2,4,64,512]{3,2,1,0:T(8,128)S(1)} %copy-done.1), custom_call_target="tpu_custom_call" | custom-call | bytes 8388608 | tf_op jit(solution)/shard_map/write/pallas_call | solution.py:446
  44.9 0.0 collective-permute-start.6
  44.9 3.4 %collective-permute-done.4.refs_2_ = bf16[128,8,128]{2,1,0:T(8,128)(2,1)S(1)} collective-permute-done((bf16[128,8,128]{2,1,0:T(8,128)(2,1)S(1)}, bf16[128,8,128]{2,1,0:T(8,128)(2,1)S(1)}, u32[]{:S(2)}, u32[]{:S(2)}) %collective-permute-start.4) | collective-permute-done | bytes 262176 | tf_op jit(solution)/shard_map/ppermute | solution.py:445
  48.4 0.0 collective-permute-start.7
  48.4 0.2 collective-permute-done.3.refs_0_
  48.5 0.4 collective-permute-start.5
  48.9 0.0 collective-permute-done.6.refs_4_
  48.9 1.0 %collective-permute-done.7.refs_5_ = bf16[128,8,128]{2,1,0:T(8,128)(2,1)S(1)} collective-permute-done((bf16[128,8,128]{2,1,0:T(8,128)(2,1)S(1)}, bf16[128,8,128]{2,1,0:T(8,128)(2,1)S(1)}, u32[]{:S(2)}, u32[]{:S(2)}) %collective-permute-start.7) | collective-permute-done | bytes 262176 | tf_op jit(solution)/shard_map/ppermute | solution.py:462
  49.9 0.4 collective-permute-done.5.refs_3_
  50.3 3.7 %regrid.1 = bf16[256,512]{1,0:T(8,128)(2,1)} custom-call(s32[384]{0:T(512)S(1)} %fusion.6.position_ref, bf16[128,8,128]{2,1,0:T(8,128)(2,1)S(1)} %collective-permute-done.3.refs_0_, bf16[128,8,128]{2,1,0:T(8,128)(2,1)S(1)} %collective-permute-done.2.refs_1_, bf16[128,8,128]{2,1,0:T(8,128)(2,1)S(1)} %collective-permute-done.4.refs_2_, ...), custom_call_target="tpu_custom_call" | custom-call | flops 1000000000 | bytes 16777216 | tf_op jit(solution)/shard_map/regrid/pallas_call | solution.py:464
  (5 shorter events, 0.0 us)
Async XLA Ops:
  0.6 5.8 %copy-start.2 = (f32[1,64,64]{2,1,0:T(8,128)S(1)}, f32[1,64,64]{2,1,0:T(8,128)}, u32[]{:S(2)}) copy-start(f32[1,64,64]{2,1,0:T(8,128)} %param.13) | copy-start | bytes 49156
  0.6 5.8 %copy-start.3 = (f32[1,8,64]{2,1,0:T(8,128)S(1)}, f32[1,8,64]{2,1,0:T(8,128)}, u32[]{:S(2)}) copy-start(f32[1,8,64]{2,1,0:T(8,128)} %param.14) | copy-start | bytes 6148
  0.7 5.8 %copy-start.4 = (f32[1,64]{1,0:T(1,128)S(1)}, f32[1,64]{1,0:T(1,128)}, u32[]{:S(2)}) copy-start(f32[1,64]{1,0:T(1,128)} %rate_ref.3) | copy-start | bytes 772
  2.7 16.0 %collective-permute-start = (bf16[272,512]{1,0:T(8,128)(2,1)S(1)}, bf16[272,512]{1,0:T(8,128)(2,1)S(1)}, u32[]{:S(2)}, u32[]{:S(2)}) collective-permute-start(bf16[272,512]{1,0:T(8,128)(2,1)S(1)} %get-tuple-element.18), channel_id=1, source_target_pairs={{0,1},{1,2},{2,3},{3,4},{4,5},{5,6},{6,7},{7,8},{8,9},{9,10},{10,1... | collective-permute-start | bytes 835592 | tf_op jit(solution)/shard_map/ppermute | solution.py:370
  5.1 13.7 %collective-permute-start.1 = (bf16[272,512]{1,0:T(8,128)(2,1)S(1)}, bf16[272,512]{1,0:T(8,128)(2,1)S(1)}, u32[]{:S(2)}, u32[]{:S(2)}) collective-permute-start(bf16[272,512]{1,0:T(8,128)(2,1)S(1)} %get-tuple-element.19), channel_id=1, source_target_pairs={{1,0},{2,1},{3,2},{4,3},{5,4},{6,5},{7,6},{8,7},{9,8},{10,9},{11,1... | collective-permute-start | bytes 835592 | tf_op jit(solution)/shard_map/ppermute | solution.py:371
  18.8 7.6 %copy-start.5 = (s32[1,128,3]{1,0,2:T(1,128)S(1)}, s32[1,128,3]{1,0,2:T(1,128)}, u32[]{:S(2)}) copy-start(s32[1,128,3]{1,0,2:T(1,128)} %param.16) | copy-start | bytes 4612
  23.1 1.0 %copy-start = (f32[2,4,64,512]{3,2,1,0:T(8,128)}, f32[2,4,64,512]{3,2,1,0:T(8,128)S(1)}, u32[]{:S(2)}) copy-start(f32[2,4,64,512]{3,2,1,0:T(8,128)S(1)} %get-tuple-element.29.outer_ref) | copy-start | bytes 3145732
  24.1 7.8 %collective-permute-start.2 = (bf16[128,8,128]{2,1,0:T(8,128)(2,1)}, bf16[128,8,128]{2,1,0:T(8,128)(2,1)S(1)}, u32[]{:S(2)}, u32[]{:S(2)}) collective-permute-start(bf16[128,8,128]{2,1,0:T(8,128)(2,1)} %get-tuple-element.23), channel_id=1, source_target_pairs={{0,16},{16,0},{1,17},{17,1},{2,18},{18,2},{3,19},{19,3},{4,20},{20... | collective-permute-start | bytes 786440 | tf_op jit(solution)/shard_map/ppermute | solution.py:430
  26.7 12.4 %copy-start.1 = (f32[2,4,64,512]{3,2,1,0:T(8,128)S(1)}, f32[2,4,64,512]{3,2,1,0:T(8,128)}, u32[]{:S(2)}) copy-start(f32[2,4,64,512]{3,2,1,0:T(8,128)} %copy-done) | copy-start | bytes 3145732
  31.8 16.5 %collective-permute-start.4 = (bf16[128,8,128]{2,1,0:T(8,128)(2,1)S(1)}, bf16[128,8,128]{2,1,0:T(8,128)(2,1)S(1)}, u32[]{:S(2)}, u32[]{:S(2)}) collective-permute-start(bf16[128,8,128]{2,1,0:T(8,128)(2,1)S(1)} %collective-permute-done.2.refs_1_), channel_id=1, source_target_pairs={{0,14},{1,15},{2,0},{3,1},{4,2},{5,3},{6,4},{7,5},{8,6},{9,7},{10,... | collective-permute-start | bytes 786440 | tf_op jit(solution)/shard_map/ppermute | solution.py:445
  39.2 9.4 %collective-permute-start.3 = (bf16[128,8,128]{2,1,0:T(8,128)(2,1)S(1)}, bf16[128,8,128]{2,1,0:T(8,128)(2,1)S(1)}, u32[]{:S(2)}, u32[]{:S(2)}) collective-permute-start(bf16[128,8,128]{2,1,0:T(8,128)(2,1)S(1)} %collective-permute-done.2.refs_1_), channel_id=1, source_target_pairs={{0,2},{1,3},{2,4},{3,5},{4,6},{5,7},{6,8},{7,9},{8,10},{9,11},{10,... | collective-permute-start | bytes 786440 | tf_op jit(solution)/shard_map/ppermute | solution.py:444
  44.9 4.0 %collective-permute-start.6 = (bf16[128,8,128]{2,1,0:T(8,128)(2,1)S(1)}, bf16[128,8,128]{2,1,0:T(8,128)(2,1)S(1)}, u32[]{:S(2)}, u32[]{:S(2)}) collective-permute-start(bf16[128,8,128]{2,1,0:T(8,128)(2,1)S(1)} %collective-permute-done.2.refs_1_), channel_id=1, source_target_pairs={{0,1},{1,0},{2,3},{3,2},{4,5},{5,4},{6,7},{7,6},{8,9},{9,8},{10,11... | collective-permute-start | bytes 786440 | tf_op jit(solution)/shard_map/ppermute | solution.py:460
  48.4 1.5 %collective-permute-start.7 = (bf16[128,8,128]{2,1,0:T(8,128)(2,1)S(1)}, bf16[128,8,128]{2,1,0:T(8,128)(2,1)S(1)}, u32[]{:S(2)}, u32[]{:S(2)}) collective-permute-start(bf16[128,8,128]{2,1,0:T(8,128)(2,1)S(1)} %collective-permute-done.4.refs_2_), channel_id=1, source_target_pairs={{0,1},{1,0},{2,3},{3,2},{4,5},{5,4},{6,7},{7,6},{8,9},{9,8},{10,11... | collective-permute-start | bytes 786440 | tf_op jit(solution)/shard_map/ppermute | solution.py:462
  48.5 1.8 %collective-permute-start.5 = (bf16[128,8,128]{2,1,0:T(8,128)(2,1)S(1)}, bf16[128,8,128]{2,1,0:T(8,128)(2,1)S(1)}, u32[]{:S(2)}, u32[]{:S(2)}) collective-permute-start(bf16[128,8,128]{2,1,0:T(8,128)(2,1)S(1)} %collective-permute-done.3.refs_0_), channel_id=1, source_target_pairs={{0,1},{1,0},{2,3},{3,2},{4,5},{5,4},{6,7},{7,6},{8,9},{9,8},{10,11... | collective-permute-start | bytes 786440 | tf_op jit(solution)/shard_map/ppermute | solution.py:462

commit v5 on v4

--- a/solution.py
+++ b/solution.py
@@ -59,9 +59,8 @@
 def diffused(here, above, below, wet, rate):
     columns = here.shape[1]
     rounded = here.astype(BF16)
-    left = pltpu.roll(rounded, 1, 1).astype(F32)
-    right = pltpu.roll(rounded, columns - 1, 1).astype(F32)
-    near = (above + below) + (left + right)
+    sides = pltpu.roll(rounded, 1, 1) + pltpu.roll(rounded, columns - 1, 1)
+    near = (above + below) + sides.astype(F32)
     return here + wet * (rate * (near - 4.0 * here))
 
 
@@ -274,7 +273,7 @@
     piece_refs = refs[0:6]
     weights, out_ref, held, sums, sems = refs[6:]
     tiles, fields, _ = piece_refs[0].shape
-    chunks = 4
+    chunks = 1
     tiles_chunk = tiles // chunks
     per_row, total_rows, _ = sums.shape
     rows = total_rows // fields
@@ -287,8 +286,7 @@
     for copy in copies:
         copy.wait()
 
-    @pl.loop(0, chunks)
-    def _(chunk):
+    for chunk in range(chunks):
         for pair in range(tiles_chunk // 2):
             first = chunk * tiles_chunk + 2 * pair
             lefts = []

time: 54.3 us -> 53.4 us (0.983)
  Pallas kernels: 33 us -> 32 us
    pallas_call x1, Pallas kernels: 12.3 us -> 11.8 us  [on_device(): pl.pallas_call(inner_kernel, in_specs=[pl.BlockSpec(memory_space=pl.ANY)]...]
where the time goes in v5:
time: 53.4 us; the launch traced here: 53.1 us
  Pallas kernels  32 us (60%)
  starting transfers between devices  13.6 us (25%)
  waiting for transfers between devices  5.29 us (10%)
  local copies, waits for them, and re-layouts  1.31 us (2%)
  between operations  0.92 us (2%)
    pallas_call x1, Pallas kernels, on_device(): pl.pallas_call(inner_kernel, in_specs=[pl.BlockSpec(memory_space=pl.ANY)]...  11.8 us
    ppermute x1, starting transfers between devices, on_device(): after = lax.ppermute(here, 'blk', earlier)  7.27 us
    pallas_call x1, Pallas kernels, on_device(): pl.pallas_call(write_kernel, grid=(per_row,), in_specs=[pl.BlockSpec((inn...  5.75 us
    pallas_call x1, Pallas kernels, on_device(): pl.pallas_call(load_kernel, in_specs=[anywhere], out_specs=whole, out_sha...  4.81 us
    pallas_call x1, Pallas kernels, on_device(): pl.pallas_call(outer_kernel, in_specs=[whole] * 8, out_specs=[whole] * 2,...  4.14 us
    pallas_call x1, Pallas kernels, on_device(): pl.pallas_call(regrid_kernel, grid_spec=pltpu.PrefetchScalarGridSpec(num_...  3.47 us
    ppermute x1, waiting for transfers between devices, on_device(): after = lax.ppermute(here, 'blk', earlier)  3.41 us
    ppermute x1, starting transfers between devices, on_device(): low = lax.ppermute(up, 'blk', upward)  2.38 us
  transfers between devices with their start and end apart: 8, of which 5 were waited for; matrix products, arithmetic and copies ran while one was open for 1% of the time, Pallas kernels for 42%

profile of v5, /device:TPU:0, one launch (start us, length us, event | category | flops | bytes accessed | tf_op | source)
XLA Modules:
  0.0 53.1 jit_solution(5861989337227837432)
XLA Ops:
  0.6 0.0 copy-start.2
  0.6 0.0 copy-start.3
  0.7 0.0 copy-start.4
  0.7 2.0 %edges.1 = (bf16[272,512]{1,0:T(8,128)(2,1)S(1)}, bf16[272,512]{1,0:T(8,128)(2,1)S(1)}) custom-call(f32[64,32,512]{2,1,0:T(8,128)} %bitcast.14, f32[64,32,512]{2,1,0:T(8,128)} %bitcast.15, f32[64,32,512]{2,1,0:T(8,128)} %bitcast.16, f32[64,32,512]{2,1,0:T(8,128)} %bitcast.17, f32[64,32,512]{2,1,0:T(8,128)} %bitcast.18, f32[64,32,512]{2,1,0:T(8,128)} %bitcast.19, ...), custom_call_target="tpu_custom_call" | custom-call | flops 10000000 | bytes 3145728 | tf_op jit(solution)/shard_map/edges/pallas_call | solution.py:346
  2.7 2.4 %collective-permute-start = (bf16[272,512]{1,0:T(8,128)(2,1)S(1)}, bf16[272,512]{1,0:T(8,128)(2,1)S(1)}, u32[]{:S(2)}, u32[]{:S(2)}) collective-permute-start(bf16[272,512]{1,0:T(8,128)(2,1)S(1)} %get-tuple-element.18), channel_id=1, source_target_pairs={{0,1},{1,2},{2,3},{3,4},{4,5},{5,6},{6,7},{7,8},{8,9},{9,10},{10,1... | collective-permute-start | bytes 835592 | tf_op jit(solution)/shard_map/ppermute | solution.py:368
  5.1 1.3 %collective-permute-start.1 = (bf16[272,512]{1,0:T(8,128)(2,1)S(1)}, bf16[272,512]{1,0:T(8,128)(2,1)S(1)}, u32[]{:S(2)}, u32[]{:S(2)}) collective-permute-start(bf16[272,512]{1,0:T(8,128)(2,1)S(1)} %get-tuple-element.19), channel_id=1, source_target_pairs={{1,0},{2,1},{3,2},{4,3},{5,4},{6,5},{7,6},{8,7},{9,8},{10,9},{11,1... | collective-permute-start | bytes 835592 | tf_op jit(solution)/shard_map/ppermute | solution.py:369
  6.4 0.0 copy-done.2
  6.4 0.0 copy-done.3
  6.4 11.8 %inner.1 = (f32[24,64,512]{2,1,0:T(8,128)S(1)}, f32[2,4,2,64,512]{4,3,2,1,0:T(8,128)S(1)}, bf16[96,8,128]{2,1,0:T(8,128)(2,1)S(1)}) custom-call(f32[64,32,512]{2,1,0:T(8,128)} %bitcast.22, bf16[256,512]{1,0:T(8,128)(2,1)} %bitcast.26, bf16[8,64]{1,0:T(8,128)(2,1)} %bitcast.29, f32[1,64]{1,0:T(1,128)S(1)} %copy-done.4, f32[64,64]{1,0:T(8,128)S(1)} %bitcast.10, ...), custom_call_target="tpu_custom_call" | custom-call | flops 10000000000 | bytes 20971520 | tf_op jit(solution)/shard_map/inner/pallas_call | solution.py:371
  18.2 0.0 collective-permute-done.low_ref
  18.2 0.0 collective-permute-done.1.high_ref
  18.2 0.0 copy-start.5
  18.2 4.1 %outer.1 = (f32[2,4,64,512]{3,2,1,0:T(8,128)S(1)}, bf16[128,8,128]{2,1,0:T(8,128)(2,1)}) custom-call(bf16[272,512]{1,0:T(8,128)(2,1)S(1)} %collective-permute-done.low_ref, bf16[272,512]{1,0:T(8,128)(2,1)S(1)} %collective-permute-done.1.high_ref, f32[2,4,2,64,512]{4,3,2,1,0:T(8,128)S(1)} %get-tuple-element.20.edge_ref, f32[1,64]{1,0:T(1,128)S(1)} %copy-done.4, ...), custom_call_target="tpu_custom_call" | custom-call | flops 3000000000 | bytes 4194304 | tf_op jit(solution)/shard_map/outer/pallas_call | solution.py:393
  22.4 1.0 %copy-done = f32[2,4,64,512]{3,2,1,0:T(8,128)} copy-done((f32[2,4,64,512]{3,2,1,0:T(8,128)}, f32[2,4,64,512]{3,2,1,0:T(8,128)S(1)}, u32[]{:S(2)}) %copy-start) | copy-done | bytes 1048600
  23.3 2.3 %collective-permute-start.2 = (bf16[128,8,128]{2,1,0:T(8,128)(2,1)}, bf16[128,8,128]{2,1,0:T(8,128)(2,1)S(1)}, u32[]{:S(2)}, u32[]{:S(2)}) collective-permute-start(bf16[128,8,128]{2,1,0:T(8,128)(2,1)} %get-tuple-element.23), channel_id=1, source_target_pairs={{0,16},{16,0},{1,17},{17,1},{2,18},{18,2},{3,19},{19,3},{4,20},{20... | collective-permute-start | bytes 786440 | tf_op jit(solution)/shard_map/ppermute | solution.py:428
  25.6 0.1 copy.11
  25.7 0.2 reshape.21
  26.0 0.0 copy-start.1
  26.0 4.8 %load.1.refs_6_ = bf16[128,384,128]{2,1,0:T(8,128)(2,1)S(1)} custom-call(bf16[128,384,128]{2,1,0:T(8,128)(2,1)} %bitcast.23), custom_call_target="tpu_custom_call" | custom-call | bytes 12582912 | tf_op jit(solution)/shard_map/load/pallas_call | solution.py:429
  30.8 0.3 collective-permute-done.2.refs_1_
  31.1 7.3 %collective-permute-start.4 = (bf16[128,8,128]{2,1,0:T(8,128)(2,1)S(1)}, bf16[128,8,128]{2,1,0:T(8,128)(2,1)S(1)}, u32[]{:S(2)}, u32[]{:S(2)}) collective-permute-start(bf16[128,8,128]{2,1,0:T(8,128)(2,1)S(1)} %collective-permute-done.2.refs_1_), channel_id=1, source_target_pairs={{0,14},{1,15},{2,0},{3,1},{4,2},{5,3},{6,4},{7,5},{8,6},{9,7},{10,... | collective-permute-start | bytes 786440 | tf_op jit(solution)/shard_map/ppermute | solution.py:443
  38.4 0.0 collective-permute-start.3
  38.4 5.8 %write.1 = f32[2048,512]{1,0:T(8,128)} custom-call(f32[24,64,512]{2,1,0:T(8,128)S(1)} %get-tuple-element.28.inner_ref, f32[2,4,64,512]{3,2,1,0:T(8,128)S(1)} %copy-done.1), custom_call_target="tpu_custom_call" | custom-call | bytes 8388608 | tf_op jit(solution)/shard_map/write/pallas_call | solution.py:444
  44.2 0.0 collective-permute-start.6
  44.2 3.4 %collective-permute-done.4.refs_2_ = bf16[128,8,128]{2,1,0:T(8,128)(2,1)S(1)} collective-permute-done((bf16[128,8,128]{2,1,0:T(8,128)(2,1)S(1)}, bf16[128,8,128]{2,1,0:T(8,128)(2,1)S(1)}, u32[]{:S(2)}, u32[]{:S(2)}) %collective-permute-start.4) | collective-permute-done | bytes 262176 | tf_op jit(solution)/shard_map/ppermute | solution.py:443
  47.6 0.0 collective-permute-start.7
  47.6 0.2 collective-permute-done.3.refs_0_
  47.7 0.4 collective-permute-start.5
  48.1 0.0 collective-permute-done.6.refs_4_
  48.1 1.0 %collective-permute-done.7.refs_5_ = bf16[128,8,128]{2,1,0:T(8,128)(2,1)S(1)} collective-permute-done((bf16[128,8,128]{2,1,0:T(8,128)(2,1)S(1)}, bf16[128,8,128]{2,1,0:T(8,128)(2,1)S(1)}, u32[]{:S(2)}, u32[]{:S(2)}) %collective-permute-start.7) | collective-permute-done | bytes 262176 | tf_op jit(solution)/shard_map/ppermute | solution.py:460
  49.1 0.4 collective-permute-done.5.refs_3_
  49.5 3.5 %regrid.1 = bf16[256,512]{1,0:T(8,128)(2,1)} custom-call(s32[384]{0:T(512)S(1)} %fusion.6.position_ref, bf16[128,8,128]{2,1,0:T(8,128)(2,1)S(1)} %collective-permute-done.3.refs_0_, bf16[128,8,128]{2,1,0:T(8,128)(2,1)S(1)} %collective-permute-done.2.refs_1_, bf16[128,8,128]{2,1,0:T(8,128)(2,1)S(1)} %collective-permute-done.4.refs_2_, ...), custom_call_target="tpu_custom_call" | custom-call | flops 1000000000 | bytes 16777216 | tf_op jit(solution)/shard_map/regrid/pallas_call | solution.py:462
  (5 shorter events, 0.0 us)
Async XLA Ops:
  0.6 5.8 %copy-start.2 = (f32[1,64,64]{2,1,0:T(8,128)S(1)}, f32[1,64,64]{2,1,0:T(8,128)}, u32[]{:S(2)}) copy-start(f32[1,64,64]{2,1,0:T(8,128)} %param.13) | copy-start | bytes 49156
  0.6 5.8 %copy-start.3 = (f32[1,8,64]{2,1,0:T(8,128)S(1)}, f32[1,8,64]{2,1,0:T(8,128)}, u32[]{:S(2)}) copy-start(f32[1,8,64]{2,1,0:T(8,128)} %param.14) | copy-start | bytes 6148
  0.7 5.8 %copy-start.4 = (f32[1,64]{1,0:T(1,128)S(1)}, f32[1,64]{1,0:T(1,128)}, u32[]{:S(2)}) copy-start(f32[1,64]{1,0:T(1,128)} %rate_ref.3) | copy-start | bytes 772
  2.7 15.5 %collective-permute-start = (bf16[272,512]{1,0:T(8,128)(2,1)S(1)}, bf16[272,512]{1,0:T(8,128)(2,1)S(1)}, u32[]{:S(2)}, u32[]{:S(2)}) collective-permute-start(bf16[272,512]{1,0:T(8,128)(2,1)S(1)} %get-tuple-element.18), channel_id=1, source_target_pairs={{0,1},{1,2},{2,3},{3,4},{4,5},{5,6},{6,7},{7,8},{8,9},{9,10},{10,1... | collective-permute-start | bytes 835592 | tf_op jit(solution)/shard_map/ppermute | solution.py:368
  5.1 13.1 %collective-permute-start.1 = (bf16[272,512]{1,0:T(8,128)(2,1)S(1)}, bf16[272,512]{1,0:T(8,128)(2,1)S(1)}, u32[]{:S(2)}, u32[]{:S(2)}) collective-permute-start(bf16[272,512]{1,0:T(8,128)(2,1)S(1)} %get-tuple-element.19), channel_id=1, source_target_pairs={{1,0},{2,1},{3,2},{4,3},{5,4},{6,5},{7,6},{8,7},{9,8},{10,9},{11,1... | collective-permute-start | bytes 835592 | tf_op jit(solution)/shard_map/ppermute | solution.py:369
  18.2 7.4 %copy-start.5 = (s32[1,128,3]{1,0,2:T(1,128)S(1)}, s32[1,128,3]{1,0,2:T(1,128)}, u32[]{:S(2)}) copy-start(s32[1,128,3]{1,0,2:T(1,128)} %param.16) | copy-start | bytes 4612
  22.4 1.0 %copy-start = (f32[2,4,64,512]{3,2,1,0:T(8,128)}, f32[2,4,64,512]{3,2,1,0:T(8,128)S(1)}, u32[]{:S(2)}) copy-start(f32[2,4,64,512]{3,2,1,0:T(8,128)S(1)} %get-tuple-element.29.outer_ref) | copy-start | bytes 3145732
  23.3 7.8 %collective-permute-start.2 = (bf16[128,8,128]{2,1,0:T(8,128)(2,1)}, bf16[128,8,128]{2,1,0:T(8,128)(2,1)S(1)}, u32[]{:S(2)}, u32[]{:S(2)}) collective-permute-start(bf16[128,8,128]{2,1,0:T(8,128)(2,1)} %get-tuple-element.23), channel_id=1, source_target_pairs={{0,16},{16,0},{1,17},{17,1},{2,18},{18,2},{3,19},{19,3},{4,20},{20... | collective-permute-start | bytes 786440 | tf_op jit(solution)/shard_map/ppermute | solution.py:428
  26.0 12.4 %copy-start.1 = (f32[2,4,64,512]{3,2,1,0:T(8,128)S(1)}, f32[2,4,64,512]{3,2,1,0:T(8,128)}, u32[]{:S(2)}) copy-start(f32[2,4,64,512]{3,2,1,0:T(8,128)} %copy-done) | copy-start | bytes 3145732
  31.1 16.4 %collective-permute-start.4 = (bf16[128,8,128]{2,1,0:T(8,128)(2,1)S(1)}, bf16[128,8,128]{2,1,0:T(8,128)(2,1)S(1)}, u32[]{:S(2)}, u32[]{:S(2)}) collective-permute-start(bf16[128,8,128]{2,1,0:T(8,128)(2,1)S(1)} %collective-permute-done.2.refs_1_), channel_id=1, source_target_pairs={{0,14},{1,15},{2,0},{3,1},{4,2},{5,3},{6,4},{7,5},{8,6},{9,7},{10,... | collective-permute-start | bytes 786440 | tf_op jit(solution)/shard_map/ppermute | solution.py:443
  38.4 9.3 %collective-permute-start.3 = (bf16[128,8,128]{2,1,0:T(8,128)(2,1)S(1)}, bf16[128,8,128]{2,1,0:T(8,128)(2,1)S(1)}, u32[]{:S(2)}, u32[]{:S(2)}) collective-permute-start(bf16[128,8,128]{2,1,0:T(8,128)(2,1)S(1)} %collective-permute-done.2.refs_1_), channel_id=1, source_target_pairs={{0,2},{1,3},{2,4},{3,5},{4,6},{5,7},{6,8},{7,9},{8,10},{9,11},{10,... | collective-permute-start | bytes 786440 | tf_op jit(solution)/shard_map/ppermute | solution.py:442
  44.2 3.9 %collective-permute-start.6 = (bf16[128,8,128]{2,1,0:T(8,128)(2,1)S(1)}, bf16[128,8,128]{2,1,0:T(8,128)(2,1)S(1)}, u32[]{:S(2)}, u32[]{:S(2)}) collective-permute-start(bf16[128,8,128]{2,1,0:T(8,128)(2,1)S(1)} %collective-permute-done.2.refs_1_), channel_id=1, source_target_pairs={{0,1},{1,0},{2,3},{3,2},{4,5},{5,4},{6,7},{7,6},{8,9},{9,8},{10,11... | collective-permute-start | bytes 786440 | tf_op jit(solution)/shard_map/ppermute | solution.py:458
  47.6 1.5 %collective-permute-start.7 = (bf16[128,8,128]{2,1,0:T(8,128)(2,1)S(1)}, bf16[128,8,128]{2,1,0:T(8,128)(2,1)S(1)}, u32[]{:S(2)}, u32[]{:S(2)}) collective-permute-start(bf16[128,8,128]{2,1,0:T(8,128)(2,1)S(1)} %collective-permute-done.4.refs_2_), channel_id=1, source_target_pairs={{0,1},{1,0},{2,3},{3,2},{4,5},{5,4},{6,7},{7,6},{8,9},{9,8},{10,11... | collective-permute-start | bytes 786440 | tf_op jit(solution)/shard_map/ppermute | solution.py:460
  47.7 1.8 %collective-permute-start.5 = (bf16[128,8,128]{2,1,0:T(8,128)(2,1)S(1)}, bf16[128,8,128]{2,1,0:T(8,128)(2,1)S(1)}, u32[]{:S(2)}, u32[]{:S(2)}) collective-permute-start(bf16[128,8,128]{2,1,0:T(8,128)(2,1)S(1)} %collective-permute-done.3.refs_0_), channel_id=1, source_target_pairs={{0,1},{1,0},{2,3},{3,2},{4,5},{5,4},{6,7},{7,6},{8,9},{9,8},{10,11... | collective-permute-start | bytes 786440 | tf_op jit(solution)/shard_map/ppermute | solution.py:460

commit v6 on v5

--- a/solution.py
+++ b/solution.py
@@ -146,8 +146,13 @@
             row = group * 8 + part
             pushed = rows_of(blocks_of(force), row, fields, rows).astype(BF16)
             even[row] = rows_of(state, part, levels, 8) + driven(gain, pushed)
-
-    for step in range(1, NSTEP + 1):
+        for row in range(max(1, group * 8 - 1), group * 8 + 7):
+            odd[row] = mixed(
+                step_factor,
+                diffused(even[row], even[row - 1], even[row + 1], wet_ref[row : row + 1, :], rate),
+            )
+
+    for step in range(2, NSTEP + 1):
         source, target = (even, odd) if step % 2 else (odd, even)
         last = step == NSTEP
 

time: 53.4 us -> 53.7 us (level)
  no operation moved by 1% of the time
where the time goes in v6:
time: 53.7 us; the launch traced here: 53.5 us
  Pallas kernels  32.3 us (60%)
  starting transfers between devices  13.6 us (25%)
  waiting for transfers between devices  5.3 us (10%)
  local copies, waits for them, and re-layouts  1.31 us (2%)
  between operations  0.92 us (2%)
    pallas_call x1, Pallas kernels, on_device(): pl.pallas_call(inner_kernel, in_specs=[pl.BlockSpec(memory_space=pl.ANY)]...  12.1 us
    ppermute x1, starting transfers between devices, on_device(): after = lax.ppermute(here, 'blk', earlier)  7.28 us
    pallas_call x1, Pallas kernels, on_device(): pl.pallas_call(write_kernel, grid=(per_row,), in_specs=[pl.BlockSpec((inn...  5.75 us
    pallas_call x1, Pallas kernels, on_device(): pl.pallas_call(load_kernel, in_specs=[anywhere], out_specs=whole, out_sha...  4.81 us
    pallas_call x1, Pallas kernels, on_device(): pl.pallas_call(outer_kernel, in_specs=[whole] * 8, out_specs=[whole] * 2,...  4.15 us
    pallas_call x1, Pallas kernels, on_device(): pl.pallas_call(regrid_kernel, grid_spec=pltpu.PrefetchScalarGridSpec(num_...  3.47 us
    ppermute x1, waiting for transfers between devices, on_device(): after = lax.ppermute(here, 'blk', earlier)  3.43 us
    ppermute x1, starting transfers between devices, on_device(): low = lax.ppermute(up, 'blk', upward)  2.38 us
  transfers between devices with their start and end apart: 8, of which 5 were waited for; matrix products, arithmetic and copies ran while one was open for 1% of the time, Pallas kernels for 42%

profile of v6, /device:TPU:0, one launch (start us, length us, event | category | flops | bytes accessed | tf_op | source)
XLA Modules:
  0.0 53.5 jit_solution(4655279729904548824)
XLA Ops:
  0.6 0.0 copy-start.2
  0.6 0.0 copy-start.3
  0.7 0.0 copy-start.4
  0.7 2.0 %edges.1 = (bf16[272,512]{1,0:T(8,128)(2,1)S(1)}, bf16[272,512]{1,0:T(8,128)(2,1)S(1)}) custom-call(f32[64,32,512]{2,1,0:T(8,128)} %bitcast.14, f32[64,32,512]{2,1,0:T(8,128)} %bitcast.15, f32[64,32,512]{2,1,0:T(8,128)} %bitcast.16, f32[64,32,512]{2,1,0:T(8,128)} %bitcast.17, f32[64,32,512]{2,1,0:T(8,128)} %bitcast.18, f32[64,32,512]{2,1,0:T(8,128)} %bitcast.19, ...), custom_call_target="tpu_custom_call" | custom-call | flops 10000000 | bytes 3145728 | tf_op jit(solution)/shard_map/edges/pallas_call | solution.py:351
  2.7 2.4 %collective-permute-start = (bf16[272,512]{1,0:T(8,128)(2,1)S(1)}, bf16[272,512]{1,0:T(8,128)(2,1)S(1)}, u32[]{:S(2)}, u32[]{:S(2)}) collective-permute-start(bf16[272,512]{1,0:T(8,128)(2,1)S(1)} %get-tuple-element.18), channel_id=1, source_target_pairs={{0,1},{1,2},{2,3},{3,4},{4,5},{5,6},{6,7},{7,8},{8,9},{9,10},{10,1... | collective-permute-start | bytes 835592 | tf_op jit(solution)/shard_map/ppermute | solution.py:373
  5.1 1.3 %collective-permute-start.1 = (bf16[272,512]{1,0:T(8,128)(2,1)S(1)}, bf16[272,512]{1,0:T(8,128)(2,1)S(1)}, u32[]{:S(2)}, u32[]{:S(2)}) collective-permute-start(bf16[272,512]{1,0:T(8,128)(2,1)S(1)} %get-tuple-element.19), channel_id=1, source_target_pairs={{1,0},{2,1},{3,2},{4,3},{5,4},{6,5},{7,6},{8,7},{9,8},{10,9},{11,1... | collective-permute-start | bytes 835592 | tf_op jit(solution)/shard_map/ppermute | solution.py:374
  6.4 0.0 copy-done.2
  6.4 0.0 copy-done.3
  6.4 12.1 %inner.1 = (f32[24,64,512]{2,1,0:T(8,128)S(1)}, f32[2,4,2,64,512]{4,3,2,1,0:T(8,128)S(1)}, bf16[96,8,128]{2,1,0:T(8,128)(2,1)S(1)}) custom-call(f32[64,32,512]{2,1,0:T(8,128)} %bitcast.22, bf16[256,512]{1,0:T(8,128)(2,1)} %bitcast.26, bf16[8,64]{1,0:T(8,128)(2,1)} %bitcast.29, f32[1,64]{1,0:T(1,128)S(1)} %copy-done.4, f32[64,64]{1,0:T(8,128)S(1)} %bitcast.10, ...), custom_call_target="tpu_custom_call" | custom-call | flops 10000000000 | bytes 20971520 | tf_op jit(solution)/shard_map/inner/pallas_call | solution.py:376
  18.5 0.0 collective-permute-done.low_ref
  18.5 0.0 collective-permute-done.1.high_ref
  18.5 0.0 copy-start.5
  18.5 4.1 %outer.1 = (f32[2,4,64,512]{3,2,1,0:T(8,128)S(1)}, bf16[128,8,128]{2,1,0:T(8,128)(2,1)}) custom-call(bf16[272,512]{1,0:T(8,128)(2,1)S(1)} %collective-permute-done.low_ref, bf16[272,512]{1,0:T(8,128)(2,1)S(1)} %collective-permute-done.1.high_ref, f32[2,4,2,64,512]{4,3,2,1,0:T(8,128)S(1)} %get-tuple-element.20.edge_ref, f32[1,64]{1,0:T(1,128)S(1)} %copy-done.4, ...), custom_call_target="tpu_custom_call" | custom-call | flops 3000000000 | bytes 4194304 | tf_op jit(solution)/shard_map/outer/pallas_call | solution.py:398
  22.7 1.0 %copy-done = f32[2,4,64,512]{3,2,1,0:T(8,128)} copy-done((f32[2,4,64,512]{3,2,1,0:T(8,128)}, f32[2,4,64,512]{3,2,1,0:T(8,128)S(1)}, u32[]{:S(2)}) %copy-start) | copy-done | bytes 1048600
  23.6 2.3 %collective-permute-start.2 = (bf16[128,8,128]{2,1,0:T(8,128)(2,1)}, bf16[128,8,128]{2,1,0:T(8,128)(2,1)S(1)}, u32[]{:S(2)}, u32[]{:S(2)}) collective-permute-start(bf16[128,8,128]{2,1,0:T(8,128)(2,1)} %get-tuple-element.23), channel_id=1, source_target_pairs={{0,16},{16,0},{1,17},{17,1},{2,18},{18,2},{3,19},{19,3},{4,20},{20... | collective-permute-start | bytes 786440 | tf_op jit(solution)/shard_map/ppermute | solution.py:433
  26.0 0.1 copy.11
  26.1 0.2 reshape.21
  26.3 0.0 copy-start.1
  26.3 4.8 %load.1.refs_6_ = bf16[128,384,128]{2,1,0:T(8,128)(2,1)S(1)} custom-call(bf16[128,384,128]{2,1,0:T(8,128)(2,1)} %bitcast.23), custom_call_target="tpu_custom_call" | custom-call | bytes 12582912 | tf_op jit(solution)/shard_map/load/pallas_call | solution.py:434
  31.1 0.3 collective-permute-done.2.refs_1_
  31.5 7.3 %collective-permute-start.4 = (bf16[128,8,128]{2,1,0:T(8,128)(2,1)S(1)}, bf16[128,8,128]{2,1,0:T(8,128)(2,1)S(1)}, u32[]{:S(2)}, u32[]{:S(2)}) collective-permute-start(bf16[128,8,128]{2,1,0:T(8,128)(2,1)S(1)} %collective-permute-done.2.refs_1_), channel_id=1, source_target_pairs={{0,14},{1,15},{2,0},{3,1},{4,2},{5,3},{6,4},{7,5},{8,6},{9,7},{10,... | collective-permute-start | bytes 786440 | tf_op jit(solution)/shard_map/ppermute | solution.py:448
  38.7 0.0 collective-permute-start.3
  38.7 5.8 %write.1 = f32[2048,512]{1,0:T(8,128)} custom-call(f32[24,64,512]{2,1,0:T(8,128)S(1)} %get-tuple-element.28.inner_ref, f32[2,4,64,512]{3,2,1,0:T(8,128)S(1)} %copy-done.1), custom_call_target="tpu_custom_call" | custom-call | bytes 8388608 | tf_op jit(solution)/shard_map/write/pallas_call | solution.py:449
  44.5 0.0 collective-permute-start.6
  44.5 3.4 %collective-permute-done.4.refs_2_ = bf16[128,8,128]{2,1,0:T(8,128)(2,1)S(1)} collective-permute-done((bf16[128,8,128]{2,1,0:T(8,128)(2,1)S(1)}, bf16[128,8,128]{2,1,0:T(8,128)(2,1)S(1)}, u32[]{:S(2)}, u32[]{:S(2)}) %collective-permute-start.4) | collective-permute-done | bytes 262176 | tf_op jit(solution)/shard_map/ppermute | solution.py:448
  47.9 0.0 collective-permute-start.7
  47.9 0.2 collective-permute-done.3.refs_0_
  48.1 0.4 collective-permute-start.5
  48.4 0.0 collective-permute-done.6.refs_4_
  48.4 1.0 %collective-permute-done.7.refs_5_ = bf16[128,8,128]{2,1,0:T(8,128)(2,1)S(1)} collective-permute-done((bf16[128,8,128]{2,1,0:T(8,128)(2,1)S(1)}, bf16[128,8,128]{2,1,0:T(8,128)(2,1)S(1)}, u32[]{:S(2)}, u32[]{:S(2)}) %collective-permute-start.7) | collective-permute-done | bytes 262176 | tf_op jit(solution)/shard_map/ppermute | solution.py:465
  49.5 0.4 collective-permute-done.5.refs_3_
  49.8 3.5 %regrid.1 = bf16[256,512]{1,0:T(8,128)(2,1)} custom-call(s32[384]{0:T(512)S(1)} %fusion.6.position_ref, bf16[128,8,128]{2,1,0:T(8,128)(2,1)S(1)} %collective-permute-done.3.refs_0_, bf16[128,8,128]{2,1,0:T(8,128)(2,1)S(1)} %collective-permute-done.2.refs_1_, bf16[128,8,128]{2,1,0:T(8,128)(2,1)S(1)} %collective-permute-done.4.refs_2_, ...), custom_call_target="tpu_custom_call" | custom-call | flops 1000000000 | bytes 16777216 | tf_op jit(solution)/shard_map/regrid/pallas_call | solution.py:467
  (5 shorter events, 0.0 us)
Async XLA Ops:
  0.6 5.8 %copy-start.2 = (f32[1,64,64]{2,1,0:T(8,128)S(1)}, f32[1,64,64]{2,1,0:T(8,128)}, u32[]{:S(2)}) copy-start(f32[1,64,64]{2,1,0:T(8,128)} %param.13) | copy-start | bytes 49156
  0.6 5.8 %copy-start.3 = (f32[1,8,64]{2,1,0:T(8,128)S(1)}, f32[1,8,64]{2,1,0:T(8,128)}, u32[]{:S(2)}) copy-start(f32[1,8,64]{2,1,0:T(8,128)} %param.14) | copy-start | bytes 6148
  0.7 5.8 %copy-start.4 = (f32[1,64]{1,0:T(1,128)S(1)}, f32[1,64]{1,0:T(1,128)}, u32[]{:S(2)}) copy-start(f32[1,64]{1,0:T(1,128)} %rate_ref.3) | copy-start | bytes 772
  2.7 15.8 %collective-permute-start = (bf16[272,512]{1,0:T(8,128)(2,1)S(1)}, bf16[272,512]{1,0:T(8,128)(2,1)S(1)}, u32[]{:S(2)}, u32[]{:S(2)}) collective-permute-start(bf16[272,512]{1,0:T(8,128)(2,1)S(1)} %get-tuple-element.18), channel_id=1, source_target_pairs={{0,1},{1,2},{2,3},{3,4},{4,5},{5,6},{6,7},{7,8},{8,9},{9,10},{10,1... | collective-permute-start | bytes 835592 | tf_op jit(solution)/shard_map/ppermute | solution.py:373
  5.1 13.4 %collective-permute-start.1 = (bf16[272,512]{1,0:T(8,128)(2,1)S(1)}, bf16[272,512]{1,0:T(8,128)(2,1)S(1)}, u32[]{:S(2)}, u32[]{:S(2)}) collective-permute-start(bf16[272,512]{1,0:T(8,128)(2,1)S(1)} %get-tuple-element.19), channel_id=1, source_target_pairs={{1,0},{2,1},{3,2},{4,3},{5,4},{6,5},{7,6},{8,7},{9,8},{10,9},{11,1... | collective-permute-start | bytes 835592 | tf_op jit(solution)/shard_map/ppermute | solution.py:374
  18.5 7.5 %copy-start.5 = (s32[1,128,3]{1,0,2:T(1,128)S(1)}, s32[1,128,3]{1,0,2:T(1,128)}, u32[]{:S(2)}) copy-start(s32[1,128,3]{1,0,2:T(1,128)} %param.16) | copy-start | bytes 4612
  22.7 1.0 %copy-start = (f32[2,4,64,512]{3,2,1,0:T(8,128)}, f32[2,4,64,512]{3,2,1,0:T(8,128)S(1)}, u32[]{:S(2)}) copy-start(f32[2,4,64,512]{3,2,1,0:T(8,128)S(1)} %get-tuple-element.29.outer_ref) | copy-start | bytes 3145732
  23.6 7.8 %collective-permute-start.2 = (bf16[128,8,128]{2,1,0:T(8,128)(2,1)}, bf16[128,8,128]{2,1,0:T(8,128)(2,1)S(1)}, u32[]{:S(2)}, u32[]{:S(2)}) collective-permute-start(bf16[128,8,128]{2,1,0:T(8,128)(2,1)} %get-tuple-element.23), channel_id=1, source_target_pairs={{0,16},{16,0},{1,17},{17,1},{2,18},{18,2},{3,19},{19,3},{4,20},{20... | collective-permute-start | bytes 786440 | tf_op jit(solution)/shard_map/ppermute | solution.py:433
  26.3 12.4 %copy-start.1 = (f32[2,4,64,512]{3,2,1,0:T(8,128)S(1)}, f32[2,4,64,512]{3,2,1,0:T(8,128)}, u32[]{:S(2)}) copy-start(f32[2,4,64,512]{3,2,1,0:T(8,128)} %copy-done) | copy-start | bytes 3145732
  31.5 16.5 %collective-permute-start.4 = (bf16[128,8,128]{2,1,0:T(8,128)(2,1)S(1)}, bf16[128,8,128]{2,1,0:T(8,128)(2,1)S(1)}, u32[]{:S(2)}, u32[]{:S(2)}) collective-permute-start(bf16[128,8,128]{2,1,0:T(8,128)(2,1)S(1)} %collective-permute-done.2.refs_1_), channel_id=1, source_target_pairs={{0,14},{1,15},{2,0},{3,1},{4,2},{5,3},{6,4},{7,5},{8,6},{9,7},{10,... | collective-permute-start | bytes 786440 | tf_op jit(solution)/shard_map/ppermute | solution.py:448
  38.7 9.4 %collective-permute-start.3 = (bf16[128,8,128]{2,1,0:T(8,128)(2,1)S(1)}, bf16[128,8,128]{2,1,0:T(8,128)(2,1)S(1)}, u32[]{:S(2)}, u32[]{:S(2)}) collective-permute-start(bf16[128,8,128]{2,1,0:T(8,128)(2,1)S(1)} %collective-permute-done.2.refs_1_), channel_id=1, source_target_pairs={{0,2},{1,3},{2,4},{3,5},{4,6},{5,7},{6,8},{7,9},{8,10},{9,11},{10,... | collective-permute-start | bytes 786440 | tf_op jit(solution)/shard_map/ppermute | solution.py:447
  44.5 3.9 %collective-permute-start.6 = (bf16[128,8,128]{2,1,0:T(8,128)(2,1)S(1)}, bf16[128,8,128]{2,1,0:T(8,128)(2,1)S(1)}, u32[]{:S(2)}, u32[]{:S(2)}) collective-permute-start(bf16[128,8,128]{2,1,0:T(8,128)(2,1)S(1)} %collective-permute-done.2.refs_1_), channel_id=1, source_target_pairs={{0,1},{1,0},{2,3},{3,2},{4,5},{5,4},{6,7},{7,6},{8,9},{9,8},{10,11... | collective-permute-start | bytes 786440 | tf_op jit(solution)/shard_map/ppermute | solution.py:463
  47.9 1.5 %collective-permute-start.7 = (bf16[128,8,128]{2,1,0:T(8,128)(2,1)S(1)}, bf16[128,8,128]{2,1,0:T(8,128)(2,1)S(1)}, u32[]{:S(2)}, u32[]{:S(2)}) collective-permute-start(bf16[128,8,128]{2,1,0:T(8,128)(2,1)S(1)} %collective-permute-done.4.refs_2_), channel_id=1, source_target_pairs={{0,1},{1,0},{2,3},{3,2},{4,5},{5,4},{6,7},{7,6},{8,9},{9,8},{10,11... | collective-permute-start | bytes 786440 | tf_op jit(solution)/shard_map/ppermute | solution.py:465
  48.1 1.8 %collective-permute-start.5 = (bf16[128,8,128]{2,1,0:T(8,128)(2,1)S(1)}, bf16[128,8,128]{2,1,0:T(8,128)(2,1)S(1)}, u32[]{:S(2)}, u32[]{:S(2)}) collective-permute-start(bf16[128,8,128]{2,1,0:T(8,128)(2,1)S(1)} %collective-permute-done.3.refs_0_), channel_id=1, source_target_pairs={{0,1},{1,0},{2,3},{3,2},{4,5},{5,4},{6,7},{7,6},{8,9},{9,8},{10,11... | collective-permute-start | bytes 786440 | tf_op jit(solution)/shard_map/ppermute | solution.py:465
